TPU v7x, 32 devices: a whole 2x2x4 slice. The times are simulated.
32 devices in a mesh: slab: 8 (over z, core), col: 4 (over y, x).
Axes of the slice: x: 2, y: 2, z: 4, core: 2. Of those that a mesh axis runs over, the one named last changes fastest.
Arguments:
- sensitivity: bfloat16 [3, 512, 32768], P(None, 'col', 'slab'), may hold values from -0.046875 to 0.046875
- residual_force: bfloat16 [3, 32768], P(None, 'slab'), may hold values from -6 to 6
- moments: float32 [6, 32, 1024], P(None, 'slab'), as said below
- zone_label: int32 [32, 1024], P('slab'), may hold values from 0 to 511, as said below
- misfit: float32 [32, 1024], P('slab'), may hold values from 0.1 to 10
Outputs:
- hessian: float32 [512, 512], P('col', 'slab')
- gradient: float32 [512], replicated
- zone_misfit: float32 [512], replicated
Inputs may be any that keep to these rules, and one draw needn't show every extreme that they name: zone_label is the box of a 8 x 8 x 8 partition of the specimen that holds the element, the in-plane box borders displaced by at most one element; every zone occurs. `moments`: each element's moment matrix is symmetric with positive diagonal, and each diagonal entry exceeds the sum of the magnitudes of the others in its row.
All inputs are finite; a program needn't handle non-finite values.
Results may differ from a plain program's by a relative error of at most 0.0003.
Values may be sent and summed in bfloat16 or wider, within the bound.
No kernel may reach another device: no remote copies, remote signals or barrier semaphores. Data moves between devices by JAX's collectives and lax.ppermute only.
A program may use at most 128 MiB of HBM per device.

v0:
```python
import functools

import jax
import jax.numpy as jnp
from jax import lax
from jax.experimental import pallas as pl
from jax.experimental.pallas import tpu as pltpu
from jax.sharding import PartitionSpec as P

GX = 64
GY = 16
TILE = 128
EDGE = 256


def exchange(value, axis, by):
    count = lax.axis_size(axis)
    return lax.ppermute(value, axis, [(i, i ^ by) for i in range(count)])


def shifted(value, axis, by):
    count = lax.axis_size(axis)
    pairs = [(i, i + by) for i in range(count) if 0 <= i + by < count]
    return lax.ppermute(value, axis, pairs)


def lane_of(shape):
    return lax.broadcasted_iota(jnp.int32, shape, 1)


def pack_kernel(layers, width, last, target, *refs):
    planes, edges = refs[:layers], refs[layers : 2 * layers]
    first_ref, rest_ref = refs[2 * layers :]
    inside = target[0] != last
    rows = first_ref.shape[0]
    lane = lane_of((rows, TILE))
    for k in range(3):
        first_ref[:, k * width : (k + 1) * width] = planes[0][k]
        for level in range(1, layers):
            start = (3 * (level - 1) + k) * width
            rest_ref[:, start : start + width] = planes[level][k]
    halo = [jnp.zeros((rows, TILE), jnp.float32)] * (EDGE // TILE)
    for k in range(3):
        for level in range(layers):
            tile, at = divmod(edge_at(k, level, layers), TILE)
            edge = edges[level][k].astype(jnp.float32)
            edge = pltpu.roll(edge, at, 1) if at else edge
            halo[tile] = jnp.where((lane >= at) & (lane < at + GY) & inside, edge, halo[tile])
    for tile, value in enumerate(halo):
        start = 3 * width + tile * TILE
        first_ref[:, start : start + TILE] = value.astype(first_ref.dtype)


def edge_at(k, level, layers):
    return (k * (layers + 1) + level) * GY


def pack(sensitivity, target, layers, plane, n_col):
    cols = sensitivity.shape[1]
    width = plane // n_col
    top_block = layers * plane // TILE - 1

    def plane_spec(level):
        return pl.BlockSpec((3, cols, width), lambda i, t: (0, 0, level * n_col + t[0]))

    def edge_spec(level):
        def place(i, t):
            block = (level * plane + (t[0] + 1) * width) // TILE
            return (0, 0, jnp.minimum(block, top_block))

        return pl.BlockSpec((3, cols, TILE), place)

    first = jax.ShapeDtypeStruct((cols, 3 * width + EDGE), sensitivity.dtype)
    rest = jax.ShapeDtypeStruct((cols, 3 * (layers - 1) * width), sensitivity.dtype)
    return pl.pallas_call(
        functools.partial(pack_kernel, layers, width, n_col - 1),
        grid_spec=pltpu.PrefetchScalarGridSpec(
            num_scalar_prefetch=1,
            grid=(1,),
            in_specs=[plane_spec(l) for l in range(layers)] + [edge_spec(l) for l in range(layers)],
            out_specs=[
                pl.BlockSpec(first.shape, lambda i, t: (0, 0)),
                pl.BlockSpec(rest.shape, lambda i, t: (0, 0)),
            ],
        ),
        out_shape=[first, rest],
        compiler_params=pltpu.CompilerParams(vmem_limit_bytes=12 << 20),
        cost_estimate=pl.CostEstimate(flops=0, bytes_accessed=2 << 20, transcendentals=0),
        name="pack",
    )(target, *([sensitivity] * (2 * layers)))


def component(a, b):
    a, b = min(a, b), max(a, b)
    return a if a == b else a + b + 2


def tile_start(k, side, other):
    base = (0, 6, 11)[k]
    return base + (other - k if side == 0 else 3 - k + other)


def build_kernel(layers, width, _, moments_ref, plane_ref, edge_ref, corner_ref, field_ref, ahead_ref):
    f32, bf16 = jnp.float32, jnp.bfloat16
    shape = (GY, width)
    lane = lane_of(shape)
    row = lax.broadcasted_iota(jnp.int32, shape, 0)
    pos_x, pos_y = lane // GY, lane % GY
    same, up, down = row == pos_y, row == pos_y + 1, row == pos_y - 1
    zero = jnp.zeros(shape, f32)
    field_lane = lane_of((8, width))
    columns = width // GY
    near = [pos_x % 3 == r for r in range(3)]
    follow = [(pos_x + 1) % 3 == r for r in range(3)]
    band = [jnp.where((pos_x >= x - 1) & (pos_x <= x + 1), 1.0, 0.0).astype(bf16) for x in range(columns)]
    tile_lane = lane_of((GY, TILE))

    def spread(middle, ahead, behind):
        def whole(value):
            return jnp.broadcast_to(value, shape)

        return jnp.where(same, whole(middle), jnp.where(up, whole(ahead), jnp.where(down, whole(behind), zero)))

    def two_terms(value):
        hi = value.astype(bf16)
        return hi, (value - hi.astype(f32)).astype(bf16)

    edge_ref[...] = jnp.zeros_like(edge_ref)
    field_ref[...] = jnp.zeros_like(field_ref)
    for z in range(layers + 1):
        whole = None
        for level in (z, z - 1):
            if 0 <= level < layers:
                part = moments_ref[:, level, :] * (2.0 / 216.0)
                whole = part if whole is None else whole + part
        field_ref[2 * z, :6] = whole
        if z < layers:
            field_ref[2 * z + 1, :6] = moments_ref[:, z, :] * (1.0 / 216.0)

    for pair in range(2 * layers + 1):
        z, side = divmod(pair, 2)
        element = field_ref[pair]
        before = jnp.where(field_lane >= GY, pltpu.roll(element, GY, 1), 0.0)
        parts = []
        for value in (2.0 * (element + before), element, before):
            lower = jnp.where(field_lane % GY != 0, pltpu.roll(value, 1, 1), 0.0)
            parts.append((2.0 * (value + lower), value, lower))
        for c in range(6):
            here, ahead, behind = [spread(*(v[c : c + 1] for v in part)) for part in parts]
            ahead_ref[pair, c] = ahead[:, width - TILE :]
            scale = 0.5 if side == 0 and c < 3 else None
            spots = []
            for k in range(3):
                for other in range(3):
                    if component(k, other) == c and (side == 1 or other >= k):
                        spots.append(tile_start(k, side, other))
            for r in range(3):
                value = jnp.where(near[r], here, jnp.where(follow[r], ahead, behind))
                if scale is not None:
                    value = value * scale
                for term, piece in enumerate(two_terms(value)):
                    for x in range(r, columns, 3):
                        block = piece * band[x]
                        for spot in spots:
                            start = spot * width + x * GY
                            plane_ref[z, term, start : start + GY, :] = block

    edge_lane = tile_lane // GY == TILE // GY - 1
    for z in range(layers + 1):
        for other_z in range(max(z - 1, 0), min(z + 1, layers) + 1):
            pair = 2 * z if other_z == z else 2 * min(z, other_z) + 1
            for c in range(6):
                value = jnp.where(edge_lane, ahead_ref[pair, c], 0.0)
                for term, piece in enumerate(two_terms(value)):
                    for k in range(3):
                        for other in range(3):
                            if component(k, other) == c:
                                start = edge_at(other, other_z, layers)
                                edge_ref[term, 3 * z + k, start : start + GY, width - TILE :] = piece

    corner_ref[...] = jnp.zeros_like(corner_ref)
    for other_z in range(layers + 1):
        for other in range(3):
            tiles = [jnp.zeros((GY, TILE), f32)] * (EDGE // TILE)
            for z in range(max(other_z - 1, 0), min(other_z + 1, layers) + 1):
                pair = 2 * z if other_z == z else 2 * min(z, other_z) + 1
                for k in range(3):
                    tile, at = divmod(edge_at(k, z, layers), TILE)
                    value = ahead_ref[pair, component(k, other)]
                    turn = (at + GY) % TILE
                    value = pltpu.roll(value, turn, 1) if turn else value
                    tiles[tile] = jnp.where(tile_lane // GY == at // GY, value, tiles[tile])
            start = edge_at(other, other_z, layers)
            for tile, value in enumerate(tiles):
                for term, piece in enumerate(two_terms(value)):
                    corner_ref[term, start : start + GY, tile * TILE : (tile + 1) * TILE] = piece


def build(moments, place, width):
    layers = moments.shape[1]
    shapes = [
        jax.ShapeDtypeStruct((layers + 1, 2, 15 * width, width), jnp.bfloat16),
        jax.ShapeDtypeStruct((2, 3 * (layers + 1), EDGE, width), jnp.bfloat16),
        jax.ShapeDtypeStruct((2, EDGE, EDGE), jnp.bfloat16),
    ]
    return pl.pallas_call(
        functools.partial(build_kernel, layers, width),
        grid_spec=pltpu.PrefetchScalarGridSpec(
            num_scalar_prefetch=1,
            grid=(1,),
            in_specs=[pl.BlockSpec((6, layers, width), lambda i, t: (0, 0, t[0]))],
            out_specs=[pl.BlockSpec(memory_space=pltpu.VMEM)] * 3,
            scratch_shapes=[
                pltpu.VMEM((2 * layers + 1, 8, width), jnp.float32),
                pltpu.VMEM((2 * layers + 1, 6, GY, TILE), jnp.float32),
            ],
        ),
        out_shape=shapes,
        compiler_params=pltpu.CompilerParams(vmem_limit_bytes=32 << 20),
        cost_estimate=pl.CostEstimate(flops=20 << 20, bytes_accessed=24 << 20, transcendentals=0),
        name="build",
    )(place, moments)


def image_kernel(layers, width, first_ref, rest_ref, top_ref, plane_ref, edge_ref, corner_ref, *refs):
    values_ref, image_ref = refs[-2:]
    f32, bf16 = jnp.float32, jnp.bfloat16
    depth = 3 * (layers + 1) * width
    rows = first_ref.shape[0]
    values_ref[:, : 3 * width] = first_ref[:, : 3 * width]
    values_ref[:, 3 * width : 3 * layers * width] = rest_ref[...]
    values_ref[:, 3 * layers * width : depth] = top_ref[:, : 3 * width]
    lane = lane_of((rows, EDGE))
    group = lane // GY
    halo = first_ref[:, 3 * width :].astype(f32)
    top = pltpu.roll(top_ref[:, 3 * width :].astype(f32), layers * GY, 1)
    halo = jnp.where(group % (layers + 1) == layers, top, halo)
    halo = jnp.where(group < 3 * (layers + 1), halo, 0.0).astype(bf16)
    values_ref[:, depth:] = halo

    def dot(a, b):
        return jnp.dot(a, b, preferred_element_type=f32)

    for z in range(layers + 1):
        for k in range(3):
            lo = (3 * z + k) * width
            hi = min(3 * (z + 2) * width, depth)
            value = values_ref[:, lo:hi]
            start = tile_start(k, 0, k) * width
            total = dot(halo, edge_ref[0, 3 * z + k]) + dot(halo, edge_ref[1, 3 * z + k])
            for term in range(2):
                total = total + dot(value, plane_ref[z, term, start : start + hi - lo, :])
            image_ref[:, lo : lo + width] = total.astype(bf16)
    image_ref[:, depth:] = (dot(halo, corner_ref[0]) + dot(halo, corner_ref[1])).astype(bf16)


def image_piece(index, first, rest, top, matrix, buffers, n_col):
    cols = first.shape[0]
    width = (first.shape[1] - EDGE) // 3
    layers = rest.shape[1] // (3 * width) + 1
    total = 3 * (layers + 1) * width + EDGE
    shape = jax.ShapeDtypeStruct((cols * n_col, total), first.dtype)
    in_specs = [pl.BlockSpec(x.shape, lambda i: (0, 0)) for x in (first, rest, top)]
    in_specs += [pl.BlockSpec(memory_space=pltpu.VMEM)] * 3
    args = [first, rest, top, *matrix]
    aliases = {}
    if buffers is not None:
        in_specs += [pl.BlockSpec(memory_space=pl.ANY)] * 2
        args += list(buffers)
        aliases = {6: 0, 7: 1}
    return pl.pallas_call(
        functools.partial(image_kernel, layers, width),
        grid=(1,),
        in_specs=in_specs,
        out_specs=[pl.BlockSpec((cols, total), lambda i: (index, 0))] * 2,
        out_shape=[shape, shape],
        input_output_aliases=aliases,
        compiler_params=pltpu.CompilerParams(vmem_limit_bytes=40 << 20),
        cost_estimate=pl.CostEstimate(
            flops=2 * 164 * cols * width * width, bytes_accessed=4 << 20, transcendentals=0
        ),
        name="image",
    )(*args)


def hessian_kernel(blocks, half, place, values_ref, image_ref, keep_ref, send_ref, total):
    step = pl.program_id(0)

    @pl.when(step == 0)
    def _():
        total[...] = jnp.zeros_like(total)

    total[...] += lax.dot_general(
        values_ref[...], image_ref[...], (((1,), (1,)), ((), ())), preferred_element_type=jnp.float32
    )

    @pl.when(step == pl.num_programs(0) - 1)
    def _():
        full = total[...] + total[...].T
        for b in range(blocks):
            lo = full[2 * b * half : (2 * b + 1) * half, :]
            hi = full[(2 * b + 1) * half : (2 * b + 2) * half, :]
            rows = pl.ds(pl.multiple_of((b ^ place[1]) * half, half), half)
            keep_ref[rows, :] = jnp.where(place[0] == 0, lo, hi)
            send_ref[rows, :] = jnp.where(place[0] == 0, hi, lo)


def partial_hessian(values, image, place, blocks):
    width, depth = values.shape
    half = width // (2 * blocks)
    steps = 4 if depth % (4 * TILE) == 0 else 1
    out = jax.ShapeDtypeStruct((width // 2, width), jnp.float32)
    return pl.pallas_call(
        functools.partial(hessian_kernel, blocks, half),
        grid_spec=pltpu.PrefetchScalarGridSpec(
            num_scalar_prefetch=1,
            grid=(steps,),
            in_specs=[pl.BlockSpec((width, depth // steps), lambda i, t: (0, i))] * 2,
            out_specs=[pl.BlockSpec(out.shape, lambda i, t: (0, 0))] * 2,
            scratch_shapes=[pltpu.VMEM((width, width), jnp.float32)],
        ),
        out_shape=[out, out],
        compiler_params=pltpu.CompilerParams(vmem_limit_bytes=24 << 20),
        cost_estimate=pl.CostEstimate(
            flops=2 * width * width * depth, bytes_accessed=12 << 20, transcendentals=0
        ),
        name="partial_hessian",
    )(place, values, image)


def small_sums(sensitivity, residual_force, zone_label, misfit, me, n_col, width):
    cols = sensitivity.shape[1]
    grad_part = lax.dot_general(
        residual_force,
        sensitivity,
        (((0, 1), (0, 2)), ((), ())),
        preferred_element_type=jnp.float32,
    )
    grad_full = lax.dynamic_update_slice_in_dim(jnp.zeros((width,), jnp.float32), grad_part, me * cols, 0)
    elements = zone_label.size
    share = elements // n_col
    offset = me * share
    zone_part = lax.dynamic_slice_in_dim(zone_label.reshape(elements), offset, share, 0)
    misfit_part = lax.dynamic_slice_in_dim(misfit.reshape(elements), offset, share, 0)
    onehot = (zone_part[:, None] == jnp.arange(width, dtype=jnp.int32)[None, :]).astype(jnp.float32)
    zone_part_sum = jnp.dot(misfit_part, onehot, precision=lax.Precision.HIGHEST)
    return jnp.concatenate([grad_full, zone_part_sum]).reshape(8, -1)


def on_device(sensitivity, residual_force, moments, zone_label, misfit):
    cols = sensitivity.shape[1]
    layers = moments.shape[1]
    plane = GX * GY
    n_slab = lax.axis_size("slab")
    n_col = lax.axis_size("col")
    assert n_slab == 2 * n_col
    width = cols * n_col
    me = lax.axis_index("col").astype(jnp.int32)
    slab = lax.axis_index("slab").astype(jnp.int32)
    core, level_z = slab % 2, slab // 2

    firsts, rests = [], []
    for k in range(n_col):
        first, rest = pack(sensitivity, jnp.reshape(me ^ k, (1,)), layers, plane, n_col)
        if k:
            first, rest = exchange(first, "col", k), exchange(rest, "col", k)
        firsts.append(first)
        rests.append(rest)

    both = small_sums(sensitivity, residual_force, zone_label, misfit, me, n_col, width)
    stages = []
    for axis, count in (("slab", n_slab), ("col", n_col)):
        stages += [(axis, 1 << b) for b in range(count.bit_length() - 1)]
    matrix = build(moments, jnp.reshape(me, (1,)), plane // n_col)
    buffers = None
    for k in range(n_col):
        top = shifted(firsts[k], "slab", -1)
        for axis, by in stages[2 * k : 2 * k + 2]:
            both = both + exchange(both, axis, by)
        both, top = lax.optimization_barrier((both, top))
        buffers = image_piece(k, firsts[k], rests[k], top, matrix, buffers, n_col)
    place = jnp.stack([core, me ^ level_z])
    keep, send = partial_hessian(*buffers, place, n_col)

    mine = keep + exchange(send, "slab", 1)
    parts = [mine[:, k * cols : (k + 1) * cols] for k in range(n_col)]
    mine = parts[0]
    for k in range(1, n_col):
        mine = mine + exchange(parts[k], "col", k)
    half = cols // 2
    parts = [mine[k * half : (k + 1) * half] for k in range(n_col)]
    mine = parts[0]
    for k in range(1, n_col):
        mine = mine + exchange(parts[k], "slab", 2 * k)
    hessian = mine.T

    both = both.reshape(2, width)
    gradient = both[0]
    zone_misfit = both[1] * (width / (layers * plane * n_slab))
    return (hessian, gradient, zone_misfit)


def solution(mesh):
    in_specs = (
        P(None, "col", "slab"),
        P(None, "slab"),
        P(None, "slab", None),
        P("slab", None),
        P("slab", None),
    )
    out_specs = (P("col", "slab"), P(), P())
    return jax.shard_map(
        on_device, mesh=mesh, in_specs=in_specs, out_specs=out_specs, check_vma=False
    )
```

profile of v0, /device:TPU:0, one launch (start us, length us, event | category | flops | bytes accessed | tf_op | source)
XLA Modules:
  0.0 120.9 jit_solution(2230720605105399390)
XLA Ops:
  0.6 1.9 %copy-done = bf16[3,128,4096]{2,1,0:T(8,128)(2,1)S(1)} copy-done((bf16[3,128,4096]{2,1,0:T(8,128)(2,1)S(1)}, bf16[3,128,4096]{2,1,0:T(8,128)(2,1)}, u32[]{:S(2)}) %copy-start) | copy-done | bytes 3145752
  2.5 1.2 pack.6
  3.7 2.9 %collective-permute-start.7 = (bf16[128,1024]{1,0:T(8,128)(2,1)}, bf16[128,1024]{1,0:T(8,128)(2,1)S(1)}, u32[]{:S(2)}, u32[]{:S(2)}) collective-permute-start(bf16[128,1024]{1,0:T(8,128)(2,1)} %get-tuple-element.36), channel_id=1, source_target_pairs={{0,1},{1,0},{2,3},{3,2},{4,5},{5,4},{6,7},{7,6},{8,9},{9,8},{10,11... | collective-permute-start | bytes 786440 | tf_op jit(solution)/shard_map/ppermute | solution.py:18
  6.7 0.9 convolution_bitcast_fusion
  7.8 0.8 fusion
  8.8 1.0 pack.5
  9.8 0.9 copy-done.2
  10.6 1.3 %collective-permute-start.4 = (bf16[128,1024]{1,0:T(8,128)(2,1)}, bf16[128,1024]{1,0:T(8,128)(2,1)}, u32[]{:S(2)}, u32[]{:S(2)}) collective-permute-start(bf16[128,1024]{1,0:T(8,128)(2,1)} %get-tuple-element.34.first_ref), channel_id=1, source_target_pairs={{4,0},{8,4},{12,8},{16,12},{20,16},{24,20},{28,24},{5,1},{9,5},{13... | collective-permute-start | bytes 786440 | tf_op jit(solution)/shard_map/ppermute | solution.py:24
  11.9 1.0 pack.7
  12.9 0.8 copy-done.6
  13.7 1.5 %collective-permute-start.10 = (bf16[128,1024]{1,0:T(8,128)(2,1)}, bf16[128,1024]{1,0:T(8,128)(2,1)}, u32[]{:S(2)}, u32[]{:S(2)}) collective-permute-start(bf16[128,1024]{1,0:T(8,128)(2,1)} %get-tuple-element.38), channel_id=1, source_target_pairs={{0,2},{1,3},{2,0},{3,1},{4,6},{5,7},{6,4},{7,5},{8,10},{9,11},{10,... | collective-permute-start | bytes 786440 | tf_op jit(solution)/shard_map/ppermute | solution.py:18
  15.3 1.0 pack.4
  16.2 0.8 copy-done.5
  17.1 0.9 collective-permute-start
  18.0 1.3 %collective-permute-start.8 = (bf16[128,1024]{1,0:T(8,128)(2,1)S(1)}, bf16[128,1024]{1,0:T(8,128)(2,1)S(1)}, u32[]{:S(2)}, u32[]{:S(2)}) collective-permute-start(bf16[128,1024]{1,0:T(8,128)(2,1)S(1)} %collective-permute-done.7.first_ref), channel_id=1, source_target_pairs={{4,0},{8,4},{12,8},{16,12},{20,16},{24,20},{28,24},{5,1},{9,5},{13... | collective-permute-start | bytes 786440 | tf_op jit(solution)/shard_map/ppermute | solution.py:24
  19.3 3.4 %collective-permute-start.3 = (f32[8,128]{1,0:T(8,128)S(1)}, f32[8,128]{1,0:T(8,128)S(1)}, u32[]{:S(2)}, u32[]{:S(2)}) collective-permute-start(f32[8,128]{1,0:T(8,128)S(1)} %fusion.8), channel_id=1, source_target_pairs={{0,8},{4,12},{8,0},{12,4},{16,24},{20,28},{24,16},{28,20},{1,9},{5... | collective-permute-start | bytes 12296 | tf_op jit(solution)/shard_map/ppermute | solution.py:18
  22.7 4.3 %collective-permute-done.3 = f32[8,128]{1,0:T(8,128)S(1)} collective-permute-done((f32[8,128]{1,0:T(8,128)S(1)}, f32[8,128]{1,0:T(8,128)S(1)}, u32[]{:S(2)}, u32[]{:S(2)}) %collective-permute-start.3) | collective-permute-done | bytes 4128 | tf_op jit(solution)/shard_map/ppermute | solution.py:18
  27.0 1.1 collective-permute-start.14
  28.1 2.6 %collective-permute-start.5 = (f32[8,128]{1,0:T(8,128)S(1)}, f32[8,128]{1,0:T(8,128)S(1)}, u32[]{:S(2)}, u32[]{:S(2)}) collective-permute-start(f32[8,128]{1,0:T(8,128)S(1)} %add.52), channel_id=1, source_target_pairs={{0,16},{4,20},{8,24},{12,28},{16,0},{20,4},{24,8},{28,12},{1,17},{... | collective-permute-start | bytes 12296 | tf_op jit(solution)/shard_map/ppermute | solution.py:18
  30.7 1.9 %collective-permute-done.5 = f32[8,128]{1,0:T(8,128)S(1)} collective-permute-done((f32[8,128]{1,0:T(8,128)S(1)}, f32[8,128]{1,0:T(8,128)S(1)}, u32[]{:S(2)}, u32[]{:S(2)}) %collective-permute-start.5) | collective-permute-done | bytes 4128 | tf_op jit(solution)/shard_map/ppermute | solution.py:18
  32.6 1.0 collective-permute-start.6
  33.5 1.5 %collective-permute-start.13 = (bf16[128,2304]{1,0:T(8,128)(2,1)}, bf16[128,2304]{1,0:T(8,128)(2,1)S(1)}, u32[]{:S(2)}, u32[]{:S(2)}) collective-permute-start(bf16[128,2304]{1,0:T(8,128)(2,1)} %copy-done.6), channel_id=1, source_target_pairs={{0,2},{1,3},{2,0},{3,1},{4,6},{5,7},{6,4},{7,5},{8,10},{9,11},{10,... | collective-permute-start | bytes 1769480 | tf_op jit(solution)/shard_map/ppermute | solution.py:18
  35.0 1.3 %collective-permute-start.11 = (bf16[128,1024]{1,0:T(8,128)(2,1)}, bf16[128,1024]{1,0:T(8,128)(2,1)S(1)}, u32[]{:S(2)}, u32[]{:S(2)}) collective-permute-start(bf16[128,1024]{1,0:T(8,128)(2,1)} %collective-permute-done.10.first_ref), channel_id=1, source_target_pairs={{4,0},{8,4},{12,8},{16,12},{20,16},{24,20},{28,24},{5,1},{9,5},{13... | collective-permute-start | bytes 786440 | tf_op jit(solution)/shard_map/ppermute | solution.py:24
  36.3 3.5 %collective-permute-done.6 = f32[8,128]{1,0:T(8,128)S(1)} collective-permute-done((f32[8,128]{1,0:T(8,128)S(1)}, f32[8,128]{1,0:T(8,128)S(1)}, u32[]{:S(2)}, u32[]{:S(2)}) %collective-permute-start.6) | collective-permute-done | bytes 4128 | tf_op jit(solution)/shard_map/ppermute | solution.py:18
  39.8 1.5 %collective-permute-start.12 = (bf16[128,1024]{1,0:T(8,128)(2,1)S(1)}, bf16[128,1024]{1,0:T(8,128)(2,1)S(1)}, u32[]{:S(2)}, u32[]{:S(2)}) collective-permute-start(bf16[128,1024]{1,0:T(8,128)(2,1)S(1)} %collective-permute-done.first_ref), channel_id=1, source_target_pairs={{4,0},{8,4},{12,8},{16,12},{20,16},{24,20},{28,24},{5,1},{9,5},{13... | collective-permute-start | bytes 786440 | tf_op jit(solution)/shard_map/ppermute | solution.py:24
  41.3 1.6 %collective-permute-start.9 = (f32[8,128]{1,0:T(8,128)S(1)}, f32[8,128]{1,0:T(8,128)S(1)}, u32[]{:S(2)}, u32[]{:S(2)}) collective-permute-start(f32[8,128]{1,0:T(8,128)S(1)} %add.54), channel_id=1, source_target_pairs={{0,2},{1,3},{2,0},{3,1},{4,6},{5,7},{6,4},{7,5},{8,10},{9,11},{10,... | collective-permute-start | bytes 12296 | tf_op jit(solution)/shard_map/ppermute | solution.py:18
  43.0 9.4 %build.1 = (bf16[5,2,3840,256]{3,2,1,0:T(8,128)(2,1)}, bf16[2,15,256,256]{3,2,1,0:T(8,128)(2,1)S(1)}, bf16[2,256,256]{2,1,0:T(8,128)(2,1)S(1)}) custom-call(s32[1]{0:T(128)} %bitcast.9.target._, f32[6,4,1024]{2,1,0:T(4,128)S(1)} %copy-done.4), custom_call_target="tpu_custom_call" | custom-call | flops 20971520 | bytes 25165824 | tf_op jit(solution)/shard_map/build/pallas_call | solution.py:206
  52.4 1.0 collective-permute-start.1
  53.4 1.1 copy-done.3
  54.5 9.8 %image.4 = (bf16[512,4096]{1,0:T(8,128)(2,1)S(1)}, bf16[512,4096]{1,0:T(8,128)(2,1)S(1)}) custom-call(bf16[128,1024]{1,0:T(8,128)(2,1)} %get-tuple-element.34.first_ref, bf16[128,2304]{1,0:T(8,128)(2,1)S(1)} %copy-done.3, bf16[128,1024]{1,0:T(8,128)(2,1)} %collective-permute-done.4.top_ref, bf16[5,2,3840,256]{3,2,1,0:T(8,128)(2,1)} %get-tuple-element.41.plane_ref, ...), custom_call_target="tpu_custom_call" | custom-call | flops 2751463424 | bytes 4194304 | tf_op jit(solution)/shard_map/image/pallas_call | solution.py:271
  64.3 9.6 %image.5 = (bf16[512,4096]{1,0:T(8,128)(2,1)S(1)}, bf16[512,4096]{1,0:T(8,128)(2,1)S(1)}) custom-call(bf16[128,1024]{1,0:T(8,128)(2,1)S(1)} %collective-permute-done.7.first_ref, bf16[128,2304]{1,0:T(8,128)(2,1)S(1)} %collective-permute-done.14.rest_ref, ...), custom_call_target="tpu_custom_call", output_to_operand_aliasing={{0}: (6, {}), {1}: (7, {})} | custom-call | flops 2751463424 | bytes 4194304 | tf_op jit(solution)/shard_map/image/pallas_call | solution.py:271
  73.9 9.9 %image.6 = (bf16[512,4096]{1,0:T(8,128)(2,1)S(1)}, bf16[512,4096]{1,0:T(8,128)(2,1)S(1)}) custom-call(bf16[128,1024]{1,0:T(8,128)(2,1)} %collective-permute-done.10.first_ref, bf16[128,2304]{1,0:T(8,128)(2,1)S(1)} %collective-permute-done.13.rest_ref, ...), custom_call_target="tpu_custom_call", output_to_operand_aliasing={{0}: (6, {}), {1}: (7, {})} | custom-call | flops 2751463424 | bytes 4194304 | tf_op jit(solution)/shard_map/image/pallas_call | solution.py:271
  83.8 9.6 %image.7 = (bf16[512,4096]{1,0:T(8,128)(2,1)S(1)}, bf16[512,4096]{1,0:T(8,128)(2,1)S(1)}) custom-call(bf16[128,1024]{1,0:T(8,128)(2,1)S(1)} %collective-permute-done.first_ref, bf16[128,2304]{1,0:T(8,128)(2,1)S(1)} %collective-permute-done.1.rest_ref, ...), custom_call_target="tpu_custom_call", output_to_operand_aliasing={{0}: (6, {}), {1}: (7, {})} | custom-call | flops 2751463424 | bytes 4194304 | tf_op jit(solution)/shard_map/image/pallas_call | solution.py:271
  93.4 4.6 %partial_hessian.1 = (f32[256,512]{1,0:T(8,128)S(1)}, f32[256,512]{1,0:T(8,128)S(1)}) custom-call(s32[2]{0:T(128)S(1)} %pad_add_fusion.place, bf16[512,4096]{1,0:T(8,128)(2,1)S(1)} %get-tuple-element.56.values_ref, bf16[512,4096]{1,0:T(8,128)(2,1)S(1)} %get-tuple-element.57.image_ref), custom_call_target="tpu_custom_call" | custom-call | flops 2147483648 | bytes 12582912 | tf_op jit(solution)/shard_map/partial_hessian/pallas_call | solution.py:313
  98.0 0.6 collective-permute-start.15
  98.6 1.5 %collective-permute-done.15 = f32[256,512]{1,0:T(8,128)S(1)} collective-permute-done((f32[256,512]{1,0:T(8,128)S(1)}, f32[256,512]{1,0:T(8,128)S(1)}, u32[]{:S(2)}, u32[]{:S(2)}) %collective-permute-start.15) | collective-permute-done | bytes 524320 | tf_op jit(solution)/shard_map/ppermute | solution.py:18
  100.3 1.0 collective-permute-start.16
  101.3 1.5 %collective-permute-start.17 = (f32[256,128]{1,0:T(8,128)S(1)}, f32[256,128]{1,0:T(8,128)S(1)}, u32[]{:S(2)}, u32[]{:S(2)}) collective-permute-start(f32[256,128]{1,0:T(8,128)S(1)} %get-tuple-element.63), channel_id=1, source_target_pairs={{0,2},{1,3},{2,0},{3,1},{4,6},{5,7},{6,4},{7,5},{8,10},{9,11},{10,... | collective-permute-start | bytes 393224 | tf_op jit(solution)/shard_map/ppermute | solution.py:18
  102.9 1.0 collective-permute-start.18
  103.9 2.8 %collective-permute-done.16 = f32[256,128]{1,0:T(8,128)S(1)} collective-permute-done((f32[256,128]{1,0:T(8,128)S(1)}, f32[256,128]{1,0:T(8,128)S(1)}, u32[]{:S(2)}, u32[]{:S(2)}) %collective-permute-start.16) | collective-permute-done | bytes 131104 | tf_op jit(solution)/shard_map/ppermute | solution.py:18
  106.7 2.0 %collective-permute-done.17 = f32[256,128]{1,0:T(8,128)S(1)} collective-permute-done((f32[256,128]{1,0:T(8,128)S(1)}, f32[256,128]{1,0:T(8,128)S(1)}, u32[]{:S(2)}, u32[]{:S(2)}) %collective-permute-start.17) | collective-permute-done | bytes 131104 | tf_op jit(solution)/shard_map/ppermute | solution.py:18
  108.7 1.2 %collective-permute-done.18 = f32[256,128]{1,0:T(8,128)S(1)} collective-permute-done((f32[256,128]{1,0:T(8,128)S(1)}, f32[256,128]{1,0:T(8,128)S(1)}, u32[]{:S(2)}, u32[]{:S(2)}) %collective-permute-start.18) | collective-permute-done | bytes 131104 | tf_op jit(solution)/shard_map/ppermute | solution.py:18
  110.0 2.0 %collective-permute-start.19 = (f32[64,128]{1,0:T(8,128)S(1)}, f32[64,128]{1,0:T(8,128)S(1)}, u32[]{:S(2)}, u32[]{:S(2)}) collective-permute-start(f32[64,128]{1,0:T(8,128)S(1)} %get-tuple-element.64), channel_id=1, source_target_pairs={{0,8},{4,12},{8,0},{12,4},{16,24},{20,28},{24,16},{28,20},{1,9},{5... | collective-permute-start | bytes 98312 | tf_op jit(solution)/shard_map/ppermute | solution.py:18
  112.0 2.6 %collective-permute-start.20 = (f32[64,128]{1,0:T(8,128)S(1)}, f32[64,128]{1,0:T(8,128)S(1)}, u32[]{:S(2)}, u32[]{:S(2)}) collective-permute-start(f32[64,128]{1,0:T(8,128)S(1)} %get-tuple-element.66), channel_id=1, source_target_pairs={{0,16},{4,20},{8,24},{12,28},{16,0},{20,4},{24,8},{28,12},{1,17},{... | collective-permute-start | bytes 98312 | tf_op jit(solution)/shard_map/ppermute | solution.py:18
  114.6 0.6 multiply_bitcast_fusion
  115.2 1.9 %collective-permute-done.20 = f32[64,128]{1,0:T(8,128)S(1)} collective-permute-done((f32[64,128]{1,0:T(8,128)S(1)}, f32[64,128]{1,0:T(8,128)S(1)}, u32[]{:S(2)}, u32[]{:S(2)}) %collective-permute-start.20) | collective-permute-done | bytes 32800 | tf_op jit(solution)/shard_map/ppermute | solution.py:18
  117.1 3.2 %collective-permute-done.21 = f32[64,128]{1,0:T(8,128)S(1)} collective-permute-done((f32[64,128]{1,0:T(8,128)S(1)}, f32[64,128]{1,0:T(8,128)S(1)}, u32[]{:S(2)}, u32[]{:S(2)}) %collective-permute-start.21) | collective-permute-done | bytes 32800 | tf_op jit(solution)/shard_map/ppermute | solution.py:18
  120.3 0.6 fusion.7
  (47 shorter events, 0.6 us)
Async XLA Ops:
  0.6 1.9 %copy-start = (bf16[3,128,4096]{2,1,0:T(8,128)(2,1)S(1)}, bf16[3,128,4096]{2,1,0:T(8,128)(2,1)}, u32[]{:S(2)}) copy-start(bf16[3,128,4096]{2,1,0:T(8,128)(2,1)} %refs_7_.7) | copy-start | bytes 9437188
  2.5 4.1 %copy-start.8 = (f32[4,1024]{1,0:T(4,128)S(1)}, f32[4,1024]{1,0:T(4,128)}, u32[]{:S(2)}) copy-start(f32[4,1024]{1,0:T(4,128)} %param.9) | copy-start | bytes 49156
  2.5 4.1 %copy-start.9 = (s32[4,1024]{1,0:T(4,128)S(1)}, s32[4,1024]{1,0:T(4,128)}, u32[]{:S(2)}) copy-start(s32[4,1024]{1,0:T(4,128)} %param.8) | copy-start | bytes 49156
  2.5 4.2 %copy-start.1 = (bf16[3,128,4096]{2,1,0:T(8,128)(2,1)S(1)}, bf16[3,128,4096]{2,1,0:T(8,128)(2,1)}, u32[]{:S(2)}) copy-start(bf16[3,128,4096]{2,1,0:T(8,128)(2,1)} %refs_7_.7) | copy-start | bytes 9437188
  2.5 4.2 %copy-start.7 = (bf16[3,4096]{1,0:T(4,128)(2,1)S(1)}, bf16[3,4096]{1,0:T(4,128)(2,1)}, u32[]{:S(2)}) copy-start(bf16[3,4096]{1,0:T(4,128)(2,1)} %param.6) | copy-start | bytes 73732
  3.7 14.2 %collective-permute-start.7 = (bf16[128,1024]{1,0:T(8,128)(2,1)}, bf16[128,1024]{1,0:T(8,128)(2,1)S(1)}, u32[]{:S(2)}, u32[]{:S(2)}) collective-permute-start(bf16[128,1024]{1,0:T(8,128)(2,1)} %get-tuple-element.36), channel_id=1, source_target_pairs={{0,1},{1,0},{2,3},{3,2},{4,5},{5,4},{6,7},{7,6},{8,9},{9,8},{10,11... | collective-permute-start | bytes 786440 | tf_op jit(solution)/shard_map/ppermute | solution.py:18
  8.7 10.6 %collective-permute-start.2 = (f32[8,128]{1,0:T(8,128)S(1)}, f32[8,128]{1,0:T(8,128)S(1)}, u32[]{:S(2)}, u32[]{:S(2)}) collective-permute-start(f32[8,128]{1,0:T(8,128)S(1)} %pad_maximum_fusion), channel_id=1, source_target_pairs={{0,4},{4,0},{8,12},{12,8},{16,20},{20,16},{24,28},{28,24},{1,5},{5... | collective-permute-start | bytes 12296 | tf_op jit(solution)/shard_map/ppermute | solution.py:18
  9.7 0.9 copy-start.2
  10.6 17.4 %collective-permute-start.4 = (bf16[128,1024]{1,0:T(8,128)(2,1)}, bf16[128,1024]{1,0:T(8,128)(2,1)}, u32[]{:S(2)}, u32[]{:S(2)}) collective-permute-start(bf16[128,1024]{1,0:T(8,128)(2,1)} %get-tuple-element.34.first_ref), channel_id=1, source_target_pairs={{4,0},{8,4},{12,8},{16,12},{20,16},{24,20},{28,24},{5,1},{9,5},{13... | collective-permute-start | bytes 786440 | tf_op jit(solution)/shard_map/ppermute | solution.py:24
  12.9 0.8 copy-start.6
  13.7 19.8 %collective-permute-start.10 = (bf16[128,1024]{1,0:T(8,128)(2,1)}, bf16[128,1024]{1,0:T(8,128)(2,1)}, u32[]{:S(2)}, u32[]{:S(2)}) collective-permute-start(bf16[128,1024]{1,0:T(8,128)(2,1)} %get-tuple-element.38), channel_id=1, source_target_pairs={{0,2},{1,3},{2,0},{3,1},{4,6},{5,7},{6,4},{7,5},{8,10},{9,11},{10,... | collective-permute-start | bytes 786440 | tf_op jit(solution)/shard_map/ppermute | solution.py:18
  15.3 27.7 %copy-start.4 = (f32[6,4,1024]{2,1,0:T(4,128)S(1)}, f32[6,4,1024]{2,1,0:T(4,128)}, u32[]{:S(2)}) copy-start(f32[6,4,1024]{2,1,0:T(4,128)} %moments_ref.1) | copy-start | bytes 294916
  16.2 0.8 copy-start.5
  17.1 18.0 %collective-permute-start = (bf16[128,1024]{1,0:T(8,128)(2,1)}, bf16[128,1024]{1,0:T(8,128)(2,1)S(1)}, u32[]{:S(2)}, u32[]{:S(2)}) collective-permute-start(bf16[128,1024]{1,0:T(8,128)(2,1)} %get-tuple-element.32), channel_id=1, source_target_pairs={{0,3},{1,2},{2,1},{3,0},{4,7},{5,6},{6,5},{7,4},{8,11},{9,10},{10,... | collective-permute-start | bytes 786440 | tf_op jit(solution)/shard_map/ppermute | solution.py:18
  18.0 23.4 %collective-permute-start.8 = (bf16[128,1024]{1,0:T(8,128)(2,1)S(1)}, bf16[128,1024]{1,0:T(8,128)(2,1)S(1)}, u32[]{:S(2)}, u32[]{:S(2)}) collective-permute-start(bf16[128,1024]{1,0:T(8,128)(2,1)S(1)} %collective-permute-done.7.first_ref), channel_id=1, source_target_pairs={{4,0},{8,4},{12,8},{16,12},{20,16},{24,20},{28,24},{5,1},{9,5},{13... | collective-permute-start | bytes 786440 | tf_op jit(solution)/shard_map/ppermute | solution.py:24
  19.3 7.7 %collective-permute-start.3 = (f32[8,128]{1,0:T(8,128)S(1)}, f32[8,128]{1,0:T(8,128)S(1)}, u32[]{:S(2)}, u32[]{:S(2)}) collective-permute-start(f32[8,128]{1,0:T(8,128)S(1)} %fusion.8), channel_id=1, source_target_pairs={{0,8},{4,12},{8,0},{12,4},{16,24},{20,28},{24,16},{28,20},{1,9},{5... | collective-permute-start | bytes 12296 | tf_op jit(solution)/shard_map/ppermute | solution.py:18
  27.0 37.3 %collective-permute-start.14 = (bf16[128,2304]{1,0:T(8,128)(2,1)}, bf16[128,2304]{1,0:T(8,128)(2,1)S(1)}, u32[]{:S(2)}, u32[]{:S(2)}) collective-permute-start(bf16[128,2304]{1,0:T(8,128)(2,1)} %get-tuple-element.46), channel_id=1, source_target_pairs={{0,1},{1,0},{2,3},{3,2},{4,5},{5,4},{6,7},{7,6},{8,9},{9,8},{10,11... | collective-permute-start | bytes 1769480 | tf_op jit(solution)/shard_map/ppermute | solution.py:18
  28.1 4.5 %collective-permute-start.5 = (f32[8,128]{1,0:T(8,128)S(1)}, f32[8,128]{1,0:T(8,128)S(1)}, u32[]{:S(2)}, u32[]{:S(2)}) collective-permute-start(f32[8,128]{1,0:T(8,128)S(1)} %add.52), channel_id=1, source_target_pairs={{0,16},{4,20},{8,24},{12,28},{16,0},{20,4},{24,8},{28,12},{1,17},{... | collective-permute-start | bytes 12296 | tf_op jit(solution)/shard_map/ppermute | solution.py:18
  32.6 7.3 %collective-permute-start.6 = (f32[8,128]{1,0:T(8,128)S(1)}, f32[8,128]{1,0:T(8,128)S(1)}, u32[]{:S(2)}, u32[]{:S(2)}) collective-permute-start(f32[8,128]{1,0:T(8,128)S(1)} %add.53), channel_id=1, source_target_pairs={{0,1},{1,0},{2,3},{3,2},{4,5},{5,4},{6,7},{7,6},{8,9},{9,8},{10,11... | collective-permute-start | bytes 12296 | tf_op jit(solution)/shard_map/ppermute | solution.py:18
  33.5 40.4 %collective-permute-start.13 = (bf16[128,2304]{1,0:T(8,128)(2,1)}, bf16[128,2304]{1,0:T(8,128)(2,1)S(1)}, u32[]{:S(2)}, u32[]{:S(2)}) collective-permute-start(bf16[128,2304]{1,0:T(8,128)(2,1)} %copy-done.6), channel_id=1, source_target_pairs={{0,2},{1,3},{2,0},{3,1},{4,6},{5,7},{6,4},{7,5},{8,10},{9,11},{10,... | collective-permute-start | bytes 1769480 | tf_op jit(solution)/shard_map/ppermute | solution.py:18
  35.0 29.2 %collective-permute-start.11 = (bf16[128,1024]{1,0:T(8,128)(2,1)}, bf16[128,1024]{1,0:T(8,128)(2,1)S(1)}, u32[]{:S(2)}, u32[]{:S(2)}) collective-permute-start(bf16[128,1024]{1,0:T(8,128)(2,1)} %collective-permute-done.10.first_ref), channel_id=1, source_target_pairs={{4,0},{8,4},{12,8},{16,12},{20,16},{24,20},{28,24},{5,1},{9,5},{13... | collective-permute-start | bytes 786440 | tf_op jit(solution)/shard_map/ppermute | solution.py:24
  39.8 24.4 %collective-permute-start.12 = (bf16[128,1024]{1,0:T(8,128)(2,1)S(1)}, bf16[128,1024]{1,0:T(8,128)(2,1)S(1)}, u32[]{:S(2)}, u32[]{:S(2)}) collective-permute-start(bf16[128,1024]{1,0:T(8,128)(2,1)S(1)} %collective-permute-done.first_ref), channel_id=1, source_target_pairs={{4,0},{8,4},{12,8},{16,12},{20,16},{24,20},{28,24},{5,1},{9,5},{13... | collective-permute-start | bytes 786440 | tf_op jit(solution)/shard_map/ppermute | solution.py:24
  41.3 11.0 %collective-permute-start.9 = (f32[8,128]{1,0:T(8,128)S(1)}, f32[8,128]{1,0:T(8,128)S(1)}, u32[]{:S(2)}, u32[]{:S(2)}) collective-permute-start(f32[8,128]{1,0:T(8,128)S(1)} %add.54), channel_id=1, source_target_pairs={{0,2},{1,3},{2,0},{3,1},{4,6},{5,7},{6,4},{7,5},{8,10},{9,11},{10,... | collective-permute-start | bytes 12296 | tf_op jit(solution)/shard_map/ppermute | solution.py:18
  52.4 31.5 %collective-permute-start.1 = (bf16[128,2304]{1,0:T(8,128)(2,1)}, bf16[128,2304]{1,0:T(8,128)(2,1)S(1)}, u32[]{:S(2)}, u32[]{:S(2)}) collective-permute-start(bf16[128,2304]{1,0:T(8,128)(2,1)} %copy-done.5), channel_id=1, source_target_pairs={{0,3},{1,2},{2,1},{3,0},{4,7},{5,6},{6,5},{7,4},{8,11},{9,10},{10,... | collective-permute-start | bytes 1769480 | tf_op jit(solution)/shard_map/ppermute | solution.py:18
  53.4 1.1 copy-start.3
  98.0 2.2 %collective-permute-start.15 = (f32[256,512]{1,0:T(8,128)S(1)}, f32[256,512]{1,0:T(8,128)S(1)}, u32[]{:S(2)}, u32[]{:S(2)}) collective-permute-start(f32[256,512]{1,0:T(8,128)S(1)} %get-tuple-element.59), channel_id=1, source_target_pairs={{0,4},{4,0},{8,12},{12,8},{16,20},{20,16},{24,28},{28,24},{1,5},{5... | collective-permute-start | bytes 1572872 | tf_op jit(solution)/shard_map/ppermute | solution.py:18
  100.3 6.4 %collective-permute-start.16 = (f32[256,128]{1,0:T(8,128)S(1)}, f32[256,128]{1,0:T(8,128)S(1)}, u32[]{:S(2)}, u32[]{:S(2)}) collective-permute-start(f32[256,128]{1,0:T(8,128)S(1)} %get-tuple-element.61), channel_id=1, source_target_pairs={{0,1},{1,0},{2,3},{3,2},{4,5},{5,4},{6,7},{7,6},{8,9},{9,8},{10,11... | collective-permute-start | bytes 393224 | tf_op jit(solution)/shard_map/ppermute | solution.py:18
  101.3 7.3 %collective-permute-start.17 = (f32[256,128]{1,0:T(8,128)S(1)}, f32[256,128]{1,0:T(8,128)S(1)}, u32[]{:S(2)}, u32[]{:S(2)}) collective-permute-start(f32[256,128]{1,0:T(8,128)S(1)} %get-tuple-element.63), channel_id=1, source_target_pairs={{0,2},{1,3},{2,0},{3,1},{4,6},{5,7},{6,4},{7,5},{8,10},{9,11},{10,... | collective-permute-start | bytes 393224 | tf_op jit(solution)/shard_map/ppermute | solution.py:18
  102.9 7.1 %collective-permute-start.18 = (f32[256,128]{1,0:T(8,128)S(1)}, f32[256,128]{1,0:T(8,128)S(1)}, u32[]{:S(2)}, u32[]{:S(2)}) collective-permute-start(f32[256,128]{1,0:T(8,128)S(1)} %get-tuple-element.62), channel_id=1, source_target_pairs={{0,3},{1,2},{2,1},{3,0},{4,7},{5,6},{6,5},{7,4},{8,11},{9,10},{10,... | collective-permute-start | bytes 393224 | tf_op jit(solution)/shard_map/ppermute | solution.py:18
  110.0 5.2 %collective-permute-start.19 = (f32[64,128]{1,0:T(8,128)S(1)}, f32[64,128]{1,0:T(8,128)S(1)}, u32[]{:S(2)}, u32[]{:S(2)}) collective-permute-start(f32[64,128]{1,0:T(8,128)S(1)} %get-tuple-element.64), channel_id=1, source_target_pairs={{0,8},{4,12},{8,0},{12,4},{16,24},{20,28},{24,16},{28,20},{1,9},{5... | collective-permute-start | bytes 98312 | tf_op jit(solution)/shard_map/ppermute | solution.py:18
  112.0 5.1 %collective-permute-start.20 = (f32[64,128]{1,0:T(8,128)S(1)}, f32[64,128]{1,0:T(8,128)S(1)}, u32[]{:S(2)}, u32[]{:S(2)}) collective-permute-start(f32[64,128]{1,0:T(8,128)S(1)} %get-tuple-element.66), channel_id=1, source_target_pairs={{0,16},{4,20},{8,24},{12,28},{16,0},{20,4},{24,8},{28,12},{1,17},{... | collective-permute-start | bytes 98312 | tf_op jit(solution)/shard_map/ppermute | solution.py:18
  114.6 5.7 %collective-permute-start.21 = (f32[64,128]{1,0:T(8,128)S(1)}, f32[64,128]{1,0:T(8,128)S(1)}, u32[]{:S(2)}, u32[]{:S(2)}) collective-permute-start(f32[64,128]{1,0:T(8,128)S(1)} %get-tuple-element.65), channel_id=1, source_target_pairs={{0,24},{4,28},{8,16},{12,20},{16,8},{20,12},{24,0},{28,4},{1,25},{... | collective-permute-start | bytes 98312 | tf_op jit(solution)/shard_map/ppermute | solution.py:18
where the time goes:
time: 121 us
  Pallas kernels  57 us (47%)
  starting transfers between devices  31.8 us (26%)
  waiting for transfers between devices  22.4 us (19%)
  local copies, waits for them, and re-layouts  5.72 us (5%)
  matrix products  1.72 us (1%)
  other arithmetic  1.44 us (1%)
    pallas_call x4, Pallas kernels, image_piece(): pl.pallas_call(functools.partial(image_kernel, layers, width), grid=(1,),...  38.9 us
    ppermute x18, starting transfers between devices, exchange(): return lax.ppermute(value, axis, [(i, i ^ by) for i in range(count)])  26.5 us
    ppermute x18, waiting for transfers between devices, exchange(): return lax.ppermute(value, axis, [(i, i ^ by) for i in range(count)])  22.4 us
    pallas_call x1, Pallas kernels, build(): pl.pallas_call(functools.partial(build_kernel, layers, width), grid_spec=...  9.38 us
    unnamed x22, local copies, waits for them, and re-layouts  5.47 us
    ppermute x4, starting transfers between devices, shifted(): return lax.ppermute(value, axis, pairs)  5.3 us
    pallas_call x1, Pallas kernels, partial_hessian(): pl.pallas_call(functools.partial(hessian_kernel, blocks, half), grid_spec...  4.58 us
    pallas_call x4, Pallas kernels, pack(): pl.pallas_call(functools.partial(pack_kernel, layers, width, n_col - 1),...  4.17 us
  transfers between devices with their start and end apart: 22, of which 9 were waited for; matrix products, arithmetic and copies ran while one was open for 2% of the time, Pallas kernels for 34%

commit v1 on v0

--- a/solution.py
+++ b/solution.py
@@ -30,14 +30,15 @@
 
 def pack_kernel(layers, width, last, target, *refs):
     planes, edges = refs[:layers], refs[layers : 2 * layers]
-    first_ref, rest_ref = refs[2 * layers :]
+    first_ref, rest_ref = refs[2 * layers], refs[-1]
+    offset = 0 if rest_ref is not first_ref else 3 * width + EDGE
     inside = target[0] != last
     rows = first_ref.shape[0]
     lane = lane_of((rows, TILE))
     for k in range(3):
         first_ref[:, k * width : (k + 1) * width] = planes[0][k]
         for level in range(1, layers):
-            start = (3 * (level - 1) + k) * width
+            start = offset + (3 * (level - 1) + k) * width
             rest_ref[:, start : start + width] = planes[level][k]
     halo = [jnp.zeros((rows, TILE), jnp.float32)] * (EDGE // TILE)
     for k in range(3):
@@ -55,7 +56,7 @@
     return (k * (layers + 1) + level) * GY
 
 
-def pack(sensitivity, target, layers, plane, n_col):
+def pack(sensitivity, target, layers, plane, n_col, split):
     cols = sensitivity.shape[1]
     width = plane // n_col
     top_block = layers * plane // TILE - 1
@@ -70,20 +71,17 @@
 
         return pl.BlockSpec((3, cols, TILE), place)
 
-    first = jax.ShapeDtypeStruct((cols, 3 * width + EDGE), sensitivity.dtype)
-    rest = jax.ShapeDtypeStruct((cols, 3 * (layers - 1) * width), sensitivity.dtype)
+    sizes = [3 * width + EDGE, 3 * (layers - 1) * width]
+    outs = [jax.ShapeDtypeStruct((cols, size), sensitivity.dtype) for size in (sizes if split else [sum(sizes)])]
     return pl.pallas_call(
         functools.partial(pack_kernel, layers, width, n_col - 1),
         grid_spec=pltpu.PrefetchScalarGridSpec(
             num_scalar_prefetch=1,
             grid=(1,),
             in_specs=[plane_spec(l) for l in range(layers)] + [edge_spec(l) for l in range(layers)],
-            out_specs=[
-                pl.BlockSpec(first.shape, lambda i, t: (0, 0)),
-                pl.BlockSpec(rest.shape, lambda i, t: (0, 0)),
-            ],
+            out_specs=[pl.BlockSpec(out.shape, lambda i, t: (0, 0)) for out in outs],
         ),
-        out_shape=[first, rest],
+        out_shape=outs,
         compiler_params=pltpu.CompilerParams(vmem_limit_bytes=12 << 20),
         cost_estimate=pl.CostEstimate(flops=0, bytes_accessed=2 << 20, transcendentals=0),
         name="pack",
@@ -196,14 +194,18 @@
                     corner_ref[term, start : start + GY, tile * TILE : (tile + 1) * TILE] = piece
 
 
+def in_vmem(x):
+    return pltpu.with_memory_space_constraint(x, pltpu.VMEM)
+
+
 def build(moments, place, width):
     layers = moments.shape[1]
     shapes = [
-        jax.ShapeDtypeStruct((layers + 1, 2, 15 * width, width), jnp.bfloat16),
-        jax.ShapeDtypeStruct((2, 3 * (layers + 1), EDGE, width), jnp.bfloat16),
-        jax.ShapeDtypeStruct((2, EDGE, EDGE), jnp.bfloat16),
+        pltpu.VMEM((layers + 1, 2, 15 * width, width), jnp.bfloat16),
+        pltpu.VMEM((2, 3 * (layers + 1), EDGE, width), jnp.bfloat16),
+        pltpu.VMEM((2, EDGE, EDGE), jnp.bfloat16),
     ]
-    return pl.pallas_call(
+    out = pl.pallas_call(
         functools.partial(build_kernel, layers, width),
         grid_spec=pltpu.PrefetchScalarGridSpec(
             num_scalar_prefetch=1,
@@ -216,23 +218,36 @@
             ],
         ),
         out_shape=shapes,
-        compiler_params=pltpu.CompilerParams(vmem_limit_bytes=32 << 20),
+        compiler_params=pltpu.CompilerParams(vmem_limit_bytes=6 << 20),
         cost_estimate=pl.CostEstimate(flops=20 << 20, bytes_accessed=24 << 20, transcendentals=0),
         name="build",
     )(place, moments)
-
-
-def image_kernel(layers, width, first_ref, rest_ref, top_ref, plane_ref, edge_ref, corner_ref, *refs):
-    values_ref, image_ref = refs[-2:]
+    return [in_vmem(x) for x in out]
+
+
+def image_kernel(layers, width, parts, index, blocks, *refs):
+    refs = list(refs)
+    pieces = [refs.pop(0) for _ in range(parts)]
+    first_ref, rest_ref = pieces[0], pieces[-1]
+    offset = 0 if parts == 2 else 3 * width + EDGE
+    top_ref, plane_ref, edge_ref, corner_ref = (refs.pop(0) for _ in range(4))
+    before = [(refs.pop(0), refs.pop(0)) for _ in range(index)]
+    last = index == blocks - 1
+    if last:
+        block_refs = [refs.pop(0) for _ in range(index)]
+        place = refs.pop(0)
+        keep_ref, send_ref, values_ref, image_ref = refs
+    else:
+        values_ref, image_ref, block_ref = refs
     f32, bf16 = jnp.float32, jnp.bfloat16
     depth = 3 * (layers + 1) * width
     rows = first_ref.shape[0]
     values_ref[:, : 3 * width] = first_ref[:, : 3 * width]
-    values_ref[:, 3 * width : 3 * layers * width] = rest_ref[...]
+    values_ref[:, 3 * width : 3 * layers * width] = rest_ref[:, offset:]
     values_ref[:, 3 * layers * width : depth] = top_ref[:, : 3 * width]
     lane = lane_of((rows, EDGE))
     group = lane // GY
-    halo = first_ref[:, 3 * width :].astype(f32)
+    halo = first_ref[:, 3 * width : 3 * width + EDGE].astype(f32)
     top = pltpu.roll(top_ref[:, 3 * width :].astype(f32), layers * GY, 1)
     halo = jnp.where(group % (layers + 1) == layers, top, halo)
     halo = jnp.where(group < 3 * (layers + 1), halo, 0.0).astype(bf16)
@@ -253,79 +268,56 @@
             image_ref[:, lo : lo + width] = total.astype(bf16)
     image_ref[:, depth:] = (dot(halo, corner_ref[0]) + dot(halo, corner_ref[1])).astype(bf16)
 
-
-def image_piece(index, first, rest, top, matrix, buffers, n_col):
-    cols = first.shape[0]
-    width = (first.shape[1] - EDGE) // 3
-    layers = rest.shape[1] // (3 * width) + 1
+    def product(a, b):
+        return lax.dot_general(a[...], b[...], (((1,), (1,)), ((), ())), preferred_element_type=f32)
+
+    found = [product(v, image_ref) + product(i, values_ref) for v, i in before]
+    own = product(values_ref, image_ref)
+    found.append(own + own.T)
+    if not last:
+        for j, value in enumerate(found):
+            block_ref[j] = value
+        return
+    half = rows // 2
+    for i in range(blocks):
+        at = pl.ds(pl.multiple_of((i ^ place[1]) * half, half), half)
+        for j in range(blocks):
+            lo, hi = min(i, j), max(i, j)
+            block = found[lo] if hi == index else block_refs[hi][lo]
+            block = block.T if i > j else block
+            for ref, low in ((keep_ref, 0), (send_ref, 1)):
+                ref[at, j * rows : (j + 1) * rows] = jnp.where(place[0] == low, block[:half], block[half:])
+
+
+def image_piece(index, piece, top, matrix, before, blocks, place, n_col):
+    cols = top.shape[0]
+    width = (top.shape[1] - EDGE) // 3
+    layers = (sum(x.shape[1] for x in piece) - EDGE) // (3 * width)
     total = 3 * (layers + 1) * width + EDGE
-    shape = jax.ShapeDtypeStruct((cols * n_col, total), first.dtype)
-    in_specs = [pl.BlockSpec(x.shape, lambda i: (0, 0)) for x in (first, rest, top)]
-    in_specs += [pl.BlockSpec(memory_space=pltpu.VMEM)] * 3
-    args = [first, rest, top, *matrix]
-    aliases = {}
-    if buffers is not None:
-        in_specs += [pl.BlockSpec(memory_space=pl.ANY)] * 2
-        args += list(buffers)
-        aliases = {6: 0, 7: 1}
-    return pl.pallas_call(
-        functools.partial(image_kernel, layers, width),
-        grid=(1,),
+    args = [*piece, top, *matrix, *(x for pair in before for x in pair)]
+    shape = pltpu.VMEM((cols, total), top.dtype)
+    scratch = []
+    vmem = pl.BlockSpec(memory_space=pltpu.VMEM)
+    in_specs = [vmem] * len(args)
+    if index == n_col - 1:
+        args += [*blocks, place]
+        in_specs += [vmem] * len(blocks) + [pl.BlockSpec(memory_space=pltpu.SMEM)]
+        outs = [pltpu.VMEM((cols * n_col // 2, cols * n_col), jnp.float32)] * 2
+        scratch = [shape] * 2
+    else:
+        outs = [shape, shape, pltpu.VMEM((index + 1, cols, cols), jnp.float32)]
+    flops = 2 * 164 * cols * width * width + 4 * (index + 1) * cols * cols * total
+    out = pl.pallas_call(
+        functools.partial(image_kernel, layers, width, len(piece), index, n_col),
         in_specs=in_specs,
-        out_specs=[pl.BlockSpec((cols, total), lambda i: (index, 0))] * 2,
-        out_shape=[shape, shape],
-        input_output_aliases=aliases,
-        compiler_params=pltpu.CompilerParams(vmem_limit_bytes=40 << 20),
-        cost_estimate=pl.CostEstimate(
-            flops=2 * 164 * cols * width * width, bytes_accessed=4 << 20, transcendentals=0
-        ),
+        out_specs=[vmem] * len(outs),
+        out_shape=outs,
+        scratch_shapes=scratch,
+        compiler_params=pltpu.CompilerParams(vmem_limit_bytes=8 << 20),
+        cost_estimate=pl.CostEstimate(flops=flops, bytes_accessed=24 << 20, transcendentals=0),
         name="image",
     )(*args)
-
-
-def hessian_kernel(blocks, half, place, values_ref, image_ref, keep_ref, send_ref, total):
-    step = pl.program_id(0)
-
-    @pl.when(step == 0)
-    def _():
-        total[...] = jnp.zeros_like(total)
-
-    total[...] += lax.dot_general(
-        values_ref[...], image_ref[...], (((1,), (1,)), ((), ())), preferred_element_type=jnp.float32
-    )
-
-    @pl.when(step == pl.num_programs(0) - 1)
-    def _():
-        full = total[...] + total[...].T
-        for b in range(blocks):
-            lo = full[2 * b * half : (2 * b + 1) * half, :]
-            hi = full[(2 * b + 1) * half : (2 * b + 2) * half, :]
-            rows = pl.ds(pl.multiple_of((b ^ place[1]) * half, half), half)
-            keep_ref[rows, :] = jnp.where(place[0] == 0, lo, hi)
-            send_ref[rows, :] = jnp.where(place[0] == 0, hi, lo)
-
-
-def partial_hessian(values, image, place, blocks):
-    width, depth = values.shape
-    half = width // (2 * blocks)
-    steps = 4 if depth % (4 * TILE) == 0 else 1
-    out = jax.ShapeDtypeStruct((width // 2, width), jnp.float32)
-    return pl.pallas_call(
-        functools.partial(hessian_kernel, blocks, half),
-        grid_spec=pltpu.PrefetchScalarGridSpec(
-            num_scalar_prefetch=1,
-            grid=(steps,),
-            in_specs=[pl.BlockSpec((width, depth // steps), lambda i, t: (0, i))] * 2,
-            out_specs=[pl.BlockSpec(out.shape, lambda i, t: (0, 0))] * 2,
-            scratch_shapes=[pltpu.VMEM((width, width), jnp.float32)],
-        ),
-        out_shape=[out, out],
-        compiler_params=pltpu.CompilerParams(vmem_limit_bytes=24 << 20),
-        cost_estimate=pl.CostEstimate(
-            flops=2 * width * width * depth, bytes_accessed=12 << 20, transcendentals=0
-        ),
-        name="partial_hessian",
-    )(place, values, image)
+    return out if index == n_col - 1 else [in_vmem(x) for x in out]
 
 
 def small_sums(sensitivity, residual_force, zone_label, misfit, me, n_col, width):
@@ -359,28 +351,29 @@
     slab = lax.axis_index("slab").astype(jnp.int32)
     core, level_z = slab % 2, slab // 2
 
-    firsts, rests = [], []
-    for k in range(n_col):
-        first, rest = pack(sensitivity, jnp.reshape(me ^ k, (1,)), layers, plane, n_col)
-        if k:
-            first, rest = exchange(first, "col", k), exchange(rest, "col", k)
-        firsts.append(first)
-        rests.append(rest)
-
+    source = pltpu.with_memory_space_constraint(sensitivity, pltpu.HBM)
+    bottom = 3 * (plane // n_col) + EDGE
+    pieces = [None] * n_col
+    for k in (*range(1, n_col), 0):
+        packed = pack(source, jnp.reshape(me ^ k, (1,)), layers, plane, n_col, k == n_col - 1)
+        pieces[k] = [exchange(x, "col", k) if k else x for x in packed]
     both = small_sums(sensitivity, residual_force, zone_label, misfit, me, n_col, width)
     stages = []
     for axis, count in (("slab", n_slab), ("col", n_col)):
         stages += [(axis, 1 << b) for b in range(count.bit_length() - 1)]
     matrix = build(moments, jnp.reshape(me, (1,)), plane // n_col)
-    buffers = None
+    place = jnp.stack([core, me ^ level_z])
+    before, blocks = [], []
     for k in range(n_col):
-        top = shifted(firsts[k], "slab", -1)
-        for axis, by in stages[2 * k : 2 * k + 2]:
+        top = shifted(pieces[k][0][:, :bottom], "slab", -1)
+        for axis, by in stages[k :: n_col]:
             both = both + exchange(both, axis, by)
         both, top = lax.optimization_barrier((both, top))
-        buffers = image_piece(k, firsts[k], rests[k], top, matrix, buffers, n_col)
-    place = jnp.stack([core, me ^ level_z])
-    keep, send = partial_hessian(*buffers, place, n_col)
+        out = image_piece(k, pieces[k], top, matrix, before, blocks, place, n_col)
+        if k < n_col - 1:
+            before.append(out[:2])
+            blocks.append(out[2])
+    keep, send = out
 
     mine = keep + exchange(send, "slab", 1)
     parts = [mine[:, k * cols : (k + 1) * cols] for k in range(n_col)]

time: 121 us -> 87.3 us (0.72)
  Pallas kernels: 57 us -> 29.9 us
  local copies, waits for them, and re-layouts: 5.72 us -> 1.88 us
  starting transfers between devices: 31.8 us -> 29.3 us
  waiting for transfers between devices: 22.4 us -> 19.9 us
  matrix products: 1.72 us -> 3.61 us
    pallas_call x5 -> x4, Pallas kernels: 43.5 us -> 19.3 us  [image_piece(): pl.pallas_call(functools.partial(image_kernel, layers, width, len(piece),...]
    pallas_call x1, Pallas kernels: 9.38 us -> 2.77 us  [build(): pl.pallas_call(functools.partial(build_kernel, layers, width), grid_spec=...]
    unnamed x22 -> x12, local copies, waits for them, and re-layouts: 5.47 us -> 0.86 us
    pallas_call x4, Pallas kernels: 4.17 us -> 7.89 us  [pack(): pl.pallas_call(functools.partial(pack_kernel, layers, width, n_col - 1),...]
    ppermute x18 -> x16, waiting for transfers between devices: 22.4 us -> 19.9 us  [exchange(): return lax.ppermute(value, axis, [(i, i ^ by) for i in range(count)])]
    ppermute x18 -> x16, starting transfers between devices: 26.5 us -> 24 us  [exchange(): return lax.ppermute(value, axis, [(i, i ^ by) for i in range(count)])]
    dot_general x1, matrix products: 0.91 us -> 2.8 us  [small_sums(): lax.dot_general(residual_force, sensitivity, (((0, 1), (0, 2)), ((), ()))...]
  transfers between devices with their start and end apart: 22 -> 20, of which waited for: 9 -> 7; matrix products, arithmetic and copies ran while one was open for 2% -> 6% of each run, Pallas kernels for 34% -> 25%
where the time goes in v1:
time: 87.3 us; the launch traced here: 86.9 us
  Pallas kernels  29.9 us (34%)
  starting transfers between devices  29.3 us (34%)
  waiting for transfers between devices  19.9 us (23%)
  matrix products  3.61 us (4%)
  local copies, waits for them, and re-layouts  1.88 us (2%)
  other arithmetic  1.43 us (2%)
  between operations  0.91 us (1%)
    ppermute x16, starting transfers between devices, exchange(): return lax.ppermute(value, axis, [(i, i ^ by) for i in range(count)])  24 us
    ppermute x16, waiting for transfers between devices, exchange(): return lax.ppermute(value, axis, [(i, i ^ by) for i in range(count)])  19.9 us
    pallas_call x4, Pallas kernels, image_piece(): pl.pallas_call(functools.partial(image_kernel, layers, width, len(piece),...  19.3 us
    pallas_call x4, Pallas kernels, pack(): pl.pallas_call(functools.partial(pack_kernel, layers, width, n_col - 1),...  7.89 us
    ppermute x4, starting transfers between devices, shifted(): return lax.ppermute(value, axis, pairs)  5.34 us
    dot_general x1, matrix products, small_sums(): lax.dot_general(residual_force, sensitivity, (((0, 1), (0, 2)), ((), ()))...  2.8 us
    pallas_call x1, Pallas kernels, build(): pl.pallas_call(functools.partial(build_kernel, layers, width), grid_spec=...  2.77 us
  transfers between devices with their start and end apart: 20, of which 7 were waited for; matrix products, arithmetic and copies ran while one was open for 6% of the time, Pallas kernels for 25%

profile of v1, /device:TPU:0, one launch (start us, length us, event | category | flops | bytes accessed | tf_op | source)
XLA Modules:
  0.0 86.9 jit_solution(10661607023213112124)
XLA Ops:
  0.6 2.4 %pack.6 = bf16[128,3328]{1,0:T(8,128)(2,1)} custom-call(s32[1]{0:T(128)} %bitcast.8.target, bf16[3,128,4096]{2,1,0:T(8,128)(2,1)} %refs_7_.7, bf16[3,128,4096]{2,1,0:T(8,128)(2,1)} %refs_7_.7, bf16[3,128,4096]{2,1,0:T(8,128)(2,1)} %refs_7_.7, bf16[3,128,4096]{2,1,0:T(8,128)(2,1)} %refs_7_.7, bf16[3,128,4096]{2,1,0:T(8,128)(2,1)} %refs_7_.7, ...), custom_call_target="tpu_custom_call" | custom-call | bytes 2097152 | tf_op jit(solution)/shard_map/pack/pallas_call | solution.py:76
  3.1 2.9 %collective-permute-start.6 = (bf16[128,3328]{1,0:T(8,128)(2,1)}, bf16[128,3328]{1,0:T(8,128)(2,1)S(1)}, u32[]{:S(2)}, u32[]{:S(2)}) collective-permute-start(bf16[128,3328]{1,0:T(8,128)(2,1)} %pack.6), channel_id=1, source_target_pairs={{0,1},{1,0},{2,3},{3,2},{4,5},{5,4},{6,7},{7,6},{8,9},{9,8},{10,11... | collective-permute-start | bytes 2555912 | tf_op jit(solution)/shard_map/ppermute | solution.py:18
  6.0 1.6 %pack.7 = bf16[128,3328]{1,0:T(8,128)(2,1)S(1)} custom-call(s32[1]{0:T(128)} %bitcast.9.target, bf16[3,128,4096]{2,1,0:T(8,128)(2,1)} %refs_7_.7, bf16[3,128,4096]{2,1,0:T(8,128)(2,1)} %refs_7_.7, bf16[3,128,4096]{2,1,0:T(8,128)(2,1)} %refs_7_.7, bf16[3,128,4096]{2,1,0:T(8,128)(2,1)} %refs_7_.7, bf16[3,128,4096]{2,1,0:T(8,128)(2,1)} %refs_7_.7, ...), custom_call_target="tpu_custom_call" | custom-call | bytes 2097152 | tf_op jit(solution)/shard_map/pack/pallas_call | solution.py:76
  7.6 1.6 %collective-permute-start.9 = (bf16[128,3328]{1,0:T(8,128)(2,1)S(1)}, bf16[128,3328]{1,0:T(8,128)(2,1)S(1)}, u32[]{:S(2)}, u32[]{:S(2)}) collective-permute-start(bf16[128,3328]{1,0:T(8,128)(2,1)S(1)} %pack.7), channel_id=1, source_target_pairs={{0,2},{1,3},{2,0},{3,1},{4,6},{5,7},{6,4},{7,5},{8,10},{9,11},{10,... | collective-permute-start | bytes 2555912 | tf_op jit(solution)/shard_map/ppermute | solution.py:18
  9.3 2.8 %convolution_bitcast_fusion = f32[128]{0:T(128)S(1)} fusion(bf16[3,128,4096]{2,1,0:T(8,128)(2,1)} %refs_7_.7, bf16[3,4096,1]{1,0,2:T(4,128)(2,1)S(1)} %bitcast.30), kind=kOutput, calls=%fused_computation.2 | convolution fusion | flops 3145728 | bytes 3170816 | tf_op jit(solution)/shard_map/dot_general | solution.py:325
  12.1 0.2 dynamic_update_slice.3
  12.3 0.8 fusion
  13.1 0.1 collective-permute-start.2
  13.2 1.6 %pack.5.refs_0_ = bf16[128,3328]{1,0:T(8,128)(2,1)S(1)} custom-call(s32[1]{0:T(128)} %bitcast.7.target._, bf16[3,128,4096]{2,1,0:T(8,128)(2,1)} %refs_7_.7, bf16[3,128,4096]{2,1,0:T(8,128)(2,1)} %refs_7_.7, bf16[3,128,4096]{2,1,0:T(8,128)(2,1)} %refs_7_.7, bf16[3,128,4096]{2,1,0:T(8,128)(2,1)} %refs_7_.7, bf16[3,128,4096]{2,1,0:T(8,128)(2,1)} %refs_7_.7, ...), custom_call_target="tpu_custom_call" | custom-call | bytes 2097152 | tf_op jit(solution)/shard_map/pack/pallas_call | solution.py:76
  14.7 0.7 slice.54
  15.5 1.3 %collective-permute-start.4 = (bf16[128,1024]{1,0:T(8,128)(2,1)}, bf16[128,1024]{1,0:T(8,128)(2,1)}, u32[]{:S(2)}, u32[]{:S(2)}) collective-permute-start(bf16[128,1024]{1,0:T(8,128)(2,1)} %slice.54), channel_id=1, source_target_pairs={{4,0},{8,4},{12,8},{16,12},{20,16},{24,20},{28,24},{5,1},{9,5},{13... | collective-permute-start | bytes 786440 | tf_op jit(solution)/shard_map/ppermute | solution.py:24
  16.8 0.0 copy-start
  16.8 2.3 %pack.4 = (bf16[128,1024]{1,0:T(8,128)(2,1)}, bf16[128,2304]{1,0:T(8,128)(2,1)S(1)}) custom-call(s32[1]{0:T(128)} %bitcast.target, bf16[3,128,4096]{2,1,0:T(8,128)(2,1)} %refs_7_.7, bf16[3,128,4096]{2,1,0:T(8,128)(2,1)} %refs_7_.7, bf16[3,128,4096]{2,1,0:T(8,128)(2,1)} %refs_7_.7, bf16[3,128,4096]{2,1,0:T(8,128)(2,1)} %refs_7_.7, ...), custom_call_target="tpu_custom_call" | custom-call | bytes 2097152 | tf_op jit(solution)/shard_map/pack/pallas_call | solution.py:76
  19.1 0.8 copy-done.1
  19.9 0.0 collective-permute-start
  19.9 2.0 %collective-permute-start.3 = (f32[8,128]{1,0:T(8,128)S(1)}, f32[8,128]{1,0:T(8,128)S(1)}, u32[]{:S(2)}, u32[]{:S(2)}) collective-permute-start(f32[8,128]{1,0:T(8,128)S(1)} %fusion.8), channel_id=1, source_target_pairs={{0,2},{1,3},{2,0},{3,1},{4,6},{5,7},{6,4},{7,5},{8,10},{9,11},{10,... | collective-permute-start | bytes 12296 | tf_op jit(solution)/shard_map/ppermute | solution.py:18
  22.0 0.1 pad_add_fusion.refs_15_
  22.1 2.8 %build.1 = (bf16[5,2,3840,256]{3,2,1,0:T(8,128)(2,1)S(1)}, bf16[2,15,256,256]{3,2,1,0:T(8,128)(2,1)S(1)}, bf16[2,256,256]{2,1,0:T(8,128)(2,1)S(1)}) custom-call(s32[1]{0:T(128)} %bitcast.7.target._, f32[6,4,1024]{2,1,0:T(4,128)S(1)} %copy-done), custom_call_target="tpu_custom_call" | custom-call | flops 20971520 | bytes 25165824 | tf_op jit(solution)/shard_map/build/pallas_call | solution.py:208
  24.8 8.9 %collective-permute-done.3 = f32[8,128]{1,0:T(8,128)S(1)} collective-permute-done((f32[8,128]{1,0:T(8,128)S(1)}, f32[8,128]{1,0:T(8,128)S(1)}, u32[]{:S(2)}, u32[]{:S(2)}) %collective-permute-start.3) | collective-permute-done | bytes 4128 | tf_op jit(solution)/shard_map/ppermute | solution.py:18
  33.8 1.5 %collective-permute-start.1 = (bf16[128,2304]{1,0:T(8,128)(2,1)}, bf16[128,2304]{1,0:T(8,128)(2,1)S(1)}, u32[]{:S(2)}, u32[]{:S(2)}) collective-permute-start(bf16[128,2304]{1,0:T(8,128)(2,1)} %copy-done.1), channel_id=1, source_target_pairs={{0,3},{1,2},{2,1},{3,0},{4,7},{5,6},{6,5},{7,4},{8,11},{9,10},{10,... | collective-permute-start | bytes 1769480 | tf_op jit(solution)/shard_map/ppermute | solution.py:18
  35.3 0.0 collective-permute-done.4.refs_1_
  35.3 1.6 %collective-permute-start.5 = (f32[8,128]{1,0:T(8,128)S(1)}, f32[8,128]{1,0:T(8,128)S(1)}, u32[]{:S(2)}, u32[]{:S(2)}) collective-permute-start(f32[8,128]{1,0:T(8,128)S(1)} %add.51), channel_id=1, source_target_pairs={{0,8},{4,12},{8,0},{12,4},{16,24},{20,28},{24,16},{28,20},{1,9},{5... | collective-permute-start | bytes 12296 | tf_op jit(solution)/shard_map/ppermute | solution.py:18
  36.9 1.3 %collective-permute-start.7 = (bf16[128,1024]{1,0:T(8,128)(2,1)S(1)}, bf16[128,1024]{1,0:T(8,128)(2,1)S(1)}, u32[]{:S(2)}, u32[]{:S(2)}) collective-permute-start(bf16[128,1024]{1,0:T(8,128)(2,1)S(1)} %slice.55), channel_id=1, source_target_pairs={{4,0},{8,4},{12,8},{16,12},{20,16},{24,20},{28,24},{5,1},{9,5},{13... | collective-permute-start | bytes 786440 | tf_op jit(solution)/shard_map/ppermute | solution.py:24
  38.2 4.6 %image.4 = (bf16[128,4096]{1,0:T(8,128)(2,1)S(1)}, bf16[128,4096]{1,0:T(8,128)(2,1)S(1)}, f32[1,128,128]{2,1,0:T(8,128)S(1)}) custom-call(bf16[128,3328]{1,0:T(8,128)(2,1)S(1)} %pack.5.refs_0_, bf16[128,1024]{1,0:T(8,128)(2,1)} %collective-permute-done.4.refs_1_, bf16[5,2,3840,256]{3,2,1,0:T(8,128)(2,1)S(1)} %get-tuple-element.33.refs_2_.refs_3_, ...), custom_call_target="tpu_custom_call" | custom-call | flops 3019898880 | bytes 25165824 | tf_op jit(solution)/shard_map/image/pallas_call | solution.py:310
  42.8 1.3 %collective-permute-start.12 = (bf16[128,1024]{1,0:T(8,128)(2,1)}, bf16[128,1024]{1,0:T(8,128)(2,1)S(1)}, u32[]{:S(2)}, u32[]{:S(2)}) collective-permute-start(bf16[128,1024]{1,0:T(8,128)(2,1)} %collective-permute-done.refs_0_), channel_id=1, source_target_pairs={{4,0},{8,4},{12,8},{16,12},{20,16},{24,20},{28,24},{5,1},{9,5},{13... | collective-permute-start | bytes 786440 | tf_op jit(solution)/shard_map/ppermute | solution.py:24
  44.1 0.0 collective-permute-done.5
  44.2 1.5 %collective-permute-start.10 = (bf16[128,1024]{1,0:T(8,128)(2,1)S(1)}, bf16[128,1024]{1,0:T(8,128)(2,1)S(1)}, u32[]{:S(2)}, u32[]{:S(2)}) collective-permute-start(bf16[128,1024]{1,0:T(8,128)(2,1)S(1)} %slice.56), channel_id=1, source_target_pairs={{4,0},{8,4},{12,8},{16,12},{20,16},{24,20},{28,24},{5,1},{9,5},{13... | collective-permute-start | bytes 786440 | tf_op jit(solution)/shard_map/ppermute | solution.py:24
  45.7 0.0 collective-permute-done.7.refs_1_
  45.7 4.5 %collective-permute-start.8 = (f32[8,128]{1,0:T(8,128)S(1)}, f32[8,128]{1,0:T(8,128)S(1)}, u32[]{:S(2)}, u32[]{:S(2)}) collective-permute-start(f32[8,128]{1,0:T(8,128)S(1)} %add.52), channel_id=1, source_target_pairs={{0,16},{4,20},{8,24},{12,28},{16,0},{20,4},{24,8},{28,12},{1,17},{... | collective-permute-start | bytes 12296 | tf_op jit(solution)/shard_map/ppermute | solution.py:18
  50.2 4.0 %image.5 = (bf16[128,4096]{1,0:T(8,128)(2,1)S(1)}, bf16[128,4096]{1,0:T(8,128)(2,1)S(1)}, f32[2,128,128]{2,1,0:T(8,128)S(1)}) custom-call(bf16[128,3328]{1,0:T(8,128)(2,1)S(1)} %collective-permute-done.6.refs_0_, bf16[128,1024]{1,0:T(8,128)(2,1)S(1)} %collective-permute-done.7.refs_1_, bf16[5,2,3840,256]{3,2,1,0:T(8,128)(2,1)S(1)} %get-tuple-element.33.refs_2_.refs_3_, ...), custom_call_target="tpu_custom_call" | custom-call | flops 3288334336 | bytes 25165824 | tf_op jit(solution)/shard_map/image/pallas_call | solution.py:310
  54.3 1.2 %collective-permute-done.8 = f32[8,128]{1,0:T(8,128)S(1)} collective-permute-done((f32[8,128]{1,0:T(8,128)S(1)}, f32[8,128]{1,0:T(8,128)S(1)}, u32[]{:S(2)}, u32[]{:S(2)}) %collective-permute-start.8) | collective-permute-done | bytes 4128 | tf_op jit(solution)/shard_map/ppermute | solution.py:18
  55.5 1.5 %collective-permute-start.11 = (f32[8,128]{1,0:T(8,128)S(1)}, f32[8,128]{1,0:T(8,128)S(1)}, u32[]{:S(2)}, u32[]{:S(2)}) collective-permute-start(f32[8,128]{1,0:T(8,128)S(1)} %add.53), channel_id=1, source_target_pairs={{0,1},{1,0},{2,3},{3,2},{4,5},{5,4},{6,7},{7,6},{8,9},{9,8},{10,11... | collective-permute-start | bytes 12296 | tf_op jit(solution)/shard_map/ppermute | solution.py:18
  57.0 4.6 %image.6 = (bf16[128,4096]{1,0:T(8,128)(2,1)S(1)}, bf16[128,4096]{1,0:T(8,128)(2,1)S(1)}, f32[3,128,128]{2,1,0:T(8,128)S(1)}) custom-call(bf16[128,3328]{1,0:T(8,128)(2,1)S(1)} %collective-permute-done.9.refs_0_, bf16[128,1024]{1,0:T(8,128)(2,1)S(1)} %collective-permute-done.10.refs_1_, bf16[5,2,3840,256]{3,2,1,0:T(8,128)(2,1)S(1)} %get-tuple-element.33.refs_2_.refs_3_, ...), custom_call_target="tpu_custom_call" | custom-call | flops 3556769792 | bytes 25165824 | tf_op jit(solution)/shard_map/image/pallas_call | solution.py:310
  61.6 6.0 %image.7 = (f32[256,512]{1,0:T(8,128)S(1)}, f32[256,512]{1,0:T(8,128)S(1)}) custom-call(bf16[128,1024]{1,0:T(8,128)(2,1)} %collective-permute-done.refs_0_, bf16[128,2304]{1,0:T(8,128)(2,1)S(1)} %collective-permute-done.1.refs_1_, bf16[128,1024]{1,0:T(8,128)(2,1)S(1)} %collective-permute-done.12.refs_2_, ...), custom_call_target="tpu_custom_call" | custom-call | flops 3825205248 | bytes 25165824 | tf_op jit(solution)/shard_map/image/pallas_call | solution.py:310
  67.6 0.1 collective-permute-start.13
  67.7 1.9 %collective-permute-done.13 = f32[256,512]{1,0:T(8,128)S(1)} collective-permute-done((f32[256,512]{1,0:T(8,128)S(1)}, f32[256,512]{1,0:T(8,128)S(1)}, u32[]{:S(2)}, u32[]{:S(2)}) %collective-permute-start.13) | collective-permute-done | bytes 524320 | tf_op jit(solution)/shard_map/ppermute | solution.py:18
  69.6 0.1 add.56
  69.7 0.6 collective-permute-start.14
  70.3 0.5 collective-permute-start.15
  70.8 2.4 %collective-permute-start.16 = (f32[256,128]{1,0:T(8,128)S(1)}, f32[256,128]{1,0:T(8,128)S(1)}, u32[]{:S(2)}, u32[]{:S(2)}) collective-permute-start(f32[256,128]{1,0:T(8,128)S(1)} %get-tuple-element.52), channel_id=1, source_target_pairs={{0,3},{1,2},{2,1},{3,0},{4,7},{5,6},{6,5},{7,4},{8,11},{9,10},{10,... | collective-permute-start | bytes 393224 | tf_op jit(solution)/shard_map/ppermute | solution.py:18
  73.3 2.9 %collective-permute-done.14 = f32[256,128]{1,0:T(8,128)S(1)} collective-permute-done((f32[256,128]{1,0:T(8,128)S(1)}, f32[256,128]{1,0:T(8,128)S(1)}, u32[]{:S(2)}, u32[]{:S(2)}) %collective-permute-start.14) | collective-permute-done | bytes 131104 | tf_op jit(solution)/shard_map/ppermute | solution.py:18
  76.1 2.3 %collective-permute-done.15 = f32[256,128]{1,0:T(8,128)S(1)} collective-permute-done((f32[256,128]{1,0:T(8,128)S(1)}, f32[256,128]{1,0:T(8,128)S(1)}, u32[]{:S(2)}, u32[]{:S(2)}) %collective-permute-start.15) | collective-permute-done | bytes 131104 | tf_op jit(solution)/shard_map/ppermute | solution.py:18
  78.4 2.1 %collective-permute-start.17 = (f32[64,128]{1,0:T(8,128)S(1)}, f32[64,128]{1,0:T(8,128)S(1)}, u32[]{:S(2)}, u32[]{:S(2)}) collective-permute-start(f32[64,128]{1,0:T(8,128)S(1)} %get-tuple-element.54), channel_id=1, source_target_pairs={{0,8},{4,12},{8,0},{12,4},{16,24},{20,28},{24,16},{28,20},{1,9},{5... | collective-permute-start | bytes 98312 | tf_op jit(solution)/shard_map/ppermute | solution.py:18
  80.6 2.4 %collective-permute-start.19 = (f32[64,128]{1,0:T(8,128)S(1)}, f32[64,128]{1,0:T(8,128)S(1)}, u32[]{:S(2)}, u32[]{:S(2)}) collective-permute-start(f32[64,128]{1,0:T(8,128)S(1)} %get-tuple-element.55), channel_id=1, source_target_pairs={{0,24},{4,28},{8,16},{12,20},{16,8},{20,12},{24,0},{28,4},{1,25},{... | collective-permute-start | bytes 98312 | tf_op jit(solution)/shard_map/ppermute | solution.py:18
  83.0 0.6 multiply_bitcast_fusion
  83.6 1.8 %collective-permute-done.18 = f32[64,128]{1,0:T(8,128)S(1)} collective-permute-done((f32[64,128]{1,0:T(8,128)S(1)}, f32[64,128]{1,0:T(8,128)S(1)}, u32[]{:S(2)}, u32[]{:S(2)}) %collective-permute-start.18) | collective-permute-done | bytes 32800 | tf_op jit(solution)/shard_map/ppermute | solution.py:18
  85.4 0.9 %collective-permute-done.19 = f32[64,128]{1,0:T(8,128)S(1)} collective-permute-done((f32[64,128]{1,0:T(8,128)S(1)}, f32[64,128]{1,0:T(8,128)S(1)}, u32[]{:S(2)}, u32[]{:S(2)}) %collective-permute-start.19) | collective-permute-done | bytes 32800 | tf_op jit(solution)/shard_map/ppermute | solution.py:18
  86.3 0.6 fusion.7
  (35 shorter events, 0.2 us)
Async XLA Ops:
  3.1 33.8 %collective-permute-start.6 = (bf16[128,3328]{1,0:T(8,128)(2,1)}, bf16[128,3328]{1,0:T(8,128)(2,1)S(1)}, u32[]{:S(2)}, u32[]{:S(2)}) collective-permute-start(bf16[128,3328]{1,0:T(8,128)(2,1)} %pack.6), channel_id=1, source_target_pairs={{0,1},{1,0},{2,3},{3,2},{4,5},{5,4},{6,7},{7,6},{8,9},{9,8},{10,11... | collective-permute-start | bytes 2555912 | tf_op jit(solution)/shard_map/ppermute | solution.py:18
  6.0 3.2 %copy-start.3 = (f32[4,1024]{1,0:T(4,128)S(1)}, f32[4,1024]{1,0:T(4,128)}, u32[]{:S(2)}) copy-start(f32[4,1024]{1,0:T(4,128)} %param.9) | copy-start | bytes 49156
  6.0 3.2 %copy-start.4 = (s32[4,1024]{1,0:T(4,128)S(1)}, s32[4,1024]{1,0:T(4,128)}, u32[]{:S(2)}) copy-start(s32[4,1024]{1,0:T(4,128)} %param.8) | copy-start | bytes 49156
  6.0 3.2 %copy-start.2 = (bf16[3,4096]{1,0:T(4,128)(2,1)S(1)}, bf16[3,4096]{1,0:T(4,128)(2,1)}, u32[]{:S(2)}) copy-start(bf16[3,4096]{1,0:T(4,128)(2,1)} %param.6) | copy-start | bytes 73732
  7.6 36.6 %collective-permute-start.9 = (bf16[128,3328]{1,0:T(8,128)(2,1)S(1)}, bf16[128,3328]{1,0:T(8,128)(2,1)S(1)}, u32[]{:S(2)}, u32[]{:S(2)}) collective-permute-start(bf16[128,3328]{1,0:T(8,128)(2,1)S(1)} %pack.7), channel_id=1, source_target_pairs={{0,2},{1,3},{2,0},{3,1},{4,6},{5,7},{6,4},{7,5},{8,10},{9,11},{10,... | collective-permute-start | bytes 2555912 | tf_op jit(solution)/shard_map/ppermute | solution.py:18
  13.1 6.8 %collective-permute-start.2 = (f32[8,128]{1,0:T(8,128)S(1)}, f32[8,128]{1,0:T(8,128)S(1)}, u32[]{:S(2)}, u32[]{:S(2)}) collective-permute-start(f32[8,128]{1,0:T(8,128)S(1)} %pad_maximum_fusion), channel_id=1, source_target_pairs={{0,4},{4,0},{8,12},{12,8},{16,20},{20,16},{24,28},{28,24},{1,5},{5... | collective-permute-start | bytes 12296 | tf_op jit(solution)/shard_map/ppermute | solution.py:18
  15.5 19.8 %collective-permute-start.4 = (bf16[128,1024]{1,0:T(8,128)(2,1)}, bf16[128,1024]{1,0:T(8,128)(2,1)}, u32[]{:S(2)}, u32[]{:S(2)}) collective-permute-start(bf16[128,1024]{1,0:T(8,128)(2,1)} %slice.54), channel_id=1, source_target_pairs={{4,0},{8,4},{12,8},{16,12},{20,16},{24,20},{28,24},{5,1},{9,5},{13... | collective-permute-start | bytes 786440 | tf_op jit(solution)/shard_map/ppermute | solution.py:24
  16.8 5.3 %copy-start = (f32[6,4,1024]{2,1,0:T(4,128)S(1)}, f32[6,4,1024]{2,1,0:T(4,128)}, u32[]{:S(2)}) copy-start(f32[6,4,1024]{2,1,0:T(4,128)} %moments_ref.1) | copy-start | bytes 294916
  19.1 0.8 copy-start.1
  19.9 22.9 %collective-permute-start = (bf16[128,1024]{1,0:T(8,128)(2,1)}, bf16[128,1024]{1,0:T(8,128)(2,1)}, u32[]{:S(2)}, u32[]{:S(2)}) collective-permute-start(bf16[128,1024]{1,0:T(8,128)(2,1)} %get-tuple-element.27), channel_id=1, source_target_pairs={{0,3},{1,2},{2,1},{3,0},{4,7},{5,6},{6,5},{7,4},{8,11},{9,10},{10,... | collective-permute-start | bytes 786440 | tf_op jit(solution)/shard_map/ppermute | solution.py:18
  19.9 13.8 %collective-permute-start.3 = (f32[8,128]{1,0:T(8,128)S(1)}, f32[8,128]{1,0:T(8,128)S(1)}, u32[]{:S(2)}, u32[]{:S(2)}) collective-permute-start(f32[8,128]{1,0:T(8,128)S(1)} %fusion.8), channel_id=1, source_target_pairs={{0,2},{1,3},{2,0},{3,1},{4,6},{5,7},{6,4},{7,5},{8,10},{9,11},{10,... | collective-permute-start | bytes 12296 | tf_op jit(solution)/shard_map/ppermute | solution.py:18
  33.8 27.8 %collective-permute-start.1 = (bf16[128,2304]{1,0:T(8,128)(2,1)}, bf16[128,2304]{1,0:T(8,128)(2,1)S(1)}, u32[]{:S(2)}, u32[]{:S(2)}) collective-permute-start(bf16[128,2304]{1,0:T(8,128)(2,1)} %copy-done.1), channel_id=1, source_target_pairs={{0,3},{1,2},{2,1},{3,0},{4,7},{5,6},{6,5},{7,4},{8,11},{9,10},{10,... | collective-permute-start | bytes 1769480 | tf_op jit(solution)/shard_map/ppermute | solution.py:18
  35.3 8.9 %collective-permute-start.5 = (f32[8,128]{1,0:T(8,128)S(1)}, f32[8,128]{1,0:T(8,128)S(1)}, u32[]{:S(2)}, u32[]{:S(2)}) collective-permute-start(f32[8,128]{1,0:T(8,128)S(1)} %add.51), channel_id=1, source_target_pairs={{0,8},{4,12},{8,0},{12,4},{16,24},{20,28},{24,16},{28,20},{1,9},{5... | collective-permute-start | bytes 12296 | tf_op jit(solution)/shard_map/ppermute | solution.py:18
  36.9 8.8 %collective-permute-start.7 = (bf16[128,1024]{1,0:T(8,128)(2,1)S(1)}, bf16[128,1024]{1,0:T(8,128)(2,1)S(1)}, u32[]{:S(2)}, u32[]{:S(2)}) collective-permute-start(bf16[128,1024]{1,0:T(8,128)(2,1)S(1)} %slice.55), channel_id=1, source_target_pairs={{4,0},{8,4},{12,8},{16,12},{20,16},{24,20},{28,24},{5,1},{9,5},{13... | collective-permute-start | bytes 786440 | tf_op jit(solution)/shard_map/ppermute | solution.py:24
  42.8 18.7 %collective-permute-start.12 = (bf16[128,1024]{1,0:T(8,128)(2,1)}, bf16[128,1024]{1,0:T(8,128)(2,1)S(1)}, u32[]{:S(2)}, u32[]{:S(2)}) collective-permute-start(bf16[128,1024]{1,0:T(8,128)(2,1)} %collective-permute-done.refs_0_), channel_id=1, source_target_pairs={{4,0},{8,4},{12,8},{16,12},{20,16},{24,20},{28,24},{5,1},{9,5},{13... | collective-permute-start | bytes 786440 | tf_op jit(solution)/shard_map/ppermute | solution.py:24
  44.2 11.3 %collective-permute-start.10 = (bf16[128,1024]{1,0:T(8,128)(2,1)S(1)}, bf16[128,1024]{1,0:T(8,128)(2,1)S(1)}, u32[]{:S(2)}, u32[]{:S(2)}) collective-permute-start(bf16[128,1024]{1,0:T(8,128)(2,1)S(1)} %slice.56), channel_id=1, source_target_pairs={{4,0},{8,4},{12,8},{16,12},{20,16},{24,20},{28,24},{5,1},{9,5},{13... | collective-permute-start | bytes 786440 | tf_op jit(solution)/shard_map/ppermute | solution.py:24
  45.7 9.8 %collective-permute-start.8 = (f32[8,128]{1,0:T(8,128)S(1)}, f32[8,128]{1,0:T(8,128)S(1)}, u32[]{:S(2)}, u32[]{:S(2)}) collective-permute-start(f32[8,128]{1,0:T(8,128)S(1)} %add.52), channel_id=1, source_target_pairs={{0,16},{4,20},{8,24},{12,28},{16,0},{20,4},{24,8},{28,12},{1,17},{... | collective-permute-start | bytes 12296 | tf_op jit(solution)/shard_map/ppermute | solution.py:18
  55.5 6.1 %collective-permute-start.11 = (f32[8,128]{1,0:T(8,128)S(1)}, f32[8,128]{1,0:T(8,128)S(1)}, u32[]{:S(2)}, u32[]{:S(2)}) collective-permute-start(f32[8,128]{1,0:T(8,128)S(1)} %add.53), channel_id=1, source_target_pairs={{0,1},{1,0},{2,3},{3,2},{4,5},{5,4},{6,7},{7,6},{8,9},{9,8},{10,11... | collective-permute-start | bytes 12296 | tf_op jit(solution)/shard_map/ppermute | solution.py:18
  67.6 2.0 %collective-permute-start.13 = (f32[256,512]{1,0:T(8,128)S(1)}, f32[256,512]{1,0:T(8,128)S(1)}, u32[]{:S(2)}, u32[]{:S(2)}) collective-permute-start(f32[256,512]{1,0:T(8,128)S(1)} %get-tuple-element.49), channel_id=1, source_target_pairs={{0,4},{4,0},{8,12},{12,8},{16,20},{20,16},{24,28},{28,24},{1,5},{5... | collective-permute-start | bytes 1572872 | tf_op jit(solution)/shard_map/ppermute | solution.py:18
  69.7 6.4 %collective-permute-start.14 = (f32[256,128]{1,0:T(8,128)S(1)}, f32[256,128]{1,0:T(8,128)S(1)}, u32[]{:S(2)}, u32[]{:S(2)}) collective-permute-start(f32[256,128]{1,0:T(8,128)S(1)} %get-tuple-element.51), channel_id=1, source_target_pairs={{0,1},{1,0},{2,3},{3,2},{4,5},{5,4},{6,7},{7,6},{8,9},{9,8},{10,11... | collective-permute-start | bytes 393224 | tf_op jit(solution)/shard_map/ppermute | solution.py:18
  70.3 8.1 %collective-permute-start.15 = (f32[256,128]{1,0:T(8,128)S(1)}, f32[256,128]{1,0:T(8,128)S(1)}, u32[]{:S(2)}, u32[]{:S(2)}) collective-permute-start(f32[256,128]{1,0:T(8,128)S(1)} %get-tuple-element.53), channel_id=1, source_target_pairs={{0,2},{1,3},{2,0},{3,1},{4,6},{5,7},{6,4},{7,5},{8,10},{9,11},{10,... | collective-permute-start | bytes 393224 | tf_op jit(solution)/shard_map/ppermute | solution.py:18
  70.8 7.6 %collective-permute-start.16 = (f32[256,128]{1,0:T(8,128)S(1)}, f32[256,128]{1,0:T(8,128)S(1)}, u32[]{:S(2)}, u32[]{:S(2)}) collective-permute-start(f32[256,128]{1,0:T(8,128)S(1)} %get-tuple-element.52), channel_id=1, source_target_pairs={{0,3},{1,2},{2,1},{3,0},{4,7},{5,6},{6,5},{7,4},{8,11},{9,10},{10,... | collective-permute-start | bytes 393224 | tf_op jit(solution)/shard_map/ppermute | solution.py:18
  78.4 5.2 %collective-permute-start.17 = (f32[64,128]{1,0:T(8,128)S(1)}, f32[64,128]{1,0:T(8,128)S(1)}, u32[]{:S(2)}, u32[]{:S(2)}) collective-permute-start(f32[64,128]{1,0:T(8,128)S(1)} %get-tuple-element.54), channel_id=1, source_target_pairs={{0,8},{4,12},{8,0},{12,4},{16,24},{20,28},{24,16},{28,20},{1,9},{5... | collective-permute-start | bytes 98312 | tf_op jit(solution)/shard_map/ppermute | solution.py:18
  80.6 4.8 %collective-permute-start.18 = (f32[64,128]{1,0:T(8,128)S(1)}, f32[64,128]{1,0:T(8,128)S(1)}, u32[]{:S(2)}, u32[]{:S(2)}) collective-permute-start(f32[64,128]{1,0:T(8,128)S(1)} %get-tuple-element.56), channel_id=1, source_target_pairs={{0,16},{4,20},{8,24},{12,28},{16,0},{20,4},{24,8},{28,12},{1,17},{... | collective-permute-start | bytes 98312 | tf_op jit(solution)/shard_map/ppermute | solution.py:18
  80.6 5.7 %collective-permute-start.19 = (f32[64,128]{1,0:T(8,128)S(1)}, f32[64,128]{1,0:T(8,128)S(1)}, u32[]{:S(2)}, u32[]{:S(2)}) collective-permute-start(f32[64,128]{1,0:T(8,128)S(1)} %get-tuple-element.55), channel_id=1, source_target_pairs={{0,24},{4,28},{8,16},{12,20},{16,8},{20,12},{24,0},{28,4},{1,25},{... | collective-permute-start | bytes 98312 | tf_op jit(solution)/shard_map/ppermute | solution.py:18

commit v2 on v1

--- a/solution.py
+++ b/solution.py
@@ -28,9 +28,10 @@
     return lax.broadcasted_iota(jnp.int32, shape, 1)
 
 
-def pack_kernel(layers, width, last, target, *refs):
+def pack_kernel(layers, width, last, turn, target, *refs):
     planes, edges = refs[:layers], refs[layers : 2 * layers]
-    first_ref, rest_ref = refs[2 * layers], refs[-1]
+    first_ref, rest_ref, next_ref = refs[2 * layers], refs[-2], refs[-1]
+    next_ref[0] = target[0] ^ turn
     offset = 0 if rest_ref is not first_ref else 3 * width + EDGE
     inside = target[0] != last
     rows = first_ref.shape[0]
@@ -56,7 +57,7 @@
     return (k * (layers + 1) + level) * GY
 
 
-def pack(sensitivity, target, layers, plane, n_col, split):
+def pack(sensitivity, target, turn, layers, plane, n_col, split):
     cols = sensitivity.shape[1]
     width = plane // n_col
     top_block = layers * plane // TILE - 1
@@ -74,18 +75,35 @@
     sizes = [3 * width + EDGE, 3 * (layers - 1) * width]
     outs = [jax.ShapeDtypeStruct((cols, size), sensitivity.dtype) for size in (sizes if split else [sum(sizes)])]
     return pl.pallas_call(
-        functools.partial(pack_kernel, layers, width, n_col - 1),
+        functools.partial(pack_kernel, layers, width, n_col - 1, turn),
         grid_spec=pltpu.PrefetchScalarGridSpec(
             num_scalar_prefetch=1,
             grid=(1,),
             in_specs=[plane_spec(l) for l in range(layers)] + [edge_spec(l) for l in range(layers)],
-            out_specs=[pl.BlockSpec(out.shape, lambda i, t: (0, 0)) for out in outs],
+            out_specs=[pl.BlockSpec(out.shape, lambda i, t: (0, 0)) for out in outs]
+            + [pl.BlockSpec(memory_space=pltpu.SMEM)],
         ),
-        out_shape=outs,
+        out_shape=[*outs, jax.ShapeDtypeStruct((1,), jnp.int32)],
         compiler_params=pltpu.CompilerParams(vmem_limit_bytes=12 << 20),
         cost_estimate=pl.CostEstimate(flops=0, bytes_accessed=2 << 20, transcendentals=0),
         name="pack",
     )(target, *([sensitivity] * (2 * layers)))
+
+
+def crop_kernel(piece_ref, _, out_ref):
+    out_ref[...] = piece_ref[:, : out_ref.shape[1]]
+
+
+def crop(piece, size, after):
+    return pl.pallas_call(
+        crop_kernel,
+        in_specs=[pl.BlockSpec(memory_space=pltpu.VMEM), pl.BlockSpec(memory_space=pl.ANY)],
+        out_specs=pl.BlockSpec(memory_space=pltpu.VMEM),
+        out_shape=jax.ShapeDtypeStruct((piece.shape[0], size), piece.dtype),
+        compiler_params=pltpu.CompilerParams(vmem_limit_bytes=4 << 20),
+        cost_estimate=pl.CostEstimate(flops=0, bytes_accessed=1 << 19, transcendentals=0),
+        name="crop",
+    )(piece, after)
 
 
 def component(a, b):
@@ -235,7 +253,7 @@
     last = index == blocks - 1
     if last:
         block_refs = [refs.pop(0) for _ in range(index)]
-        place = refs.pop(0)
+        small_ref, place = refs.pop(0), refs.pop(0)
         keep_ref, send_ref, values_ref, image_ref = refs
     else:
         values_ref, image_ref, block_ref = refs
@@ -287,9 +305,12 @@
             block = block.T if i > j else block
             for ref, low in ((keep_ref, 0), (send_ref, 1)):
                 ref[at, j * rows : (j + 1) * rows] = jnp.where(place[0] == low, block[:half], block[half:])
-
-
-def image_piece(index, piece, top, matrix, before, blocks, place, n_col):
+    for j in range(blocks):
+        for ref in (keep_ref, send_ref):
+            ref[blocks * half :, j * rows : (j + 1) * rows] = small_ref[...]
+
+
+def image_piece(index, piece, top, matrix, before, blocks, small, place, n_col):
     cols = top.shape[0]
     width = (top.shape[1] - EDGE) // 3
     layers = (sum(x.shape[1] for x in piece) - EDGE) // (3 * width)
@@ -300,9 +321,9 @@
     vmem = pl.BlockSpec(memory_space=pltpu.VMEM)
     in_specs = [vmem] * len(args)
     if index == n_col - 1:
-        args += [*blocks, place]
-        in_specs += [vmem] * len(blocks) + [pl.BlockSpec(memory_space=pltpu.SMEM)]
-        outs = [pltpu.VMEM((cols * n_col // 2, cols * n_col), jnp.float32)] * 2
+        args += [*blocks, small, place]
+        in_specs += [vmem] * (len(blocks) + 1) + [pl.BlockSpec(memory_space=pltpu.SMEM)]
+        outs = [pltpu.VMEM((cols * n_col // 2 + small.shape[0], cols * n_col), jnp.float32)] * 2
         scratch = [shape] * 2
     else:
         outs = [shape, shape, pltpu.VMEM((index + 1, cols, cols), jnp.float32)]
@@ -336,7 +357,7 @@
     misfit_part = lax.dynamic_slice_in_dim(misfit.reshape(elements), offset, share, 0)
     onehot = (zone_part[:, None] == jnp.arange(width, dtype=jnp.int32)[None, :]).astype(jnp.float32)
     zone_part_sum = jnp.dot(misfit_part, onehot, precision=lax.Precision.HIGHEST)
-    return jnp.concatenate([grad_full, zone_part_sum]).reshape(8, -1)
+    return jnp.concatenate([grad_full, zone_part_sum]).reshape(-1, cols)
 
 
 def on_device(sensitivity, residual_force, moments, zone_label, misfit):
@@ -354,22 +375,20 @@
     source = pltpu.with_memory_space_constraint(sensitivity, pltpu.HBM)
     bottom = 3 * (plane // n_col) + EDGE
     pieces = [None] * n_col
-    for k in (*range(1, n_col), 0):
-        packed = pack(source, jnp.reshape(me ^ k, (1,)), layers, plane, n_col, k == n_col - 1)
-        pieces[k] = [exchange(x, "col", k) if k else x for x in packed]
-    both = small_sums(sensitivity, residual_force, zone_label, misfit, me, n_col, width)
-    stages = []
-    for axis, count in (("slab", n_slab), ("col", n_col)):
-        stages += [(axis, 1 << b) for b in range(count.bit_length() - 1)]
-    matrix = build(moments, jnp.reshape(me, (1,)), plane // n_col)
+    order = [*range(1, n_col), 0, 0]
+    target = jnp.reshape(me ^ order[0], (1,))
+    for k, follow in zip(order[:-1], order[1:]):
+        *packed, target = pack(source, target, k ^ follow, layers, plane, n_col, k == n_col - 1)
+        pieces[k] = [exchange(x, "col", k) for x in packed] if k else packed
+    target, residual_force, misfit = lax.optimization_barrier((target, residual_force, misfit))
+    small = small_sums(sensitivity, residual_force, zone_label, misfit, me, n_col, width)
+    matrix = build(moments, target, plane // n_col)
     place = jnp.stack([core, me ^ level_z])
     before, blocks = [], []
     for k in range(n_col):
-        top = shifted(pieces[k][0][:, :bottom], "slab", -1)
-        for axis, by in stages[k :: n_col]:
-            both = both + exchange(both, axis, by)
-        both, top = lax.optimization_barrier((both, top))
-        out = image_piece(k, pieces[k], top, matrix, before, blocks, place, n_col)
+        low = crop(pieces[k][0], bottom, blocks[0]) if k else pieces[k][0][:, :bottom]
+        top = shifted(low, "slab", -1)
+        out = image_piece(k, pieces[k], top, matrix, before, blocks, small, place, n_col)
         if k < n_col - 1:
             before.append(out[:2])
             blocks.append(out[2])
@@ -380,14 +399,13 @@
     mine = parts[0]
     for k in range(1, n_col):
         mine = mine + exchange(parts[k], "col", k)
-    half = cols // 2
-    parts = [mine[k * half : (k + 1) * half] for k in range(n_col)]
+    half, rows = cols // 2, width // 2
+    parts = [jnp.concatenate([mine[k * half : (k + 1) * half], mine[rows:]]) for k in range(n_col)]
     mine = parts[0]
     for k in range(1, n_col):
         mine = mine + exchange(parts[k], "slab", 2 * k)
-    hessian = mine.T
-
-    both = both.reshape(2, width)
+    hessian = mine[:half].T
+    both = mine[half:].reshape(2, width)
     gradient = both[0]
     zone_misfit = both[1] * (width / (layers * plane * n_slab))
     return (hessian, gradient, zone_misfit)

time: 87.3 us -> 111 us (1.27)
  local copies, waits for them, and re-layouts: 1.88 us -> 15.2 us
  waiting for transfers between devices: 19.9 us -> 32.6 us
  starting transfers between devices: 29.3 us -> 22.2 us
  Pallas kernels: 29.9 us -> 36.7 us
  matrix products: 3.61 us -> 1.72 us
    unnamed x12 -> x28, local copies, waits for them, and re-layouts: 0.86 us -> 14.3 us
    ppermute x16 -> x11, waiting for transfers between devices: 19.9 us -> 32.6 us  [exchange(): return lax.ppermute(value, axis, [(i, i ^ by) for i in range(count)])]
    ppermute x16 -> x11, starting transfers between devices: 24 us -> 16.8 us  [exchange(): return lax.ppermute(value, axis, [(i, i ^ by) for i in range(count)])]
    pallas_call x4 -> x7, Pallas kernels: 7.89 us -> 13.4 us  [the longest x4 11.5 us: pack(): pl.pallas_call(functools.partial(pack_kernel, layers, width, n_col - 1, t...]
    dot_general x1, matrix products: 2.8 us -> 0.92 us  [small_sums(): lax.dot_general(residual_force, sensitivity, (((0, 1), (0, 2)), ((), ()))...]
  transfers between devices with their start and end apart: 20 -> 15, of which waited for: 7 -> 7; matrix products, arithmetic and copies ran while one was open for 6% -> 2% of each run, Pallas kernels for 25% -> 26%
where the time goes in v2:
time: 111 us; the launch traced here: 110 us
  Pallas kernels  36.7 us (33%)
  waiting for transfers between devices  32.6 us (29%)
  starting transfers between devices  22.2 us (20%)
  local copies, waits for them, and re-layouts  15.2 us (14%)
  matrix products  1.72 us (2%)
    ppermute x11, waiting for transfers between devices, exchange(): return lax.ppermute(value, axis, [(i, i ^ by) for i in range(count)])  32.6 us
    pallas_call x4, Pallas kernels, image_piece(): pl.pallas_call(functools.partial(image_kernel, layers, width, len(piece),...  19.9 us
    ppermute x11, starting transfers between devices, exchange(): return lax.ppermute(value, axis, [(i, i ^ by) for i in range(count)])  16.8 us
    unnamed x28, local copies, waits for them, and re-layouts  14.3 us
    pallas_call x4, Pallas kernels, pack(): pl.pallas_call(functools.partial(pack_kernel, layers, width, n_col - 1, t...  11.5 us
    ppermute x4, starting transfers between devices, shifted(): return lax.ppermute(value, axis, pairs)  5.32 us
    pallas_call x1, Pallas kernels, build(): pl.pallas_call(functools.partial(build_kernel, layers, width), grid_spec=...  3.42 us
  transfers between devices with their start and end apart: 15, of which 7 were waited for; matrix products, arithmetic and copies ran while one was open for 2% of the time, Pallas kernels for 26%

profile of v2, /device:TPU:0, one launch (start us, length us, event | category | flops | bytes accessed | tf_op | source)
XLA Modules:
  0.0 110.2 jit_solution(3950822587642003603)
XLA Ops:
  0.6 2.5 %pack.4 = (bf16[128,3328]{1,0:T(8,128)(2,1)}, s32[1]{0:T(128)}) custom-call(s32[1]{0:T(128)} %bitcast.target, bf16[3,128,4096]{2,1,0:T(8,128)(2,1)} %refs_7_.7, bf16[3,128,4096]{2,1,0:T(8,128)(2,1)} %refs_7_.7, bf16[3,128,4096]{2,1,0:T(8,128)(2,1)} %refs_7_.7, bf16[3,128,4096]{2,1,0:T(8,128)(2,1)} %refs_7_.7, bf16[3,128,4096]{2,1,0:T(8,128)(2,1)} %refs_7_.7, ...), custom_call_target="tpu_custom_call" | custom-call | bytes 2097152 | tf_op jit(solution)/shard_map/pack/pallas_call | solution.py:77
  3.1 3.0 %collective-permute-start.4 = (bf16[128,3328]{1,0:T(8,128)(2,1)}, bf16[128,3328]{1,0:T(8,128)(2,1)S(1)}, u32[]{:S(2)}, u32[]{:S(2)}) collective-permute-start(bf16[128,3328]{1,0:T(8,128)(2,1)} %get-tuple-element.43), channel_id=1, source_target_pairs={{0,1},{1,0},{2,3},{3,2},{4,5},{5,4},{6,7},{7,6},{8,9},{9,8},{10,11... | collective-permute-start | bytes 2555912 | tf_op jit(solution)/shard_map/ppermute | solution.py:18
  6.1 3.1 %pack.5 = (bf16[128,3328]{1,0:T(8,128)(2,1)}, s32[1]{0:T(128)}) custom-call(s32[1]{0:T(128)} %get-tuple-element.29.target, bf16[3,128,4096]{2,1,0:T(8,128)(2,1)} %refs_7_.7, bf16[3,128,4096]{2,1,0:T(8,128)(2,1)} %refs_7_.7, bf16[3,128,4096]{2,1,0:T(8,128)(2,1)} %refs_7_.7, bf16[3,128,4096]{2,1,0:T(8,128)(2,1)} %refs_7_.7, bf16[3,128,4096]{2,1,0:T(8,128)(2,1)} %refs_7_.7, ...), custom_call_target="tpu_custom_call" | custom-call | bytes 2097152 | tf_op jit(solution)/shard_map/pack/pallas_call | solution.py:77
  9.2 3.1 %pack.6 = (bf16[128,1024]{1,0:T(8,128)(2,1)}, bf16[128,2304]{1,0:T(8,128)(2,1)}, s32[1]{0:T(128)}) custom-call(s32[1]{0:T(128)} %get-tuple-element.30.target, bf16[3,128,4096]{2,1,0:T(8,128)(2,1)} %refs_7_.7, bf16[3,128,4096]{2,1,0:T(8,128)(2,1)} %refs_7_.7, bf16[3,128,4096]{2,1,0:T(8,128)(2,1)} %refs_7_.7, bf16[3,128,4096]{2,1,0:T(8,128)(2,1)} %refs_7_.7, ...), custom_call_target="tpu_custom_call" | custom-call | bytes 2097152 | tf_op jit(solution)/shard_map/pack/pallas_call | solution.py:77
  12.3 0.0 copy-start.9
  12.4 2.8 %pack.7 = (bf16[128,3328]{1,0:T(8,128)(2,1)S(1)}, s32[1]{0:T(128)}) custom-call(s32[1]{0:T(128)} %get-tuple-element.33.target, bf16[3,128,4096]{2,1,0:T(8,128)(2,1)} %refs_7_.7, bf16[3,128,4096]{2,1,0:T(8,128)(2,1)} %refs_7_.7, bf16[3,128,4096]{2,1,0:T(8,128)(2,1)} %refs_7_.7, bf16[3,128,4096]{2,1,0:T(8,128)(2,1)} %refs_7_.7, bf16[3,128,4096]{2,1,0:T(8,128)(2,1)} %refs_7_.7, ...), custom_call_target="tpu_custom_call" | custom-call | bytes 2097152 | tf_op jit(solution)/shard_map/pack/pallas_call | solution.py:77
  15.3 0.9 copy-done.4
  16.2 1.3 %collective-permute-start.2 = (bf16[128,1024]{1,0:T(8,128)(2,1)S(1)}, bf16[128,1024]{1,0:T(8,128)(2,1)S(1)}, u32[]{:S(2)}, u32[]{:S(2)}) collective-permute-start(bf16[128,1024]{1,0:T(8,128)(2,1)S(1)} %slice.46), channel_id=1, source_target_pairs={{4,0},{8,4},{12,8},{16,12},{20,16},{24,20},{28,24},{5,1},{9,5},{13... | collective-permute-start | bytes 786440 | tf_op jit(solution)/shard_map/ppermute | solution.py:24
  17.5 1.6 %collective-permute-start.6 = (bf16[128,3328]{1,0:T(8,128)(2,1)}, bf16[128,3328]{1,0:T(8,128)(2,1)}, u32[]{:S(2)}, u32[]{:S(2)}) collective-permute-start(bf16[128,3328]{1,0:T(8,128)(2,1)} %get-tuple-element.46), channel_id=1, source_target_pairs={{0,2},{1,3},{2,0},{3,1},{4,6},{5,7},{6,4},{7,5},{8,10},{9,11},{10,... | collective-permute-start | bytes 2555912 | tf_op jit(solution)/shard_map/ppermute | solution.py:18
  19.0 0.1 collective-permute-start
  19.1 2.9 %collective-permute-start.1 = (bf16[128,2304]{1,0:T(8,128)(2,1)}, bf16[128,2304]{1,0:T(8,128)(2,1)}, u32[]{:S(2)}, u32[]{:S(2)}) collective-permute-start(bf16[128,2304]{1,0:T(8,128)(2,1)} %get-tuple-element.32), channel_id=1, source_target_pairs={{0,3},{1,2},{2,1},{3,0},{4,7},{5,6},{6,5},{7,4},{8,11},{9,10},{10,... | collective-permute-start | bytes 1769480 | tf_op jit(solution)/shard_map/ppermute | solution.py:18
  22.0 0.9 convolution_bitcast_fusion
  22.9 0.0 copy-done.12
  23.0 3.4 %build.1 = (bf16[5,2,3840,256]{3,2,1,0:T(8,128)(2,1)S(1)}, bf16[2,15,256,256]{3,2,1,0:T(8,128)(2,1)S(1)}, bf16[2,256,256]{2,1,0:T(8,128)(2,1)S(1)}) custom-call(s32[1]{0:T(128)} %get-tuple-element.36._, f32[6,4,1024]{2,1,0:T(4,128)S(1)} %copy-done.8), custom_call_target="tpu_custom_call" | custom-call | flops 20971520 | bytes 25165824 | tf_op jit(solution)/shard_map/build/pallas_call | solution.py:226
  26.4 0.7 copy-done.6
  27.2 1.8 %copy-done.5 = bf16[128,3328]{1,0:T(8,128)(2,1)S(1)} copy-done((bf16[128,3328]{1,0:T(8,128)(2,1)S(1)}, bf16[128,3328]{1,0:T(8,128)(2,1)}, u32[]{:S(2)}) %copy-start.5) | copy-done | bytes 851992
  29.0 1.1 %copy-done.7 = bf16[128,1024]{1,0:T(8,128)(2,1)S(1)} copy-done((bf16[128,1024]{1,0:T(8,128)(2,1)S(1)}, bf16[128,1024]{1,0:T(8,128)(2,1)}, u32[]{:S(2)}) %copy-start.7) | copy-done | bytes 262168
  30.1 3.5 %image.4 = (bf16[128,4096]{1,0:T(8,128)(2,1)S(1)}, bf16[128,4096]{1,0:T(8,128)(2,1)S(1)}, f32[1,128,128]{2,1,0:T(8,128)S(1)}) custom-call(bf16[128,3328]{1,0:T(8,128)(2,1)S(1)} %copy-done.5, bf16[128,1024]{1,0:T(8,128)(2,1)S(1)} %copy-done.7, bf16[5,2,3840,256]{3,2,1,0:T(8,128)(2,1)S(1)} %get-tuple-element.37.refs_2_.refs_3_, ...), custom_call_target="tpu_custom_call" | custom-call | flops 3019898880 | bytes 25165824 | tf_op jit(solution)/shard_map/image/pallas_call | solution.py:331
  33.6 1.0 copy-done.2
  34.6 0.7 crop.4
  35.3 1.3 %collective-permute-start.5 = (bf16[128,1024]{1,0:T(8,128)(2,1)}, bf16[128,1024]{1,0:T(8,128)(2,1)}, u32[]{:S(2)}, u32[]{:S(2)}) collective-permute-start(bf16[128,1024]{1,0:T(8,128)(2,1)} %crop.4), channel_id=1, source_target_pairs={{4,0},{8,4},{12,8},{16,12},{20,16},{24,20},{28,24},{5,1},{9,5},{13... | collective-permute-start | bytes 786440 | tf_op jit(solution)/shard_map/ppermute | solution.py:24
  36.6 0.8 fusion
  37.4 0.2 dynamic_update_slice.3
  37.6 0.1 pad_add_fusion.refs_16_
  37.7 1.3 %collective-permute-start.3 = (bf16[128,1024]{1,0:T(8,128)(2,1)S(1)}, bf16[128,1024]{1,0:T(8,128)(2,1)S(1)}, u32[]{:S(2)}, u32[]{:S(2)}) collective-permute-start(bf16[128,1024]{1,0:T(8,128)(2,1)S(1)} %crop.3), channel_id=1, source_target_pairs={{4,0},{8,4},{12,8},{16,12},{20,16},{24,20},{28,24},{5,1},{9,5},{13... | collective-permute-start | bytes 786440 | tf_op jit(solution)/shard_map/ppermute | solution.py:24
  39.0 18.8 %collective-permute-done.6.piece_ref.refs_0_ = bf16[128,3328]{1,0:T(8,128)(2,1)} collective-permute-done((bf16[128,3328]{1,0:T(8,128)(2,1)}, bf16[128,3328]{1,0:T(8,128)(2,1)}, u32[]{:S(2)}, u32[]{:S(2)}) %collective-permute-start.6) | collective-permute-done | bytes 852000 | tf_op jit(solution)/shard_map/ppermute | solution.py:18
  57.8 1.2 %crop.5 = bf16[128,1024]{1,0:T(8,128)(2,1)S(1)} custom-call(bf16[128,3328]{1,0:T(8,128)(2,1)} %collective-permute-done.6.piece_ref.refs_0_, f32[1,128,128]{2,1,0:T(8,128)S(1)} %get-tuple-element.40._.refs_12_), custom_call_target="tpu_custom_call" | custom-call | bytes 524288 | tf_op jit(solution)/shard_map/crop/pallas_call | solution.py:98
  58.9 1.5 %collective-permute-start.7 = (bf16[128,1024]{1,0:T(8,128)(2,1)S(1)}, bf16[128,1024]{1,0:T(8,128)(2,1)S(1)}, u32[]{:S(2)}, u32[]{:S(2)}) collective-permute-start(bf16[128,1024]{1,0:T(8,128)(2,1)S(1)} %crop.5), channel_id=1, source_target_pairs={{4,0},{8,4},{12,8},{16,12},{20,16},{24,20},{28,24},{5,1},{9,5},{13... | collective-permute-start | bytes 786440 | tf_op jit(solution)/shard_map/ppermute | solution.py:24
  60.4 6.6 %copy-done.1 = bf16[5,2,3840,256]{3,2,1,0:T(8,128)(2,1)S(1)} copy-done((bf16[5,2,3840,256]{3,2,1,0:T(8,128)(2,1)S(1)}, bf16[5,2,3840,256]{3,2,1,0:T(8,128)(2,1)}, u32[]{:S(2)}) %copy-start.1) | copy-done | bytes 19660824
  67.0 2.1 %copy-done.3 = bf16[2,15,256,256]{3,2,1,0:T(8,128)(2,1)S(1)} copy-done((bf16[2,15,256,256]{3,2,1,0:T(8,128)(2,1)S(1)}, bf16[2,15,256,256]{3,2,1,0:T(8,128)(2,1)}, u32[]{:S(2)}) %copy-start.3) | copy-done | bytes 3932184
  69.1 4.8 %image.5 = (bf16[128,4096]{1,0:T(8,128)(2,1)S(1)}, bf16[128,4096]{1,0:T(8,128)(2,1)S(1)}, f32[2,128,128]{2,1,0:T(8,128)S(1)}) custom-call(bf16[128,3328]{1,0:T(8,128)(2,1)S(1)} %collective-permute-done.4.piece_ref.refs_0_, bf16[128,1024]{1,0:T(8,128)(2,1)} %collective-permute-done.5.refs_1_, bf16[5,2,3840,256]{3,2,1,0:T(8,128)(2,1)S(1)} %copy-done.1, ...), custom_call_target="tpu_custom_call" | custom-call | flops 3288334336 | bytes 25165824 | tf_op jit(solution)/shard_map/image/pallas_call | solution.py:331
  74.0 5.5 %image.6 = (bf16[128,4096]{1,0:T(8,128)(2,1)S(1)}, bf16[128,4096]{1,0:T(8,128)(2,1)S(1)}, f32[3,128,128]{2,1,0:T(8,128)S(1)}) custom-call(bf16[128,3328]{1,0:T(8,128)(2,1)} %collective-permute-done.6.piece_ref.refs_0_, bf16[128,1024]{1,0:T(8,128)(2,1)S(1)} %collective-permute-done.7.refs_1_, bf16[5,2,3840,256]{3,2,1,0:T(8,128)(2,1)S(1)} %copy-done.1, ...), custom_call_target="tpu_custom_call" | custom-call | flops 3556769792 | bytes 25165824 | tf_op jit(solution)/shard_map/image/pallas_call | solution.py:331
  79.5 6.1 %image.7 = (f32[264,512]{1,0:T(8,128)S(1)}, f32[264,512]{1,0:T(8,128)S(1)}) custom-call(bf16[128,1024]{1,0:T(8,128)(2,1)S(1)} %collective-permute-done.piece_ref.refs_0_, bf16[128,2304]{1,0:T(8,128)(2,1)} %collective-permute-done.1.refs_1_, bf16[128,1024]{1,0:T(8,128)(2,1)S(1)} %collective-permute-done.3.refs_2_, bf16[5,2,3840,256]{3,2,1,0:T(8,128)(2,1)S(1)} %copy-done.1, ...), custom_call_target="tpu_custom_call" | custom-call | flops 3825205248 | bytes 25165824 | tf_op jit(solution)/shard_map/image/pallas_call | solution.py:331
  85.6 1.2 %collective-permute-start.8 = (f32[264,512]{1,0:T(8,128)S(1)}, f32[264,512]{1,0:T(8,128)S(1)}, u32[]{:S(2)}, u32[]{:S(2)}) collective-permute-start(f32[264,512]{1,0:T(8,128)S(1)} %get-tuple-element.54), channel_id=1, source_target_pairs={{0,4},{4,0},{8,12},{12,8},{16,20},{20,16},{24,28},{28,24},{1,5},{5... | collective-permute-start | bytes 1622024 | tf_op jit(solution)/shard_map/ppermute | solution.py:18
  86.8 1.6 %collective-permute-done.8 = f32[264,512]{1,0:T(8,128)S(1)} collective-permute-done((f32[264,512]{1,0:T(8,128)S(1)}, f32[264,512]{1,0:T(8,128)S(1)}, u32[]{:S(2)}, u32[]{:S(2)}) %collective-permute-start.8) | collective-permute-done | bytes 540704 | tf_op jit(solution)/shard_map/ppermute | solution.py:18
  88.3 0.1 add.36
  88.5 1.6 %collective-permute-start.10 = (f32[264,128]{1,0:T(8,128)S(1)}, f32[264,128]{1,0:T(8,128)S(1)}, u32[]{:S(2)}, u32[]{:S(2)}) collective-permute-start(f32[264,128]{1,0:T(8,128)S(1)} %get-tuple-element.57), channel_id=1, source_target_pairs={{0,2},{1,3},{2,0},{3,1},{4,6},{5,7},{6,4},{7,5},{8,10},{9,11},{10,... | collective-permute-start | bytes 405512 | tf_op jit(solution)/shard_map/ppermute | solution.py:18
  90.1 0.0 collective-permute-start.11
  90.1 1.9 %collective-permute-start.9 = (f32[264,128]{1,0:T(8,128)S(1)}, f32[264,128]{1,0:T(8,128)S(1)}, u32[]{:S(2)}, u32[]{:S(2)}) collective-permute-start(f32[264,128]{1,0:T(8,128)S(1)} %get-tuple-element.55), channel_id=1, source_target_pairs={{0,1},{1,0},{2,3},{3,2},{4,5},{5,4},{6,7},{7,6},{8,9},{9,8},{10,11... | collective-permute-start | bytes 405512 | tf_op jit(solution)/shard_map/ppermute | solution.py:18
  92.0 5.1 %collective-permute-done.10 = f32[264,128]{1,0:T(8,128)S(1)} collective-permute-done((f32[264,128]{1,0:T(8,128)S(1)}, f32[264,128]{1,0:T(8,128)S(1)}, u32[]{:S(2)}, u32[]{:S(2)}) %collective-permute-start.10) | collective-permute-done | bytes 135200 | tf_op jit(solution)/shard_map/ppermute | solution.py:18
  97.1 0.3 collective-permute-done.11
  97.4 1.1 collective-permute-done.9
  98.6 2.0 %collective-permute-start.12 = (f32[72,128]{1,0:T(8,128)S(1)}, f32[72,128]{1,0:T(8,128)S(1)}, u32[]{:S(2)}, u32[]{:S(2)}) collective-permute-start(f32[72,128]{1,0:T(8,128)S(1)} %get-tuple-element.63), channel_id=1, source_target_pairs={{0,8},{4,12},{8,0},{12,4},{16,24},{20,28},{24,16},{28,20},{1,9},{5... | collective-permute-start | bytes 110600 | tf_op jit(solution)/shard_map/ppermute | solution.py:18
  100.6 2.6 %collective-permute-start.13 = (f32[72,128]{1,0:T(8,128)S(1)}, f32[72,128]{1,0:T(8,128)S(1)}, u32[]{:S(2)}, u32[]{:S(2)}) collective-permute-start(f32[72,128]{1,0:T(8,128)S(1)} %get-tuple-element.64), channel_id=1, source_target_pairs={{0,16},{4,20},{8,24},{12,28},{16,0},{20,4},{24,8},{28,12},{1,17},{... | collective-permute-start | bytes 110600 | tf_op jit(solution)/shard_map/ppermute | solution.py:18
  103.2 2.6 %collective-permute-done.13 = f32[72,128]{1,0:T(8,128)S(1)} collective-permute-done((f32[72,128]{1,0:T(8,128)S(1)}, f32[72,128]{1,0:T(8,128)S(1)}, u32[]{:S(2)}, u32[]{:S(2)}) %collective-permute-start.13) | collective-permute-done | bytes 36896 | tf_op jit(solution)/shard_map/ppermute | solution.py:18
  105.8 3.2 %collective-permute-done.14 = f32[72,128]{1,0:T(8,128)S(1)} collective-permute-done((f32[72,128]{1,0:T(8,128)S(1)}, f32[72,128]{1,0:T(8,128)S(1)}, u32[]{:S(2)}, u32[]{:S(2)}) %collective-permute-start.14) | collective-permute-done | bytes 36896 | tf_op jit(solution)/shard_map/ppermute | solution.py:18
  109.0 0.6 slice_bitcast_fusion
  109.6 0.6 fusion.8
  (41 shorter events, 0.3 us)
Async XLA Ops:
  3.1 31.5 %collective-permute-start.4 = (bf16[128,3328]{1,0:T(8,128)(2,1)}, bf16[128,3328]{1,0:T(8,128)(2,1)S(1)}, u32[]{:S(2)}, u32[]{:S(2)}) collective-permute-start(bf16[128,3328]{1,0:T(8,128)(2,1)} %get-tuple-element.43), channel_id=1, source_target_pairs={{0,1},{1,0},{2,3},{3,2},{4,5},{5,4},{6,7},{7,6},{8,9},{9,8},{10,11... | collective-permute-start | bytes 2555912 | tf_op jit(solution)/shard_map/ppermute | solution.py:18
  12.3 9.6 %copy-start.9 = (bf16[3,128,4096]{2,1,0:T(8,128)(2,1)S(1)}, bf16[3,128,4096]{2,1,0:T(8,128)(2,1)}, u32[]{:S(2)}) copy-start(bf16[3,128,4096]{2,1,0:T(8,128)(2,1)} %refs_7_.7) | copy-start | bytes 9437188
  12.3 9.6 %copy-start.10 = (bf16[3,4096]{1,0:T(4,128)(2,1)S(1)}, bf16[3,4096]{1,0:T(4,128)(2,1)}, u32[]{:S(2)}) copy-start(bf16[3,4096]{1,0:T(4,128)(2,1)} %param.6) | copy-start | bytes 73732
  15.2 7.7 %copy-start.11 = (f32[4,1024]{1,0:T(4,128)S(1)}, f32[4,1024]{1,0:T(4,128)}, u32[]{:S(2)}) copy-start(f32[4,1024]{1,0:T(4,128)} %param.9) | copy-start | bytes 49156
  15.2 7.7 %copy-start.12 = (s32[4,1024]{1,0:T(4,128)S(1)}, s32[4,1024]{1,0:T(4,128)}, u32[]{:S(2)}) copy-start(s32[4,1024]{1,0:T(4,128)} %param.8) | copy-start | bytes 49156
  15.2 7.8 %copy-start.8 = (f32[6,4,1024]{2,1,0:T(4,128)S(1)}, f32[6,4,1024]{2,1,0:T(4,128)}, u32[]{:S(2)}) copy-start(f32[6,4,1024]{2,1,0:T(4,128)} %moments_ref.1) | copy-start | bytes 294916
  15.2 0.9 copy-start.4
  16.2 10.2 %collective-permute-start.2 = (bf16[128,1024]{1,0:T(8,128)(2,1)S(1)}, bf16[128,1024]{1,0:T(8,128)(2,1)S(1)}, u32[]{:S(2)}, u32[]{:S(2)}) collective-permute-start(bf16[128,1024]{1,0:T(8,128)(2,1)S(1)} %slice.46), channel_id=1, source_target_pairs={{4,0},{8,4},{12,8},{16,12},{20,16},{24,20},{28,24},{5,1},{9,5},{13... | collective-permute-start | bytes 786440 | tf_op jit(solution)/shard_map/ppermute | solution.py:24
  17.5 40.3 %collective-permute-start.6 = (bf16[128,3328]{1,0:T(8,128)(2,1)}, bf16[128,3328]{1,0:T(8,128)(2,1)}, u32[]{:S(2)}, u32[]{:S(2)}) collective-permute-start(bf16[128,3328]{1,0:T(8,128)(2,1)} %get-tuple-element.46), channel_id=1, source_target_pairs={{0,2},{1,3},{2,0},{3,1},{4,6},{5,7},{6,4},{7,5},{8,10},{9,11},{10,... | collective-permute-start | bytes 2555912 | tf_op jit(solution)/shard_map/ppermute | solution.py:18
  19.0 18.6 %collective-permute-start = (bf16[128,1024]{1,0:T(8,128)(2,1)}, bf16[128,1024]{1,0:T(8,128)(2,1)S(1)}, u32[]{:S(2)}, u32[]{:S(2)}) collective-permute-start(bf16[128,1024]{1,0:T(8,128)(2,1)} %get-tuple-element.31), channel_id=1, source_target_pairs={{0,3},{1,2},{2,1},{3,0},{4,7},{5,6},{6,5},{7,4},{8,11},{9,10},{10,... | collective-permute-start | bytes 786440 | tf_op jit(solution)/shard_map/ppermute | solution.py:18
  19.1 60.4 %collective-permute-start.1 = (bf16[128,2304]{1,0:T(8,128)(2,1)}, bf16[128,2304]{1,0:T(8,128)(2,1)}, u32[]{:S(2)}, u32[]{:S(2)}) collective-permute-start(bf16[128,2304]{1,0:T(8,128)(2,1)} %get-tuple-element.32), channel_id=1, source_target_pairs={{0,3},{1,2},{2,1},{3,0},{4,7},{5,6},{6,5},{7,4},{8,11},{9,10},{10,... | collective-permute-start | bytes 1769480 | tf_op jit(solution)/shard_map/ppermute | solution.py:18
  26.4 7.2 %copy-start = (bf16[5,2,3840,256]{3,2,1,0:T(8,128)(2,1)}, bf16[5,2,3840,256]{3,2,1,0:T(8,128)(2,1)S(1)}, u32[]{:S(2)}) copy-start(bf16[5,2,3840,256]{3,2,1,0:T(8,128)(2,1)S(1)} %get-tuple-element.37.refs_2_.refs_3_) | copy-start | bytes 58982404
  26.4 8.2 %copy-start.2 = (bf16[2,15,256,256]{3,2,1,0:T(8,128)(2,1)}, bf16[2,15,256,256]{3,2,1,0:T(8,128)(2,1)S(1)}, u32[]{:S(2)}) copy-start(bf16[2,15,256,256]{3,2,1,0:T(8,128)(2,1)S(1)} %get-tuple-element.38.refs_3_.refs_4_) | copy-start | bytes 11796484
  26.4 0.7 copy-start.6
  27.2 1.8 %copy-start.5 = (bf16[128,3328]{1,0:T(8,128)(2,1)S(1)}, bf16[128,3328]{1,0:T(8,128)(2,1)}, u32[]{:S(2)}) copy-start(bf16[128,3328]{1,0:T(8,128)(2,1)} %copy-done.4) | copy-start | bytes 2555908
  29.0 1.1 %copy-start.7 = (bf16[128,1024]{1,0:T(8,128)(2,1)S(1)}, bf16[128,1024]{1,0:T(8,128)(2,1)}, u32[]{:S(2)}) copy-start(bf16[128,1024]{1,0:T(8,128)(2,1)} %copy-done.6) | copy-start | bytes 786436
  35.3 25.1 %collective-permute-start.5 = (bf16[128,1024]{1,0:T(8,128)(2,1)}, bf16[128,1024]{1,0:T(8,128)(2,1)}, u32[]{:S(2)}, u32[]{:S(2)}) collective-permute-start(bf16[128,1024]{1,0:T(8,128)(2,1)} %crop.4), channel_id=1, source_target_pairs={{4,0},{8,4},{12,8},{16,12},{20,16},{24,20},{28,24},{5,1},{9,5},{13... | collective-permute-start | bytes 786440 | tf_op jit(solution)/shard_map/ppermute | solution.py:24
  37.7 41.8 %collective-permute-start.3 = (bf16[128,1024]{1,0:T(8,128)(2,1)S(1)}, bf16[128,1024]{1,0:T(8,128)(2,1)S(1)}, u32[]{:S(2)}, u32[]{:S(2)}) collective-permute-start(bf16[128,1024]{1,0:T(8,128)(2,1)S(1)} %crop.3), channel_id=1, source_target_pairs={{4,0},{8,4},{12,8},{16,12},{20,16},{24,20},{28,24},{5,1},{9,5},{13... | collective-permute-start | bytes 786440 | tf_op jit(solution)/shard_map/ppermute | solution.py:24
  58.9 15.0 %collective-permute-start.7 = (bf16[128,1024]{1,0:T(8,128)(2,1)S(1)}, bf16[128,1024]{1,0:T(8,128)(2,1)S(1)}, u32[]{:S(2)}, u32[]{:S(2)}) collective-permute-start(bf16[128,1024]{1,0:T(8,128)(2,1)S(1)} %crop.5), channel_id=1, source_target_pairs={{4,0},{8,4},{12,8},{16,12},{20,16},{24,20},{28,24},{5,1},{9,5},{13... | collective-permute-start | bytes 786440 | tf_op jit(solution)/shard_map/ppermute | solution.py:24
  60.4 6.6 %copy-start.1 = (bf16[5,2,3840,256]{3,2,1,0:T(8,128)(2,1)S(1)}, bf16[5,2,3840,256]{3,2,1,0:T(8,128)(2,1)}, u32[]{:S(2)}) copy-start(bf16[5,2,3840,256]{3,2,1,0:T(8,128)(2,1)} %copy-done) | copy-start | bytes 58982404
  67.0 2.1 %copy-start.3 = (bf16[2,15,256,256]{3,2,1,0:T(8,128)(2,1)S(1)}, bf16[2,15,256,256]{3,2,1,0:T(8,128)(2,1)}, u32[]{:S(2)}) copy-start(bf16[2,15,256,256]{3,2,1,0:T(8,128)(2,1)} %copy-done.2) | copy-start | bytes 11796484
  85.6 2.8 %collective-permute-start.8 = (f32[264,512]{1,0:T(8,128)S(1)}, f32[264,512]{1,0:T(8,128)S(1)}, u32[]{:S(2)}, u32[]{:S(2)}) collective-permute-start(f32[264,512]{1,0:T(8,128)S(1)} %get-tuple-element.54), channel_id=1, source_target_pairs={{0,4},{4,0},{8,12},{12,8},{16,20},{20,16},{24,28},{28,24},{1,5},{5... | collective-permute-start | bytes 1622024 | tf_op jit(solution)/shard_map/ppermute | solution.py:18
  88.5 8.7 %collective-permute-start.10 = (f32[264,128]{1,0:T(8,128)S(1)}, f32[264,128]{1,0:T(8,128)S(1)}, u32[]{:S(2)}, u32[]{:S(2)}) collective-permute-start(f32[264,128]{1,0:T(8,128)S(1)} %get-tuple-element.57), channel_id=1, source_target_pairs={{0,2},{1,3},{2,0},{3,1},{4,6},{5,7},{6,4},{7,5},{8,10},{9,11},{10,... | collective-permute-start | bytes 405512 | tf_op jit(solution)/shard_map/ppermute | solution.py:18
  90.1 7.4 %collective-permute-start.11 = (f32[264,128]{1,0:T(8,128)S(1)}, f32[264,128]{1,0:T(8,128)S(1)}, u32[]{:S(2)}, u32[]{:S(2)}) collective-permute-start(f32[264,128]{1,0:T(8,128)S(1)} %get-tuple-element.56), channel_id=1, source_target_pairs={{0,3},{1,2},{2,1},{3,0},{4,7},{5,6},{6,5},{7,4},{8,11},{9,10},{10,... | collective-permute-start | bytes 405512 | tf_op jit(solution)/shard_map/ppermute | solution.py:18
  90.1 8.4 %collective-permute-start.9 = (f32[264,128]{1,0:T(8,128)S(1)}, f32[264,128]{1,0:T(8,128)S(1)}, u32[]{:S(2)}, u32[]{:S(2)}) collective-permute-start(f32[264,128]{1,0:T(8,128)S(1)} %get-tuple-element.55), channel_id=1, source_target_pairs={{0,1},{1,0},{2,3},{3,2},{4,5},{5,4},{6,7},{7,6},{8,9},{9,8},{10,11... | collective-permute-start | bytes 405512 | tf_op jit(solution)/shard_map/ppermute | solution.py:18
  98.6 4.6 %collective-permute-start.12 = (f32[72,128]{1,0:T(8,128)S(1)}, f32[72,128]{1,0:T(8,128)S(1)}, u32[]{:S(2)}, u32[]{:S(2)}) collective-permute-start(f32[72,128]{1,0:T(8,128)S(1)} %get-tuple-element.63), channel_id=1, source_target_pairs={{0,8},{4,12},{8,0},{12,4},{16,24},{20,28},{24,16},{28,20},{1,9},{5... | collective-permute-start | bytes 110600 | tf_op jit(solution)/shard_map/ppermute | solution.py:18
  100.6 5.2 %collective-permute-start.13 = (f32[72,128]{1,0:T(8,128)S(1)}, f32[72,128]{1,0:T(8,128)S(1)}, u32[]{:S(2)}, u32[]{:S(2)}) collective-permute-start(f32[72,128]{1,0:T(8,128)S(1)} %get-tuple-element.64), channel_id=1, source_target_pairs={{0,16},{4,20},{8,24},{12,28},{16,0},{20,4},{24,8},{28,12},{1,17},{... | collective-permute-start | bytes 110600 | tf_op jit(solution)/shard_map/ppermute | solution.py:18
  103.2 5.8 %collective-permute-start.14 = (f32[72,128]{1,0:T(8,128)S(1)}, f32[72,128]{1,0:T(8,128)S(1)}, u32[]{:S(2)}, u32[]{:S(2)}) collective-permute-start(f32[72,128]{1,0:T(8,128)S(1)} %concatenate.27), channel_id=1, source_target_pairs={{0,24},{4,28},{8,16},{12,20},{16,8},{20,12},{24,0},{28,4},{1,25},{... | collective-permute-start | bytes 110600 | tf_op jit(solution)/shard_map/ppermute | solution.py:18

commit v3 on v2

v3 whole, which is shorter than its diff:
```python
import functools

import jax
import jax.numpy as jnp
from jax import lax
from jax.experimental import pallas as pl
from jax.experimental.pallas import tpu as pltpu
from jax.sharding import PartitionSpec as P

GX = 64
GY = 16
TILE = 128
EDGE = 256


def exchange(value, axis, by):
    count = lax.axis_size(axis)
    return lax.ppermute(value, axis, [(i, i ^ by) for i in range(count)])


def shifted(value, axis, by):
    count = lax.axis_size(axis)
    pairs = [(i, i + by) for i in range(count) if 0 <= i + by < count]
    return lax.ppermute(value, axis, pairs)


def lane_of(shape):
    return lax.broadcasted_iota(jnp.int32, shape, 1)


def pack_kernel(layers, plane, n_col, labels, cuts, me, sens_ref, *refs):
    outs, (planes, edges, sems, edge_sems) = refs[:-4], refs[-4:]
    next_ref, outs = outs[-1], list(outs[:-1])
    width = plane // n_col
    for i in range(3):
        next_ref[i] = me[i]
    top_block = layers * plane // TILE - 1
    rows = sens_ref.shape[1]
    pending = {}
    for index, label in enumerate(labels):
        target = me[0] ^ label
        for level in range(layers):
            source = pl.ds(pl.multiple_of((level * n_col + target) * width, width), width)
            block = jnp.minimum((level * plane + (target + 1) * width) // TILE, top_block)
            edge = pl.ds(pl.multiple_of(block * TILE, TILE), TILE)
            copies = (
                pltpu.make_async_copy(sens_ref.at[:, :, source], planes.at[index, level], sems.at[index, level]),
                pltpu.make_async_copy(sens_ref.at[:, :, edge], edges.at[index, level], edge_sems.at[index, level]),
            )
            for copy in copies:
                copy.start()
            pending[index, level] = copies
    lane = lane_of((rows, TILE))
    for index, (label, cut) in enumerate(zip(labels, cuts)):
        arrays = [outs.pop(0) for _ in range(2 if cut else 1)]

        def put(start, value):
            array = arrays[0]
            if start >= array.shape[1]:
                start, array = start - array.shape[1], arrays[1]
            array[:, start : start + value.shape[1]] = value

        inside = (me[0] ^ label) != n_col - 1
        halo = [jnp.zeros((rows, TILE), jnp.float32)] * (EDGE // TILE)
        for level in range(layers):
            for copy in pending[index, level]:
                copy.wait()
            for k in range(3):
                start = (3 * level + k) * width + (EDGE if level else 0)
                put(start, planes[index, level, k])
                tile, at = divmod(edge_at(k, level, layers), TILE)
                edge = edges[index, level, k].astype(jnp.float32)
                edge = pltpu.roll(edge, at, 1) if at else edge
                halo[tile] = jnp.where((lane >= at) & (lane < at + GY) & inside, edge, halo[tile])
        for tile, value in enumerate(halo):
            put(3 * width + tile * TILE, value.astype(sens_ref.dtype))


def edge_at(k, level, layers):
    return (k * (layers + 1) + level) * GY


def pack(sensitivity, me, labels, cuts, layers, plane, n_col):
    cols, dtype = sensitivity.shape[1], sensitivity.dtype
    width = plane // n_col
    outs, counts = [], []
    for cut in cuts:
        sizes = [3 * cut * width + EDGE, 3 * (layers - cut) * width] if cut else [3 * layers * width + EDGE]
        outs += [jax.ShapeDtypeStruct((cols, size), dtype) for size in sizes]
        counts.append(len(sizes))
    count = len(labels)
    *found, me = pl.pallas_call(
        functools.partial(pack_kernel, layers, plane, n_col, labels, cuts),
        in_specs=[pl.BlockSpec(memory_space=pltpu.SMEM), pl.BlockSpec(memory_space=pltpu.HBM)],
        out_specs=[pl.BlockSpec(memory_space=pltpu.VMEM)] * len(outs) + [pl.BlockSpec(memory_space=pltpu.SMEM)],
        out_shape=[*outs, jax.ShapeDtypeStruct((3,), jnp.int32)],
        scratch_shapes=[
            pltpu.VMEM((count, layers, 3, cols, width), dtype),
            pltpu.VMEM((count, layers, 3, cols, TILE), dtype),
            pltpu.SemaphoreType.DMA((count, layers)),
            pltpu.SemaphoreType.DMA((count, layers)),
        ],
        compiler_params=pltpu.CompilerParams(vmem_limit_bytes=8 << 20),
        cost_estimate=pl.CostEstimate(flops=0, bytes_accessed=6 << 20, transcendentals=0),
        name="pack",
    )(me, sensitivity)
    return [[found.pop(0) for _ in range(size)] for size in counts], me


def crop_kernel(piece_ref, _, out_ref):
    out_ref[...] = piece_ref[:, : out_ref.shape[1]]


def crop(piece, size, after):
    return pl.pallas_call(
        crop_kernel,
        in_specs=[pl.BlockSpec(memory_space=pltpu.VMEM), pl.BlockSpec(memory_space=pl.ANY)],
        out_specs=pl.BlockSpec(memory_space=pltpu.VMEM),
        out_shape=jax.ShapeDtypeStruct((piece.shape[0], size), piece.dtype),
        compiler_params=pltpu.CompilerParams(vmem_limit_bytes=8 << 20),
        cost_estimate=pl.CostEstimate(flops=0, bytes_accessed=0, transcendentals=0),
        name="crop",
    )(piece, after)


def component(a, b):
    a, b = min(a, b), max(a, b)
    return a if a == b else a + b + 2


def tile_start(z, k, side, other, layers):
    base = 15 * z + ((0, 6, 11)[k] if z < layers else (0, 3, 5)[k])
    return base + (other - k if side == 0 else 3 - k + other)


def build_kernel(layers, width, _, moments_ref, after_ref, plane_ref, edge_ref, corner_ref, field_ref, ahead_ref):
    f32, bf16 = jnp.float32, jnp.bfloat16
    shape = (GY, width)
    lane = lane_of(shape)
    row = lax.broadcasted_iota(jnp.int32, shape, 0)
    pos_x, pos_y = lane // GY, lane % GY
    same, up, down = row == pos_y, row == pos_y + 1, row == pos_y - 1
    zero = jnp.zeros(shape, f32)
    field_lane = lane_of((8, width))
    columns = width // GY
    near = [pos_x % 3 == r for r in range(3)]
    follow = [(pos_x + 1) % 3 == r for r in range(3)]
    band = [jnp.where((pos_x >= x - 1) & (pos_x <= x + 1), 1.0, 0.0).astype(bf16) for x in range(columns)]
    tile_lane = lane_of((GY, TILE))

    def spread(middle, ahead, behind):
        def whole(value):
            return jnp.broadcast_to(value, shape)

        return jnp.where(same, whole(middle), jnp.where(up, whole(ahead), jnp.where(down, whole(behind), zero)))

    def two_terms(value):
        hi = value.astype(bf16)
        return hi, (value - hi.astype(f32)).astype(bf16)

    edge_ref[...] = jnp.zeros_like(edge_ref)
    field_ref[...] = jnp.zeros_like(field_ref)
    for z in range(layers + 1):
        whole = None
        for level in (z, z - 1):
            if 0 <= level < layers:
                part = moments_ref[:, level, :] * (2.0 / 216.0)
                whole = part if whole is None else whole + part
        field_ref[2 * z, :6] = whole
        if z < layers:
            field_ref[2 * z + 1, :6] = moments_ref[:, z, :] * (1.0 / 216.0)

    for pair in range(2 * layers + 1):
        z, side = divmod(pair, 2)
        element = field_ref[pair]
        before = jnp.where(field_lane >= GY, pltpu.roll(element, GY, 1), 0.0)
        parts = []
        for value in (2.0 * (element + before), element, before):
            lower = jnp.where(field_lane % GY != 0, pltpu.roll(value, 1, 1), 0.0)
            parts.append((2.0 * (value + lower), value, lower))
        for c in range(6):
            here, ahead, behind = [spread(*(v[c : c + 1] for v in part)) for part in parts]
            ahead_ref[pair, c] = ahead[:, width - TILE :]
            scale = 0.5 if side == 0 and c < 3 else None
            spots = []
            for k in range(3):
                for other in range(3):
                    if component(k, other) == c and (side == 1 or other >= k):
                        spots.append(tile_start(z, k, side, other, layers))
            for r in range(3):
                value = jnp.where(near[r], here, jnp.where(follow[r], ahead, behind))
                if scale is not None:
                    value = value * scale
                for term, piece in enumerate(two_terms(value)):
                    for x in range(r, columns, 3):
                        block = piece * band[x]
                        for spot in spots:
                            start = spot * width + x * GY
                            plane_ref[term, start : start + GY, :] = block

    edge_lane = tile_lane // GY == TILE // GY - 1
    for z in range(layers + 1):
        for other_z in range(max(z - 1, 0), min(z + 1, layers) + 1):
            pair = 2 * z if other_z == z else 2 * min(z, other_z) + 1
            for c in range(6):
                value = jnp.where(edge_lane, ahead_ref[pair, c], 0.0)
                for term, piece in enumerate(two_terms(value)):
                    for k in range(3):
                        for other in range(3):
                            if component(k, other) == c:
                                start = edge_at(other, other_z, layers)
                                edge_ref[term, 3 * z + k, start : start + GY, :] = piece

    corner_ref[...] = jnp.zeros_like(corner_ref)
    for other_z in range(layers + 1):
        for other in range(3):
            tiles = [jnp.zeros((GY, TILE), f32)] * (EDGE // TILE)
            for z in range(max(other_z - 1, 0), min(other_z + 1, layers) + 1):
                pair = 2 * z if other_z == z else 2 * min(z, other_z) + 1
                for k in range(3):
                    tile, at = divmod(edge_at(k, z, layers), TILE)
                    value = ahead_ref[pair, component(k, other)]
                    turn = (at + GY) % TILE
                    value = pltpu.roll(value, turn, 1) if turn else value
                    tiles[tile] = jnp.where(tile_lane // GY == at // GY, value, tiles[tile])
            start = edge_at(other, other_z, layers)
            for tile, value in enumerate(tiles):
                for term, piece in enumerate(two_terms(value)):
                    corner_ref[term, start : start + GY, tile * TILE : (tile + 1) * TILE] = piece


def in_vmem(x):
    return pltpu.with_memory_space_constraint(x, pltpu.VMEM)


def build(moments, place, width, after):
    layers = moments.shape[1]
    shapes = [
        pltpu.VMEM((2, (15 * layers + 6) * width, width), jnp.bfloat16),
        pltpu.VMEM((2, 3 * (layers + 1), EDGE, TILE), jnp.bfloat16),
        pltpu.VMEM((2, EDGE, EDGE), jnp.bfloat16),
    ]
    out = pl.pallas_call(
        functools.partial(build_kernel, layers, width),
        grid_spec=pltpu.PrefetchScalarGridSpec(
            num_scalar_prefetch=1,
            grid=(1,),
            in_specs=[
                pl.BlockSpec((6, layers, width), lambda i, t: (0, 0, t[0])),
                pl.BlockSpec(memory_space=pl.ANY),
            ],
            out_specs=[pl.BlockSpec(memory_space=pltpu.VMEM)] * 3,
            scratch_shapes=[
                pltpu.VMEM((2 * layers + 1, 8, width), jnp.float32),
                pltpu.VMEM((2 * layers + 1, 6, GY, TILE), jnp.float32),
            ],
        ),
        out_shape=shapes,
        compiler_params=pltpu.CompilerParams(vmem_limit_bytes=8 << 20),
        cost_estimate=pl.CostEstimate(flops=0, bytes_accessed=0, transcendentals=0),
        name="build",
    )(place, moments, after)
    return [in_vmem(x) for x in out]


def image_kernel(layers, width, parts, label, seen, *refs):
    refs = list(refs)
    pieces = [refs.pop(0) for _ in range(parts)]
    first_ref = pieces[0]
    top_ref, plane_ref, edge_ref, corner_ref = (refs.pop(0) for _ in range(4))
    before = [(refs.pop(0), refs.pop(0)) for _ in seen]
    blocks = len(seen) + 1
    block_refs = None
    if len(refs) > 3:
        block_refs = [refs.pop(0) for _ in seen]
        small_ref, place = refs.pop(0), refs.pop(0)
        keep_ref, send_ref, values_ref, image_ref = refs
    else:
        values_ref, image_ref, block_ref = refs
    f32, bf16 = jnp.float32, jnp.bfloat16
    depth = 3 * (layers + 1) * width
    rows = first_ref.shape[0]

    values_ref[:, : 3 * width] = first_ref[:, : 3 * width]
    begin = 3 * width
    for array, skip in zip(pieces, (3 * width + EDGE, 0)):
        if skip < array.shape[1]:
            end = begin + array.shape[1] - skip
            values_ref[:, begin:end] = array[:, skip:]
            begin = end
    values_ref[:, 3 * layers * width : depth] = top_ref[:, : 3 * width]
    lane = lane_of((rows, EDGE))
    group = lane // GY
    halo = first_ref[:, 3 * width : 3 * width + EDGE].astype(f32)
    top = pltpu.roll(top_ref[:, 3 * width :].astype(f32), layers * GY, 1)
    halo = jnp.where(group % (layers + 1) == layers, top, halo)
    halo = jnp.where(group < 3 * (layers + 1), halo, 0.0).astype(bf16)
    values_ref[:, depth:] = halo

    def dot(a, b):
        return jnp.dot(a, b, preferred_element_type=f32)

    for z in range(layers + 1):
        for k in range(3):
            lo = (3 * z + k) * width
            hi = min(3 * (z + 2) * width, depth)
            value = values_ref[:, lo:hi]
            start = tile_start(z, k, 0, k, layers) * width
            matrix = plane_ref.at[:, start : start + hi - lo, :]
            total = dot(value, matrix[0]) + dot(value, matrix[1])
            edge = dot(halo, edge_ref[0, 3 * z + k]) + dot(halo, edge_ref[1, 3 * z + k])
            inner = width - TILE
            if inner:
                image_ref[:, lo : lo + inner] = total[:, :inner].astype(bf16)
            image_ref[:, lo + inner : lo + width] = (total[:, inner:] + edge).astype(bf16)
    image_ref[:, depth:] = (dot(halo, corner_ref[0]) + dot(halo, corner_ref[1])).astype(bf16)

    def product(a, b):
        return lax.dot_general(a[...], b[...], (((1,), (1,)), ((), ())), preferred_element_type=f32)

    found = [product(v, image_ref) + product(i, values_ref) for v, i in before]
    own = product(values_ref, image_ref)
    found.append(own + own.T)
    if block_refs is None:
        for j, value in enumerate(found):
            block_ref[j] = value
        return
    half = rows // 2
    order = [*seen, label]
    for i in range(blocks):
        at = pl.ds(pl.multiple_of((i ^ place[2]) * half, half), half)
        for j in range(blocks):
            lo, hi = sorted((order.index(i), order.index(j)))
            block = found[lo] if hi == blocks - 1 else block_refs[hi][lo]
            block = block.T if order.index(i) > order.index(j) else block
            for ref, low in ((keep_ref, 0), (send_ref, 1)):
                ref[at, j * rows : (j + 1) * rows] = jnp.where(place[1] == low, block[:half], block[half:])
    for j in range(blocks):
        for ref in (keep_ref, send_ref):
            ref[blocks * half :, j * rows : (j + 1) * rows] = small_ref[...]


def image_piece(label, seen, piece, top, matrix, before, blocks, small, place, n_col):
    cols = top.shape[0]
    width = (top.shape[1] - EDGE) // 3
    layers = (sum(x.shape[1] for x in piece) - EDGE) // (3 * width)
    total = 3 * (layers + 1) * width + EDGE
    vmem = pl.BlockSpec(memory_space=pltpu.VMEM)
    args = [*piece, top, *matrix, *(x for pair in before for x in pair)]
    in_specs = [vmem] * (len(piece) + 4 + 2 * len(before))
    shape = pltpu.VMEM((cols, total), top.dtype)
    scratch = []
    last = len(seen) == n_col - 1
    if last:
        args += [*blocks, small, place]
        in_specs += [vmem] * (len(blocks) + 1) + [pl.BlockSpec(memory_space=pltpu.SMEM)]
        outs = [pltpu.VMEM((cols * n_col // 2 + small.shape[0], cols * n_col), jnp.float32)] * 2
        scratch = [shape] * 2
    else:
        outs = [shape, shape, pltpu.VMEM((len(seen) + 1, cols, cols), jnp.float32)]
    out = pl.pallas_call(
        functools.partial(image_kernel, layers, width, len(piece), label, seen),
        in_specs=in_specs,
        out_specs=[vmem] * len(outs),
        out_shape=outs,
        scratch_shapes=scratch,
        compiler_params=pltpu.CompilerParams(vmem_limit_bytes=8 << 20),
        cost_estimate=pl.CostEstimate(flops=0, bytes_accessed=16 << 20, transcendentals=0),
        name="image",
    )(*args)
    return out if last else [in_vmem(x) for x in out]


def sums_kernel(blocks, me, sens_ref, force_ref, label_ref, misfit_ref, out_ref):
    step = pl.program_id(0)
    f32, bf16 = jnp.float32, jnp.bfloat16
    cols = sens_ref.shape[1]
    contract = (((1,), (1,)), ((), ()))

    @pl.when(step == 0)
    def _():
        layers, width = label_ref.shape
        row = lax.broadcasted_iota(jnp.int32, (8, width), 0)
        zone = lax.broadcasted_iota(jnp.int32, (cols, width), 0)
        out_ref[:blocks] = jnp.zeros((blocks, cols), f32)
        for b in range(blocks):
            total = jnp.zeros((8, cols), f32)
            for level in range(layers):
                value = jnp.broadcast_to(misfit_ref[level : level + 1], (8, width))
                high = value.astype(bf16).astype(f32)
                middle = (value - high).astype(bf16).astype(f32)
                low = value - high - middle
                terms = jnp.where(row == 0, high, jnp.where(row == 1, middle, jnp.where(row == 2, low, 0.0)))
                label = jnp.broadcast_to(label_ref[level : level + 1], (cols, width))
                chosen = jnp.where(label == zone + b * cols, 1.0, 0.0).astype(bf16)
                total += lax.dot_general(terms.astype(bf16), chosen, contract, preferred_element_type=f32)
            out_ref[blocks + b : blocks + b + 1] = jnp.sum(total, axis=0, keepdims=True)

    grad = lax.dot_general(force_ref[...], sens_ref[0], contract, preferred_element_type=f32)
    part = lax.broadcasted_iota(jnp.int32, grad.shape, 0)
    grad = jnp.sum(jnp.where(part == step, grad, 0.0), axis=0, keepdims=True)
    block = lax.broadcasted_iota(jnp.int32, (blocks, cols), 0)
    out_ref[:blocks] += jnp.where(block == me[0], jnp.broadcast_to(grad, (blocks, cols)), 0.0)


def small_sums(sensitivity, residual_force, zone_label, misfit, me, n_col):
    _, cols, nodes = sensitivity.shape
    layers, plane = zone_label.shape
    width = plane // n_col
    return pl.pallas_call(
        functools.partial(sums_kernel, n_col),
        grid_spec=pltpu.PrefetchScalarGridSpec(
            num_scalar_prefetch=1,
            grid=(3,),
            in_specs=[
                pl.BlockSpec((1, cols, nodes), lambda i, t: (i, 0, 0)),
                pl.BlockSpec((3, nodes), lambda i, t: (0, 0)),
                pl.BlockSpec((layers, width), lambda i, t: (0, t[0])),
                pl.BlockSpec((layers, width), lambda i, t: (0, t[0])),
            ],
            out_specs=pl.BlockSpec((2 * n_col, cols), lambda i, t: (0, 0)),
        ),
        out_shape=jax.ShapeDtypeStruct((2 * n_col, cols), jnp.float32),
        compiler_params=pltpu.CompilerParams(vmem_limit_bytes=8 << 20),
        cost_estimate=pl.CostEstimate(flops=0, bytes_accessed=12 << 20, transcendentals=0),
        name="sums",
    )(me, sensitivity, residual_force, zone_label, misfit)


def on_device(sensitivity, residual_force, moments, zone_label, misfit):
    cols = sensitivity.shape[1]
    layers = moments.shape[1]
    plane = GX * GY
    n_slab = lax.axis_size("slab")
    n_col = lax.axis_size("col")
    assert n_slab == 2 * n_col
    width = cols * n_col
    me = lax.axis_index("col").astype(jnp.int32)
    slab = lax.axis_index("slab").astype(jnp.int32)
    core, level_z = slab % 2, slab // 2

    source = pltpu.with_memory_space_constraint(sensitivity, pltpu.HBM)
    bottom = 3 * (plane // n_col) + EDGE
    last = n_col - 1
    order = sorted(range(1, n_col), key=lambda k: (k.bit_count(), -k))
    single = [k for k in order if k.bit_count() == 1]
    double = [k for k in order if k.bit_count() > 1] + [0]
    place = jnp.stack([me, core, me ^ level_z])
    pieces, before, blocks, seen = {}, [], [], []
    for labels in (single, double):
        packed, place = pack(source, place, labels, [1 if k == 0 else layers // 2 if k == last else 0 for k in labels], layers, plane, n_col)
        for k, piece in zip(labels, packed):
            pieces[k] = [exchange(x, "col", k) for x in piece] if k else piece
    small = small_sums(source, residual_force, zone_label, misfit, place, n_col)
    matrix = build(moments, place, plane // n_col, small)
    for k in (0, *order):
        low = crop(pieces[k][0], bottom, blocks[1 if k == last else 0]) if k else pieces[k][0]
        top = shifted(low, "slab", -1)
        out = image_piece(k, tuple(seen), pieces[k], top, matrix, before, blocks, small, place, n_col)
        seen.append(k)
        if len(seen) < n_col:
            before.append(out[:2])
            blocks.append(out[2])
    keep, send = out

    mine = keep + exchange(send, "slab", 1)
    parts = [mine[:, k * cols : (k + 1) * cols] for k in range(n_col)]
    mine = parts[0]
    for k in range(1, n_col):
        mine = mine + exchange(parts[k], "col", k)
    half = cols // 2
    count = n_col
    while count > 1:
        count //= 2
        near, far, extra = mine[: count * half], mine[count * half : 2 * count * half], mine[2 * count * half :]
        mine = jnp.concatenate([near, extra]) + exchange(jnp.concatenate([far, extra]), "slab", 2 * count)
    hessian = mine[:half].T
    both = mine[half:].reshape(2, width)
    gradient = both[0]
    zone_misfit = both[1] * (width / (layers * plane * n_slab))
    return (hessian, gradient, zone_misfit)


def solution(mesh):
    in_specs = (
        P(None, "col", "slab"),
        P(None, "slab"),
        P(None, "slab", None),
        P("slab", None),
        P("slab", None),
    )
    out_specs = (P("col", "slab"), P(), P())
    return jax.shard_map(
        on_device, mesh=mesh, in_specs=in_specs, out_specs=out_specs, check_vma=False
    )
```

time: 111 us -> 74.7 us (0.67)
  local copies, waits for them, and re-layouts: 15.2 us -> 0.69 us
  waiting for transfers between devices: 32.6 us -> 18.2 us
  Pallas kernels: 36.7 us -> 32 us
  matrix products: 1.72 us -> 0 us
    ppermute x11 -> x10, waiting for transfers between devices: 32.6 us -> 18.2 us  [exchange(): return lax.ppermute(value, axis, [(i, i ^ by) for i in range(count)])]
    unnamed x28 -> x8, local copies, waits for them, and re-layouts: 14.3 us -> 0.02 us
    pallas_call x3, Pallas kernels: 1.93 us -> 0.05 us  [crop(): pl.pallas_call(crop_kernel, in_specs=[pl.BlockSpec(memory_space=pltpu.VME...]
    dot_general x2 -> x0, matrix products: 1.72 us -> none  [the longest x1 0.92 us: small_sums(): lax.dot_general(residual_force, sensitivity, (((0, 1), (0, 2)), ((), ()))...]
    pallas_call x4, Pallas kernels: 19.9 us -> 18.2 us  [image_piece(): pl.pallas_call(functools.partial(image_kernel, layers, width, len(piece),...]
    pallas_call x4 -> x3, Pallas kernels: 11.5 us -> 10.5 us  [the longest x2 6.34 us: pack(): pl.pallas_call(functools.partial(pack_kernel, layers, plane, n_col, label...]
    ppermute x11 -> x10, starting transfers between devices: 16.8 us -> 16.4 us  [exchange(): return lax.ppermute(value, axis, [(i, i ^ by) for i in range(count)])]
  transfers between devices with their start and end apart: 15 -> 14, of which waited for: 7 -> 9; matrix products, arithmetic and copies ran while one was open for 2% -> 0% of each run, Pallas kernels for 26% -> 31%
where the time goes in v3:
time: 74.7 us; the launch traced here: 74.4 us
  Pallas kernels  32 us (43%)
  starting transfers between devices  21.8 us (29%)
  waiting for transfers between devices  18.2 us (24%)
  between operations  0.82 us (1%)
  other arithmetic  0.81 us (1%)
    ppermute x10, waiting for transfers between devices, exchange(): return lax.ppermute(value, axis, [(i, i ^ by) for i in range(count)])  18.2 us
    pallas_call x4, Pallas kernels, image_piece(): pl.pallas_call(functools.partial(image_kernel, layers, width, len(piece),...  18.2 us
    ppermute x10, starting transfers between devices, exchange(): return lax.ppermute(value, axis, [(i, i ^ by) for i in range(count)])  16.4 us
    pallas_call x2, Pallas kernels, pack(): pl.pallas_call(functools.partial(pack_kernel, layers, plane, n_col, label...  6.34 us
    ppermute x4, starting transfers between devices, shifted(): return lax.ppermute(value, axis, pairs)  5.35 us
    pallas_call x1, Pallas kernels, small_sums(): pl.pallas_call(functools.partial(sums_kernel, n_col), grid_spec=pltpu.Pre...  4.17 us
    pallas_call x1, Pallas kernels, build(): pl.pallas_call(functools.partial(build_kernel, layers, width), grid_spec=...  3.31 us
  transfers between devices with their start and end apart: 14, of which 9 were waited for; matrix products, arithmetic and copies ran while one was open for 0% of the time, Pallas kernels for 31%

profile of v3, /device:TPU:0, one launch (start us, length us, event | category | flops | bytes accessed | tf_op | source)
XLA Modules:
  0.0 74.4 jit_solution(6146056849588991651)
XLA Ops:
  0.6 0.1 pad_add_fusion.me
  0.7 0.0 copy-start.1
  0.7 0.0 copy-start.2
  0.7 0.0 copy-start.3
  0.7 3.2 %pack.2 = (bf16[128,3328]{1,0:T(8,128)(2,1)S(1)}, bf16[128,3328]{1,0:T(8,128)(2,1)S(1)}, s32[3]{0:T(128)S(1)}) custom-call(s32[3]{0:T(128)S(1)} %pad_add_fusion.me, bf16[3,128,4096]{2,1,0:T(8,128)(2,1)} %sens_ref.5), custom_call_target="tpu_custom_call" | custom-call | bytes 6291456 | tf_op jit(solution)/shard_map/pack/pallas_call | solution.py:92
  3.9 3.0 %collective-permute-start.2 = (bf16[128,3328]{1,0:T(8,128)(2,1)S(1)}, bf16[128,3328]{1,0:T(8,128)(2,1)S(1)}, u32[]{:S(2)}, u32[]{:S(2)}) collective-permute-start(bf16[128,3328]{1,0:T(8,128)(2,1)S(1)} %get-tuple-element.28), channel_id=1, source_target_pairs={{0,2},{1,3},{2,0},{3,1},{4,6},{5,7},{6,4},{7,5},{8,10},{9,11},{10,... | collective-permute-start | bytes 2555912 | tf_op jit(solution)/shard_map/ppermute | solution.py:18
  6.9 1.5 %collective-permute-start.6 = (bf16[128,3328]{1,0:T(8,128)(2,1)S(1)}, bf16[128,3328]{1,0:T(8,128)(2,1)S(1)}, u32[]{:S(2)}, u32[]{:S(2)}) collective-permute-start(bf16[128,3328]{1,0:T(8,128)(2,1)S(1)} %get-tuple-element.41), channel_id=1, source_target_pairs={{0,1},{1,0},{2,3},{3,2},{4,5},{5,4},{6,7},{7,6},{8,9},{9,8},{10,11... | collective-permute-start | bytes 2555912 | tf_op jit(solution)/shard_map/ppermute | solution.py:18
  8.4 0.0 copy-start
  8.4 3.2 %pack.3 = (bf16[128,1792]{1,0:T(8,128)(2,1)S(1)}, bf16[128,1536]{1,0:T(8,128)(2,1)S(1)}, bf16[128,1024]{1,0:T(8,128)(2,1)S(1)}, bf16[128,2304]{1,0:T(8,128)(2,1)S(1)}, s32[3]{0:T(128)S(1)}) custom-call(s32[3]{0:T(128)S(1)} %get-tuple-element.25.me, bf16[3,128,4096]{2,1,0:T(8,128)(2,1)} %sens_ref.5), custom_call_target="tpu_custom_call" | custom-call | bytes 6291456 | tf_op jit(solution)/shard_map/pack/pallas_call | solution.py:92
  11.6 1.3 %collective-permute-start.3 = (bf16[128,1024]{1,0:T(8,128)(2,1)S(1)}, bf16[128,1024]{1,0:T(8,128)(2,1)S(1)}, u32[]{:S(2)}, u32[]{:S(2)}) collective-permute-start(bf16[128,1024]{1,0:T(8,128)(2,1)S(1)} %get-tuple-element.29.refs_0_), channel_id=1, source_target_pairs={{4,0},{8,4},{12,8},{16,12},{20,16},{24,20},{28,24},{5,1},{9,5},{13... | collective-permute-start | bytes 786440 | tf_op jit(solution)/shard_map/ppermute | solution.py:24
  12.9 0.1 collective-permute-start
  13.0 0.0 copy-done.1
  13.0 0.0 copy-done.2
  13.0 0.0 copy-done.3
  13.0 4.2 %sums.1.after_ref.refs_15_ = f32[8,128]{1,0:T(8,128)S(1)} custom-call(s32[3]{0:T(128)S(1)} %get-tuple-element.31.me._.refs_16_, bf16[3,128,4096]{2,1,0:T(8,128)(2,1)} %sens_ref.5, bf16[3,4096]{1,0:T(4,128)(2,1)S(1)} %copy-done.1, s32[4,1024]{1,0:T(4,128)S(1)} %copy-done.2, f32[4,1024]{1,0:T(4,128)S(1)} %copy-done.3), custom_call_target="tpu_custom_call" | custom-call | bytes 12582912 | tf_op jit(solution)/shard_map/sums/pallas_call | solution.py:410
  17.2 0.0 copy-done
  17.2 3.3 %build.1 = (bf16[2,16896,256]{2,1,0:T(8,128)(2,1)S(1)}, bf16[2,15,256,128]{3,2,1,0:T(8,128)(2,1)S(1)}, bf16[2,256,256]{2,1,0:T(8,128)(2,1)S(1)}) custom-call(s32[3]{0:T(128)S(1)} %get-tuple-element.31.me._.refs_16_, f32[6,4,1024]{2,1,0:T(4,128)S(1)} %copy-done, f32[8,128]{1,0:T(8,128)S(1)} %sums.1.after_ref.refs_15_), custom_call_target="tpu_custom_call" | custom-call | tf_op jit(solution)/shard_map/build/pallas_call | solution.py:243
  20.5 0.0 collective-permute-done.3.refs_2_
  20.5 3.8 %image.4 = (bf16[128,4096]{1,0:T(8,128)(2,1)S(1)}, bf16[128,4096]{1,0:T(8,128)(2,1)S(1)}, f32[1,128,128]{2,1,0:T(8,128)S(1)}) custom-call(bf16[128,1024]{1,0:T(8,128)(2,1)S(1)} %get-tuple-element.29.refs_0_, bf16[128,2304]{1,0:T(8,128)(2,1)S(1)} %get-tuple-element.30.refs_1_, bf16[128,1024]{1,0:T(8,128)(2,1)S(1)} %collective-permute-done.3.refs_2_, ...), custom_call_target="tpu_custom_call" | custom-call | bytes 16777216 | tf_op jit(solution)/shard_map/image/pallas_call | solution.py:361
  24.4 1.5 %collective-permute-done.2.piece_ref.refs_0_ = bf16[128,3328]{1,0:T(8,128)(2,1)S(1)} collective-permute-done((bf16[128,3328]{1,0:T(8,128)(2,1)S(1)}, bf16[128,3328]{1,0:T(8,128)(2,1)S(1)}, u32[]{:S(2)}, u32[]{:S(2)}) %collective-permute-start.2) | collective-permute-done | bytes 852000 | tf_op jit(solution)/shard_map/ppermute | solution.py:18
  25.9 1.3 %collective-permute-start.4 = (bf16[128,1024]{1,0:T(8,128)(2,1)S(1)}, bf16[128,1024]{1,0:T(8,128)(2,1)S(1)}, u32[]{:S(2)}, u32[]{:S(2)}) collective-permute-start(bf16[128,1024]{1,0:T(8,128)(2,1)S(1)} %crop.3), channel_id=1, source_target_pairs={{4,0},{8,4},{12,8},{16,12},{20,16},{24,20},{28,24},{5,1},{9,5},{13... | collective-permute-start | bytes 786440 | tf_op jit(solution)/shard_map/ppermute | solution.py:24
  27.2 3.0 %collective-permute-start.1 = (bf16[128,1536]{1,0:T(8,128)(2,1)S(1)}, bf16[128,1536]{1,0:T(8,128)(2,1)S(1)}, u32[]{:S(2)}, u32[]{:S(2)}) collective-permute-start(bf16[128,1536]{1,0:T(8,128)(2,1)S(1)} %get-tuple-element.27), channel_id=1, source_target_pairs={{0,3},{1,2},{2,1},{3,0},{4,7},{5,6},{6,5},{7,4},{8,11},{9,10},{10,... | collective-permute-start | bytes 1179656 | tf_op jit(solution)/shard_map/ppermute | solution.py:18
  30.2 0.0 collective-permute-done.6.piece_ref.refs_0_
  30.2 1.3 %collective-permute-start.7 = (bf16[128,1024]{1,0:T(8,128)(2,1)S(1)}, bf16[128,1024]{1,0:T(8,128)(2,1)S(1)}, u32[]{:S(2)}, u32[]{:S(2)}) collective-permute-start(bf16[128,1024]{1,0:T(8,128)(2,1)S(1)} %crop.5), channel_id=1, source_target_pairs={{4,0},{8,4},{12,8},{16,12},{20,16},{24,20},{28,24},{5,1},{9,5},{13... | collective-permute-start | bytes 786440 | tf_op jit(solution)/shard_map/ppermute | solution.py:24
  31.5 0.0 collective-permute-done.4.refs_1_
  31.6 4.1 %image.5 = (bf16[128,4096]{1,0:T(8,128)(2,1)S(1)}, bf16[128,4096]{1,0:T(8,128)(2,1)S(1)}, f32[2,128,128]{2,1,0:T(8,128)S(1)}) custom-call(bf16[128,3328]{1,0:T(8,128)(2,1)S(1)} %collective-permute-done.2.piece_ref.refs_0_, bf16[128,1024]{1,0:T(8,128)(2,1)S(1)} %collective-permute-done.4.refs_1_, ...), custom_call_target="tpu_custom_call" | custom-call | bytes 16777216 | tf_op jit(solution)/shard_map/image/pallas_call | solution.py:361
  35.6 2.5 %collective-permute-done.piece_ref.refs_0_ = bf16[128,1792]{1,0:T(8,128)(2,1)S(1)} collective-permute-done((bf16[128,1792]{1,0:T(8,128)(2,1)S(1)}, bf16[128,1792]{1,0:T(8,128)(2,1)S(1)}, u32[]{:S(2)}, u32[]{:S(2)}) %collective-permute-start) | collective-permute-done | bytes 458784 | tf_op jit(solution)/shard_map/ppermute | solution.py:18
  38.1 1.5 %collective-permute-start.5 = (bf16[128,1024]{1,0:T(8,128)(2,1)S(1)}, bf16[128,1024]{1,0:T(8,128)(2,1)S(1)}, u32[]{:S(2)}, u32[]{:S(2)}) collective-permute-start(bf16[128,1024]{1,0:T(8,128)(2,1)S(1)} %crop.4), channel_id=1, source_target_pairs={{4,0},{8,4},{12,8},{16,12},{20,16},{24,20},{28,24},{5,1},{9,5},{13... | collective-permute-start | bytes 786440 | tf_op jit(solution)/shard_map/ppermute | solution.py:24
  39.6 0.0 collective-permute-done.7.refs_1_
  39.6 4.6 %image.6 = (bf16[128,4096]{1,0:T(8,128)(2,1)S(1)}, bf16[128,4096]{1,0:T(8,128)(2,1)S(1)}, f32[3,128,128]{2,1,0:T(8,128)S(1)}) custom-call(bf16[128,3328]{1,0:T(8,128)(2,1)S(1)} %collective-permute-done.6.piece_ref.refs_0_, bf16[128,1024]{1,0:T(8,128)(2,1)S(1)} %collective-permute-done.7.refs_1_, ...), custom_call_target="tpu_custom_call" | custom-call | bytes 16777216 | tf_op jit(solution)/shard_map/image/pallas_call | solution.py:361
  44.3 1.1 %collective-permute-done.1.refs_1_ = bf16[128,1536]{1,0:T(8,128)(2,1)S(1)} collective-permute-done((bf16[128,1536]{1,0:T(8,128)(2,1)S(1)}, bf16[128,1536]{1,0:T(8,128)(2,1)S(1)}, u32[]{:S(2)}, u32[]{:S(2)}) %collective-permute-start.1) | collective-permute-done | bytes 393248 | tf_op jit(solution)/shard_map/ppermute | solution.py:18
  45.4 0.0 collective-permute-done.5.refs_2_
  45.4 5.7 %image.7 = (f32[264,512]{1,0:T(8,128)S(1)}, f32[264,512]{1,0:T(8,128)S(1)}) custom-call(bf16[128,1792]{1,0:T(8,128)(2,1)S(1)} %collective-permute-done.piece_ref.refs_0_, bf16[128,1536]{1,0:T(8,128)(2,1)S(1)} %collective-permute-done.1.refs_1_, bf16[128,1024]{1,0:T(8,128)(2,1)S(1)} %collective-permute-done.5.refs_2_, ...), custom_call_target="tpu_custom_call" | custom-call | bytes 16777216 | tf_op jit(solution)/shard_map/image/pallas_call | solution.py:361
  51.1 0.9 %collective-permute-start.8 = (f32[264,512]{1,0:T(8,128)S(1)}, f32[264,512]{1,0:T(8,128)S(1)}, u32[]{:S(2)}, u32[]{:S(2)}) collective-permute-start(f32[264,512]{1,0:T(8,128)S(1)} %get-tuple-element.46), channel_id=1, source_target_pairs={{0,4},{4,0},{8,12},{12,8},{16,20},{20,16},{24,28},{28,24},{1,5},{5... | collective-permute-start | bytes 1622024 | tf_op jit(solution)/shard_map/ppermute | solution.py:18
  52.0 1.6 %collective-permute-done.8 = f32[264,512]{1,0:T(8,128)S(1)} collective-permute-done((f32[264,512]{1,0:T(8,128)S(1)}, f32[264,512]{1,0:T(8,128)S(1)}, u32[]{:S(2)}, u32[]{:S(2)}) %collective-permute-start.8) | collective-permute-done | bytes 540704 | tf_op jit(solution)/shard_map/ppermute | solution.py:18
  53.6 0.1 add.24
  53.7 1.6 %collective-permute-start.10 = (f32[264,128]{1,0:T(8,128)S(1)}, f32[264,128]{1,0:T(8,128)S(1)}, u32[]{:S(2)}, u32[]{:S(2)}) collective-permute-start(f32[264,128]{1,0:T(8,128)S(1)} %get-tuple-element.49), channel_id=1, source_target_pairs={{0,2},{1,3},{2,0},{3,1},{4,6},{5,7},{6,4},{7,5},{8,10},{9,11},{10,... | collective-permute-start | bytes 405512 | tf_op jit(solution)/shard_map/ppermute | solution.py:18
  55.3 1.4 %collective-permute-start.11 = (f32[264,128]{1,0:T(8,128)S(1)}, f32[264,128]{1,0:T(8,128)S(1)}, u32[]{:S(2)}, u32[]{:S(2)}) collective-permute-start(f32[264,128]{1,0:T(8,128)S(1)} %get-tuple-element.48), channel_id=1, source_target_pairs={{0,3},{1,2},{2,1},{3,0},{4,7},{5,6},{6,5},{7,4},{8,11},{9,10},{10,... | collective-permute-start | bytes 405512 | tf_op jit(solution)/shard_map/ppermute | solution.py:18
  56.7 0.5 collective-permute-start.9
  57.2 5.1 %collective-permute-done.10 = f32[264,128]{1,0:T(8,128)S(1)} collective-permute-done((f32[264,128]{1,0:T(8,128)S(1)}, f32[264,128]{1,0:T(8,128)S(1)}, u32[]{:S(2)}, u32[]{:S(2)}) %collective-permute-start.10) | collective-permute-done | bytes 135200 | tf_op jit(solution)/shard_map/ppermute | solution.py:18
  62.3 0.3 collective-permute-done.11
  62.7 1.1 %collective-permute-done.9 = f32[264,128]{1,0:T(8,128)S(1)} collective-permute-done((f32[264,128]{1,0:T(8,128)S(1)}, f32[264,128]{1,0:T(8,128)S(1)}, u32[]{:S(2)}, u32[]{:S(2)}) %collective-permute-start.9) | collective-permute-done | bytes 135200 | tf_op jit(solution)/shard_map/ppermute | solution.py:18
  63.8 2.7 %collective-permute-start.12 = (f32[136,128]{1,0:T(8,128)S(1)}, f32[136,128]{1,0:T(8,128)S(1)}, u32[]{:S(2)}, u32[]{:S(2)}) collective-permute-start(f32[136,128]{1,0:T(8,128)S(1)} %concatenate.16), channel_id=1, source_target_pairs={{0,16},{4,20},{8,24},{12,28},{16,0},{20,4},{24,8},{28,12},{1,17},{... | collective-permute-start | bytes 208904 | tf_op jit(solution)/shard_map/ppermute | solution.py:18
  66.5 2.6 %collective-permute-done.12 = f32[136,128]{1,0:T(8,128)S(1)} collective-permute-done((f32[136,128]{1,0:T(8,128)S(1)}, f32[136,128]{1,0:T(8,128)S(1)}, u32[]{:S(2)}, u32[]{:S(2)}) %collective-permute-start.12) | collective-permute-done | bytes 69664 | tf_op jit(solution)/shard_map/ppermute | solution.py:18
  69.1 1.6 %collective-permute-start.13 = (f32[72,128]{1,0:T(8,128)S(1)}, f32[72,128]{1,0:T(8,128)S(1)}, u32[]{:S(2)}, u32[]{:S(2)}) collective-permute-start(f32[72,128]{1,0:T(8,128)S(1)} %concatenate.17), channel_id=1, source_target_pairs={{0,8},{4,12},{8,0},{12,4},{16,24},{20,28},{24,16},{28,20},{1,9},{5... | collective-permute-start | bytes 110600 | tf_op jit(solution)/shard_map/ppermute | solution.py:18
  70.7 2.4 %collective-permute-done.13 = f32[72,128]{1,0:T(8,128)S(1)} collective-permute-done((f32[72,128]{1,0:T(8,128)S(1)}, f32[72,128]{1,0:T(8,128)S(1)}, u32[]{:S(2)}, u32[]{:S(2)}) %collective-permute-start.13) | collective-permute-done | bytes 36896 | tf_op jit(solution)/shard_map/ppermute | solution.py:18
  73.2 0.6 slice_bitcast_fusion
  73.8 0.6 fusion.2
  (13 shorter events, 0.2 us)
Async XLA Ops:
  0.7 12.3 %copy-start.1 = (bf16[3,4096]{1,0:T(4,128)(2,1)S(1)}, bf16[3,4096]{1,0:T(4,128)(2,1)}, u32[]{:S(2)}) copy-start(bf16[3,4096]{1,0:T(4,128)(2,1)} %force_ref.1) | copy-start | bytes 73732
  0.7 12.3 %copy-start.2 = (s32[4,1024]{1,0:T(4,128)S(1)}, s32[4,1024]{1,0:T(4,128)}, u32[]{:S(2)}) copy-start(s32[4,1024]{1,0:T(4,128)} %label_ref.1) | copy-start | bytes 49156
  0.7 12.3 %copy-start.3 = (f32[4,1024]{1,0:T(4,128)S(1)}, f32[4,1024]{1,0:T(4,128)}, u32[]{:S(2)}) copy-start(f32[4,1024]{1,0:T(4,128)} %misfit_ref.1) | copy-start | bytes 49156
  3.9 22.0 %collective-permute-start.2 = (bf16[128,3328]{1,0:T(8,128)(2,1)S(1)}, bf16[128,3328]{1,0:T(8,128)(2,1)S(1)}, u32[]{:S(2)}, u32[]{:S(2)}) collective-permute-start(bf16[128,3328]{1,0:T(8,128)(2,1)S(1)} %get-tuple-element.28), channel_id=1, source_target_pairs={{0,2},{1,3},{2,0},{3,1},{4,6},{5,7},{6,4},{7,5},{8,10},{9,11},{10,... | collective-permute-start | bytes 2555912 | tf_op jit(solution)/shard_map/ppermute | solution.py:18
  6.9 23.3 %collective-permute-start.6 = (bf16[128,3328]{1,0:T(8,128)(2,1)S(1)}, bf16[128,3328]{1,0:T(8,128)(2,1)S(1)}, u32[]{:S(2)}, u32[]{:S(2)}) collective-permute-start(bf16[128,3328]{1,0:T(8,128)(2,1)S(1)} %get-tuple-element.41), channel_id=1, source_target_pairs={{0,1},{1,0},{2,3},{3,2},{4,5},{5,4},{6,7},{7,6},{8,9},{9,8},{10,11... | collective-permute-start | bytes 2555912 | tf_op jit(solution)/shard_map/ppermute | solution.py:18
  8.4 8.8 %copy-start = (f32[6,4,1024]{2,1,0:T(4,128)S(1)}, f32[6,4,1024]{2,1,0:T(4,128)}, u32[]{:S(2)}) copy-start(f32[6,4,1024]{2,1,0:T(4,128)} %moments_ref.1) | copy-start | bytes 294916
  11.6 8.9 %collective-permute-start.3 = (bf16[128,1024]{1,0:T(8,128)(2,1)S(1)}, bf16[128,1024]{1,0:T(8,128)(2,1)S(1)}, u32[]{:S(2)}, u32[]{:S(2)}) collective-permute-start(bf16[128,1024]{1,0:T(8,128)(2,1)S(1)} %get-tuple-element.29.refs_0_), channel_id=1, source_target_pairs={{4,0},{8,4},{12,8},{16,12},{20,16},{24,20},{28,24},{5,1},{9,5},{13... | collective-permute-start | bytes 786440 | tf_op jit(solution)/shard_map/ppermute | solution.py:24
  12.9 25.2 %collective-permute-start = (bf16[128,1792]{1,0:T(8,128)(2,1)S(1)}, bf16[128,1792]{1,0:T(8,128)(2,1)S(1)}, u32[]{:S(2)}, u32[]{:S(2)}) collective-permute-start(bf16[128,1792]{1,0:T(8,128)(2,1)S(1)} %get-tuple-element.26), channel_id=1, source_target_pairs={{0,3},{1,2},{2,1},{3,0},{4,7},{5,6},{6,5},{7,4},{8,11},{9,10},{10,... | collective-permute-start | bytes 1376264 | tf_op jit(solution)/shard_map/ppermute | solution.py:18
  25.9 5.6 %collective-permute-start.4 = (bf16[128,1024]{1,0:T(8,128)(2,1)S(1)}, bf16[128,1024]{1,0:T(8,128)(2,1)S(1)}, u32[]{:S(2)}, u32[]{:S(2)}) collective-permute-start(bf16[128,1024]{1,0:T(8,128)(2,1)S(1)} %crop.3), channel_id=1, source_target_pairs={{4,0},{8,4},{12,8},{16,12},{20,16},{24,20},{28,24},{5,1},{9,5},{13... | collective-permute-start | bytes 786440 | tf_op jit(solution)/shard_map/ppermute | solution.py:24
  27.2 18.2 %collective-permute-start.1 = (bf16[128,1536]{1,0:T(8,128)(2,1)S(1)}, bf16[128,1536]{1,0:T(8,128)(2,1)S(1)}, u32[]{:S(2)}, u32[]{:S(2)}) collective-permute-start(bf16[128,1536]{1,0:T(8,128)(2,1)S(1)} %get-tuple-element.27), channel_id=1, source_target_pairs={{0,3},{1,2},{2,1},{3,0},{4,7},{5,6},{6,5},{7,4},{8,11},{9,10},{10,... | collective-permute-start | bytes 1179656 | tf_op jit(solution)/shard_map/ppermute | solution.py:18
  30.2 9.4 %collective-permute-start.7 = (bf16[128,1024]{1,0:T(8,128)(2,1)S(1)}, bf16[128,1024]{1,0:T(8,128)(2,1)S(1)}, u32[]{:S(2)}, u32[]{:S(2)}) collective-permute-start(bf16[128,1024]{1,0:T(8,128)(2,1)S(1)} %crop.5), channel_id=1, source_target_pairs={{4,0},{8,4},{12,8},{16,12},{20,16},{24,20},{28,24},{5,1},{9,5},{13... | collective-permute-start | bytes 786440 | tf_op jit(solution)/shard_map/ppermute | solution.py:24
  38.1 7.3 %collective-permute-start.5 = (bf16[128,1024]{1,0:T(8,128)(2,1)S(1)}, bf16[128,1024]{1,0:T(8,128)(2,1)S(1)}, u32[]{:S(2)}, u32[]{:S(2)}) collective-permute-start(bf16[128,1024]{1,0:T(8,128)(2,1)S(1)} %crop.4), channel_id=1, source_target_pairs={{4,0},{8,4},{12,8},{16,12},{20,16},{24,20},{28,24},{5,1},{9,5},{13... | collective-permute-start | bytes 786440 | tf_op jit(solution)/shard_map/ppermute | solution.py:24
  51.1 2.5 %collective-permute-start.8 = (f32[264,512]{1,0:T(8,128)S(1)}, f32[264,512]{1,0:T(8,128)S(1)}, u32[]{:S(2)}, u32[]{:S(2)}) collective-permute-start(f32[264,512]{1,0:T(8,128)S(1)} %get-tuple-element.46), channel_id=1, source_target_pairs={{0,4},{4,0},{8,12},{12,8},{16,20},{20,16},{24,28},{28,24},{1,5},{5... | collective-permute-start | bytes 1622024 | tf_op jit(solution)/shard_map/ppermute | solution.py:18
  53.7 8.7 %collective-permute-start.10 = (f32[264,128]{1,0:T(8,128)S(1)}, f32[264,128]{1,0:T(8,128)S(1)}, u32[]{:S(2)}, u32[]{:S(2)}) collective-permute-start(f32[264,128]{1,0:T(8,128)S(1)} %get-tuple-element.49), channel_id=1, source_target_pairs={{0,2},{1,3},{2,0},{3,1},{4,6},{5,7},{6,4},{7,5},{8,10},{9,11},{10,... | collective-permute-start | bytes 405512 | tf_op jit(solution)/shard_map/ppermute | solution.py:18
  55.3 7.4 %collective-permute-start.11 = (f32[264,128]{1,0:T(8,128)S(1)}, f32[264,128]{1,0:T(8,128)S(1)}, u32[]{:S(2)}, u32[]{:S(2)}) collective-permute-start(f32[264,128]{1,0:T(8,128)S(1)} %get-tuple-element.48), channel_id=1, source_target_pairs={{0,3},{1,2},{2,1},{3,0},{4,7},{5,6},{6,5},{7,4},{8,11},{9,10},{10,... | collective-permute-start | bytes 405512 | tf_op jit(solution)/shard_map/ppermute | solution.py:18
  56.7 7.0 %collective-permute-start.9 = (f32[264,128]{1,0:T(8,128)S(1)}, f32[264,128]{1,0:T(8,128)S(1)}, u32[]{:S(2)}, u32[]{:S(2)}) collective-permute-start(f32[264,128]{1,0:T(8,128)S(1)} %get-tuple-element.47), channel_id=1, source_target_pairs={{0,1},{1,0},{2,3},{3,2},{4,5},{5,4},{6,7},{7,6},{8,9},{9,8},{10,11... | collective-permute-start | bytes 405512 | tf_op jit(solution)/shard_map/ppermute | solution.py:18
  63.8 5.3 %collective-permute-start.12 = (f32[136,128]{1,0:T(8,128)S(1)}, f32[136,128]{1,0:T(8,128)S(1)}, u32[]{:S(2)}, u32[]{:S(2)}) collective-permute-start(f32[136,128]{1,0:T(8,128)S(1)} %concatenate.16), channel_id=1, source_target_pairs={{0,16},{4,20},{8,24},{12,28},{16,0},{20,4},{24,8},{28,12},{1,17},{... | collective-permute-start | bytes 208904 | tf_op jit(solution)/shard_map/ppermute | solution.py:18
  69.1 4.0 %collective-permute-start.13 = (f32[72,128]{1,0:T(8,128)S(1)}, f32[72,128]{1,0:T(8,128)S(1)}, u32[]{:S(2)}, u32[]{:S(2)}) collective-permute-start(f32[72,128]{1,0:T(8,128)S(1)} %concatenate.17), channel_id=1, source_target_pairs={{0,8},{4,12},{8,0},{12,4},{16,24},{20,28},{24,16},{28,20},{1,9},{5... | collective-permute-start | bytes 110600 | tf_op jit(solution)/shard_map/ppermute | solution.py:18

commit v4 on v2

v4 whole, which is shorter than its diff:
```python
import functools

import jax
import jax.numpy as jnp
from jax import lax
from jax.experimental import pallas as pl
from jax.experimental.pallas import tpu as pltpu
from jax.sharding import PartitionSpec as P

GX = 64
GY = 16
TILE = 128
EDGE = 256


def exchange(value, axis, by):
    count = lax.axis_size(axis)
    return lax.ppermute(value, axis, [(i, i ^ by) for i in range(count)])


def shifted(value, axis, by):
    count = lax.axis_size(axis)
    pairs = [(i, i + by) for i in range(count) if 0 <= i + by < count]
    return lax.ppermute(value, axis, pairs)


def lane_of(shape):
    return lax.broadcasted_iota(jnp.int32, shape, 1)


def pack_kernel(layers, plane, n_col, specs, after, sens_ref, *refs):
    outs, (planes, sems) = refs[:-2], refs[-2:]
    col, slab = lax.axis_index("col"), lax.axis_index("slab")
    outs = list(outs)
    next_ref = outs.pop()
    outs = outs[after:]
    width = plane // n_col
    for i, value in enumerate((col, slab % 2, col ^ (slab // 2))):
        next_ref[i] = value
    inner, both = slice(0, width), slice(0, width + TILE)
    slots, waits = {}, {}
    for label in dict.fromkeys(spec[0] for spec in specs):
        spans = [levels for name, levels, _ in specs if name == label]
        edges = any(levels[0] == 0 for levels in spans)
        for level in range(layers):
            held = any(level in levels for levels in spans)
            if not (held or edges):
                continue
            target = col ^ label
            slot = slots[label, level] = len(slots)
            start = pl.multiple_of((level * n_col + target) * width, width)

            def copy(part, start=start, slot=slot):
                source = sens_ref.at[:, :, pl.ds(start + part.start, part.stop - part.start)]
                return pltpu.make_async_copy(source, planes.at[slot, :, :, part], sems.at[slot])

            inside = target != n_col - 1
            if not edges:
                cases = [(None, inner)]
            elif held:
                cases = [(inside, both), (jnp.logical_not(inside), inner)]
            else:
                cases = [(inside, slice(width, width + TILE))]
            for case, part in cases:
                if case is None:
                    copy(part).start()
                else:
                    pl.when(case)(copy(part).start)
            waits[label, level] = [(case, copy(part)) for case, part in cases]
    dtype = sens_ref.dtype
    for array, (label, levels, rows) in zip(outs, specs):
        lane = lane_of((rows[1] - rows[0], TILE))
        halo = [jnp.zeros(lane.shape, jnp.float32)] * (EDGE // TILE)
        start = 0
        for level in range(layers):
            if level not in levels and levels[0]:
                continue
            for case, copy in waits.pop((label, level), ()):
                if case is None:
                    copy.wait()
                else:
                    pl.when(case)(copy.wait)
            for k in range(3):
                piece = planes.at[slots[label, level], k, rows[0] : rows[1]]
                if level in levels:
                    array[:, start : start + width] = piece[:, inner]
                    start += width
                if levels[0] == 0:
                    tile, at = divmod(edge_at(k, level, layers), TILE)
                    edge = piece[:, width:].astype(jnp.float32)
                    edge = pltpu.roll(edge, at, 1) if at else edge
                    keep = (lane >= at) & (lane < at + GY) & ((col ^ label) != n_col - 1)
                    halo[tile] = jnp.where(keep, edge, halo[tile])
            if level == 0:
                start += EDGE
        if levels[0] == 0:
            for tile, value in enumerate(halo):
                begin = 3 * width + tile * TILE
                array[:, begin : begin + TILE] = value.astype(dtype)


def edge_at(k, level, layers):
    return (k * (layers + 1) + level) * GY


def pack(sensitivity, after, specs, layers, plane, n_col):
    cols, dtype = sensitivity.shape[1], sensitivity.dtype
    width = plane // n_col
    outs, slots = [], set()
    for label, levels, rows in specs:
        size = 3 * len(levels) * width + (0 if levels[0] else EDGE)
        outs.append(jax.ShapeDtypeStruct((rows[1] - rows[0], size), dtype))
        slots |= {(label, level) for level in (levels if levels[0] else range(layers))}
    *found, place = pl.pallas_call(
        functools.partial(pack_kernel, layers, plane, n_col, specs, len(after)),
        in_specs=[pl.BlockSpec(memory_space=pltpu.HBM)] + [pl.BlockSpec(memory_space=pltpu.SMEM)] * len(after),
        out_specs=[pl.BlockSpec(memory_space=pltpu.VMEM)] * len(outs) + [pl.BlockSpec(memory_space=pltpu.SMEM)],
        out_shape=[*outs, jax.ShapeDtypeStruct((3,), jnp.int32)],
        scratch_shapes=[
            pltpu.VMEM((len(slots), 3, cols, width + TILE), dtype),
            pltpu.SemaphoreType.DMA((len(slots),)),
        ],
        compiler_params=pltpu.CompilerParams(vmem_limit_bytes=8 << 20),
        cost_estimate=pl.CostEstimate(flops=0, bytes_accessed=4 << 20, transcendentals=0),
        name="pack",
    )(sensitivity, *after)
    return found, place


def crop_kernel(piece_ref, _, out_ref):
    out_ref[...] = piece_ref[:, : out_ref.shape[1]]


def crop(piece, size, after):
    return pl.pallas_call(
        crop_kernel,
        in_specs=[pl.BlockSpec(memory_space=pltpu.VMEM), pl.BlockSpec(memory_space=pl.ANY)],
        out_specs=pl.BlockSpec(memory_space=pltpu.VMEM),
        out_shape=jax.ShapeDtypeStruct((piece.shape[0], size), piece.dtype),
        compiler_params=pltpu.CompilerParams(vmem_limit_bytes=8 << 20),
        cost_estimate=pl.CostEstimate(flops=0, bytes_accessed=0, transcendentals=0),
        name="crop",
    )(piece, after)


def component(a, b):
    a, b = min(a, b), max(a, b)
    return a if a == b else a + b + 2


def tile_start(z, k, side, other, layers):
    base = 15 * z + ((0, 6, 11)[k] if z < layers else (0, 3, 5)[k])
    return base + (other - k if side == 0 else 3 - k + other)


def zone_sums(label_ref, misfit_ref, zone_ref):
    f32, bf16 = jnp.float32, jnp.bfloat16
    layers, width = label_ref.shape
    blocks, cols = zone_ref.shape
    row = lax.broadcasted_iota(jnp.int32, (8, width), 0)
    zone = lax.broadcasted_iota(jnp.int32, (cols, width), 0)
    for b in range(blocks):
        total = jnp.zeros((8, cols), f32)
        for level in range(layers):
            value = jnp.broadcast_to(misfit_ref[level : level + 1], (8, width))
            high = value.astype(bf16).astype(f32)
            middle = (value - high).astype(bf16).astype(f32)
            low = value - high - middle
            terms = jnp.where(row == 0, high, jnp.where(row == 1, middle, jnp.where(row == 2, low, 0.0)))
            label = jnp.broadcast_to(label_ref[level : level + 1], (cols, width))
            chosen = jnp.where(label == zone + b * cols, 1.0, 0.0).astype(bf16)
            total += lax.dot_general(
                terms.astype(bf16), chosen, (((1,), (1,)), ((), ())), preferred_element_type=f32
            )
        zone_ref[b : b + 1] = jnp.sum(total, axis=0, keepdims=True)


def build_kernel(layers, width, place, moments_ref, label_ref, misfit_ref, *refs):
    force_refs, refs = refs[:layers], refs[layers:]
    plane_ref, edge_ref, corner_ref, force_ref, zone_ref, field_ref, ahead_ref = refs
    f32, bf16 = jnp.float32, jnp.bfloat16
    force_ref[...] = jnp.zeros_like(force_ref)
    for z in range(layers):
        for k in range(3):
            value = force_refs[z][k : k + 1].astype(f32)
            start = (3 * z + k) * width
            force_ref[:, start : start + width] = jnp.broadcast_to(value, (16, width)).astype(bf16)
    zone_sums(label_ref, misfit_ref, zone_ref)
    shape = (GY, width)
    lane = lane_of(shape)
    row = lax.broadcasted_iota(jnp.int32, shape, 0)
    pos_x, pos_y = lane // GY, lane % GY
    same, up, down = row == pos_y, row == pos_y + 1, row == pos_y - 1
    zero = jnp.zeros(shape, f32)
    field_lane = lane_of((8, width))
    columns = width // GY
    near = [pos_x % 3 == r for r in range(3)]
    follow = [(pos_x + 1) % 3 == r for r in range(3)]
    band = [jnp.where((pos_x >= x - 1) & (pos_x <= x + 1), 1.0, 0.0).astype(bf16) for x in range(columns)]
    tile_lane = lane_of((GY, TILE))

    def spread(middle, ahead, behind):
        def whole(value):
            return jnp.broadcast_to(value, shape)

        return jnp.where(same, whole(middle), jnp.where(up, whole(ahead), jnp.where(down, whole(behind), zero)))

    def two_terms(value):
        hi = value.astype(bf16)
        return hi, (value - hi.astype(f32)).astype(bf16)

    edge_ref[...] = jnp.zeros_like(edge_ref)
    field_ref[...] = jnp.zeros_like(field_ref)
    for z in range(layers + 1):
        whole = None
        for level in (z, z - 1):
            if 0 <= level < layers:
                part = moments_ref[:, level, :] * (2.0 / 216.0)
                whole = part if whole is None else whole + part
        field_ref[2 * z, :6] = whole
        if z < layers:
            field_ref[2 * z + 1, :6] = moments_ref[:, z, :] * (1.0 / 216.0)

    for pair in range(2 * layers + 1):
        z, side = divmod(pair, 2)
        element = field_ref[pair]
        before = jnp.where(field_lane >= GY, pltpu.roll(element, GY, 1), 0.0)
        parts = []
        for value in (2.0 * (element + before), element, before):
            lower = jnp.where(field_lane % GY != 0, pltpu.roll(value, 1, 1), 0.0)
            parts.append((2.0 * (value + lower), value, lower))
        for c in range(6):
            here, ahead, behind = [spread(*(v[c : c + 1] for v in part)) for part in parts]
            ahead_ref[pair, c] = ahead[:, width - TILE :]
            scale = 0.5 if side == 0 and c < 3 else None
            spots = []
            for k in range(3):
                for other in range(3):
                    if component(k, other) == c and (side == 1 or other >= k):
                        spots.append(tile_start(z, k, side, other, layers))
            for r in range(3):
                value = jnp.where(near[r], here, jnp.where(follow[r], ahead, behind))
                if scale is not None:
                    value = value * scale
                for term, piece in enumerate(two_terms(value)):
                    for x in range(r, columns, 3):
                        block = piece * band[x]
                        for spot in spots:
                            start = spot * width + x * GY
                            plane_ref[term, start : start + GY, :] = block

    edge_lane = tile_lane // GY == TILE // GY - 1
    for z in range(layers + 1):
        for other_z in range(max(z - 1, 0), min(z + 1, layers) + 1):
            pair = 2 * z if other_z == z else 2 * min(z, other_z) + 1
            for c in range(6):
                value = jnp.where(edge_lane, ahead_ref[pair, c], 0.0)
                for term, piece in enumerate(two_terms(value)):
                    for k in range(3):
                        for other in range(3):
                            if component(k, other) == c:
                                start = edge_at(other, other_z, layers)
                                n, at = divmod(3 * z + k, 2)
                                edge_ref[term, n, start : start + GY, at * TILE : (at + 1) * TILE] = piece

    corner_ref[...] = jnp.zeros_like(corner_ref)
    for other_z in range(layers + 1):
        for other in range(3):
            tiles = [jnp.zeros((GY, TILE), f32)] * (EDGE // TILE)
            for z in range(max(other_z - 1, 0), min(other_z + 1, layers) + 1):
                pair = 2 * z if other_z == z else 2 * min(z, other_z) + 1
                for k in range(3):
                    tile, at = divmod(edge_at(k, z, layers), TILE)
                    value = ahead_ref[pair, component(k, other)]
                    turn = (at + GY) % TILE
                    value = pltpu.roll(value, turn, 1) if turn else value
                    tiles[tile] = jnp.where(tile_lane // GY == at // GY, value, tiles[tile])
            start = edge_at(other, other_z, layers)
            for tile, value in enumerate(tiles):
                for term, piece in enumerate(two_terms(value)):
                    corner_ref[term, start : start + GY, tile * TILE : (tile + 1) * TILE] = piece


def in_vmem(x):
    return pltpu.with_memory_space_constraint(x, pltpu.VMEM)


def build(moments, zone_label, misfit, residual_force, place, n_col, cols):
    layers, plane = zone_label.shape
    width = plane // n_col
    shapes = [
        ((2, (15 * layers + 6) * width, width), jnp.bfloat16),
        ((2, (3 * layers + 4) // 2, EDGE, 2 * TILE), jnp.bfloat16),
        ((2, EDGE, EDGE), jnp.bfloat16),
        ((16, 3 * (layers + 1) * width + EDGE), jnp.bfloat16),
        ((n_col, cols), jnp.float32),
    ]

    def force_spec(level):
        return pl.BlockSpec((3, width), lambda i, t: (0, level * n_col + t[0]))

    out = pl.pallas_call(
        functools.partial(build_kernel, layers, width),
        grid_spec=pltpu.PrefetchScalarGridSpec(
            num_scalar_prefetch=1,
            grid=(1,),
            in_specs=[
                pl.BlockSpec((6, layers, width), lambda i, t: (0, 0, t[0])),
                pl.BlockSpec((layers, width), lambda i, t: (0, t[0])),
                pl.BlockSpec((layers, width), lambda i, t: (0, t[0])),
            ]
            + [force_spec(level) for level in range(layers)],
            out_specs=[pl.BlockSpec(memory_space=pltpu.VMEM)] * len(shapes),
            scratch_shapes=[
                pltpu.VMEM((2 * layers + 1, 8, width), jnp.float32),
                pltpu.VMEM((2 * layers + 1, 6, GY, TILE), jnp.float32),
            ],
        ),
        out_shape=[pltpu.VMEM(*shape) for shape in shapes],
        compiler_params=pltpu.CompilerParams(vmem_limit_bytes=8 << 20),
        cost_estimate=pl.CostEstimate(flops=0, bytes_accessed=12 << 20, transcendentals=0),
        name="build",
    )(place, moments, zone_label, misfit, *([residual_force] * layers))
    return [in_vmem(x) for x in out]


def image_layers(layers, width, values_ref, image_ref, matrix):
    plane_ref, edge_ref, corner_ref = matrix
    f32, bf16 = jnp.float32, jnp.bfloat16
    depth = 3 * (layers + 1) * width
    halo = values_ref[:, depth:]

    def dot(a, b):
        return jnp.dot(a, b, preferred_element_type=f32)

    edges = []
    for n in range(edge_ref.shape[1]):
        both = dot(halo, edge_ref[0, n]) + dot(halo, edge_ref[1, n])
        edges += [both[:, :TILE], both[:, TILE:]]
    for z in range(layers + 1):
        for k in range(3):
            lo = (3 * z + k) * width
            hi = min(3 * (z + 2) * width, depth)
            start = tile_start(z, k, 0, k, layers) * width
            value, held = values_ref[:, lo:hi], plane_ref.at[:, start : start + hi - lo, :]
            total = dot(value, held[0]) + dot(value, held[1])
            inner = width - TILE
            if inner:
                image_ref[:, lo : lo + inner] = total[:, :inner].astype(bf16)
            image_ref[:, lo + inner : lo + width] = (total[:, inner:] + edges[3 * z + k]).astype(bf16)
    image_ref[:, depth:] = (dot(halo, corner_ref[0]) + dot(halo, corner_ref[1])).astype(bf16)


def copy_in(pieces, start, values_ref, width):
    for array in pieces:
        if start == 0:
            values_ref[:, : 3 * width] = array[:, : 3 * width]
            start, skip = 3 * width, 3 * width + EDGE
        else:
            skip = 0
        if skip < array.shape[1]:
            end = start + array.shape[1] - skip
            values_ref[:, start:end] = array[:, skip:]
            start = end


def halo_of(first_ref, top_ref, layers, width):
    group = lane_of((first_ref.shape[0], EDGE)) // GY
    halo = first_ref[:, 3 * width : 3 * width + EDGE].astype(jnp.float32)
    top = pltpu.roll(top_ref[:, 3 * width :].astype(jnp.float32), layers * GY, 1)
    halo = jnp.where(group % (layers + 1) == layers, top, halo)
    return jnp.where(group < 3 * (layers + 1), halo, 0.0).astype(jnp.bfloat16)


def product(a, b):
    return lax.dot_general(a, b, (((1,), (1,)), ((), ())), preferred_element_type=jnp.float32)


def products(held, values_ref, image_ref, slot):
    rows = values_ref.shape[0] // 2
    value, image = (ref[slot * rows : (slot + 1) * rows] for ref in (values_ref, image_ref))
    found = []
    for v, i in held:
        both = product(image, v[...]) + product(value, i[...])
        found += [both[:, :rows], both[:, rows:]]
    if slot:
        both = product(image, values_ref[...])
        found.append(both[:, :rows] + product(value, image_ref[:rows]))
        own = both[:, rows:]
    else:
        own = product(image, value)
    return [*found, own + own.T]


def fill(layers, width, pieces, top_ref, values_ref):
    depth = 3 * (layers + 1) * width
    copy_in(pieces, 0, values_ref, width)
    values_ref[:, 3 * layers * width : depth] = top_ref[:, : 3 * width]
    values_ref[:, depth:] = halo_of(pieces[0], top_ref, layers, width)


def image_kernel(layers, width, arrays, order, last, *refs):
    refs, (pair, slot) = list(refs), divmod(len(order) - 1, 2)
    place = refs.pop(0) if last else None
    pieces = [refs.pop(0) for _ in range(arrays)]
    top_ref, *matrix, force_ref = (refs.pop(0) for _ in range(5))
    held = [(refs.pop(0), refs.pop(0)) for _ in range(pair)]
    block_refs = [refs.pop(0) for _ in range(len(order) - 1 if last else 0)]
    grad_refs = [refs.pop(0) for _ in range(pair if last else 0)]
    zone_ref = refs.pop(0) if last else None
    values_ref, image_ref, *outs = refs[2 * slot :]
    rows = values_ref.shape[0] // 2
    part = slice(slot * rows, (slot + 1) * rows)
    fill(layers, width, pieces, top_ref, values_ref.at[part])
    image_layers(layers, width, values_ref.at[part], image_ref.at[part], matrix)
    found = products(held, values_ref, image_ref, slot)
    nodes = slice(0, 3 * layers * width)
    grad = product(force_ref[:, nodes], values_ref[:, nodes])[:8] if slot else None
    if not last:
        for j, value in enumerate(found):
            outs[0][j] = value
        if slot:
            outs[1][...] = grad
        return
    keep_ref, send_ref = outs
    half, blocks = rows // 2, len(order)
    pairs = [(i, j) for i in order for j in order]
    lay_out((keep_ref, send_ref), place, half, pairs, blocks_of(order, [*block_refs, found]))
    row = lax.broadcasted_iota(jnp.int32, (blocks, rows), 0)
    small = jnp.zeros((blocks, rows), jnp.float32)
    grads = [*(r[...] for r in grad_refs), grad]
    for j, name in enumerate(order):
        value = grads[j // 2][:1, j % 2 * rows : (j % 2 + 1) * rows]
        small = jnp.where(row == (place[0] ^ name), jnp.broadcast_to(value, (blocks, rows)), small)
    for j in range(blocks):
        columns = slice(j * rows, (j + 1) * rows)
        for ref in (keep_ref, send_ref):
            ref[blocks * half : blocks * half + blocks, columns] = small
            ref[blocks * half + blocks :, columns] = zone_ref[...]


def lay_out(refs, place, half, pairs, block):
    for i, j in pairs:
        at = pl.ds(pl.multiple_of((i ^ place[2]) * half, half), half)
        value = block(i, j)
        columns = slice(2 * half * j, 2 * half * (j + 1))
        refs[0][at, columns] = jnp.where(place[1] == 0, value[:half], value[half:])
        refs[1][at, columns] = jnp.where(place[1] == 0, value[half:], value[:half])


def blocks_of(order, block_refs):
    def block(i, j):
        first, second = order.index(i), order.index(j)
        value = block_refs[max(first, second)][min(first, second)]
        return value.T if first < second else value

    return block


def vmem_call(kernel, scalars, args, outs, scratch=(), aliases=None, name="image"):
    vmem = pl.BlockSpec(memory_space=pltpu.VMEM)
    return pl.pallas_call(
        kernel,
        in_specs=[pl.BlockSpec(memory_space=pltpu.SMEM)] * len(scalars) + [vmem] * len(args),
        out_specs=[vmem] * len(outs),
        out_shape=outs,
        scratch_shapes=list(scratch),
        input_output_aliases=aliases or {},
        compiler_params=pltpu.CompilerParams(vmem_limit_bytes=8 << 20),
        cost_estimate=pl.CostEstimate(flops=0, bytes_accessed=16 << 20, transcendentals=0),
        name=name,
    )(*scalars, *args)


def on_device(sensitivity, residual_force, moments, zone_label, misfit):
    cols = sensitivity.shape[1]
    layers = moments.shape[1]
    plane = GX * GY
    n_slab = lax.axis_size("slab")
    n_col = lax.axis_size("col")
    assert n_slab == 2 * n_col
    width = cols * n_col
    source = pltpu.with_memory_space_constraint(sensitivity, pltpu.HBM)
    lanes = plane // n_col
    bottom, total = 3 * lanes + EDGE, 3 * (layers + 1) * lanes + EDGE
    last = n_col - 1
    order = sorted(range(1, n_col), key=lambda k: (k.bit_count(), -k))
    single = [k for k in order if k.bit_count() == 1]
    double = [k for k in order if k.bit_count() > 1 and k != last]
    full = (0, cols)
    calls = [
        [(k, range(layers), full) for k in single],
        [(k, range(layers), full) for k in double]
        + [(last, range(layers // 2), full), (last, range(layers // 2, layers), full)]
        + [(0, range(1), full), (0, range(1, layers), full)],
    ]
    after, pieces = [], {}
    for specs in calls:
        packed, place = pack(source, after, specs, layers, plane, n_col)
        after = [place]
        for (k, _, _), array in zip(specs, packed):
            pieces.setdefault(k, []).append(exchange(array, "col", k) if k else array)
    *matrix, zone = build(moments, zone_label, misfit, residual_force, place, n_col, cols)
    held, blocks, grads, seen = [], [], [], []
    two = pltpu.VMEM((2 * cols, total), jnp.bfloat16)
    wide = pltpu.VMEM((width // 2 + 2 * n_col, width), jnp.float32)
    for k in (0, *order):
        low = crop(pieces[k][0], bottom, blocks[1 if k == last else 0]) if k else pieces[k][0]
        top = shifted(low, "slab", -1)
        slot = len(seen) % 2
        seen.append(k)
        args = [*pieces[k], top, *matrix, *(x for pair in held for x in pair)]
        outs = [two, two]
        if k == last:
            args += [*blocks, *grads, zone]
            outs += [wide, wide]
        else:
            outs.append(pltpu.VMEM((len(seen), cols, cols), jnp.float32))
            outs += [pltpu.VMEM((8, 2 * cols), jnp.float32)] * slot
        scalars, aliases = [place] * (k == last), {}
        if slot:
            aliases = {len(scalars) + len(args) + i: i for i in range(2)}
            args += current
        kernel = functools.partial(image_kernel, layers, lanes, len(pieces[k]), tuple(seen), k == last)
        out = vmem_call(kernel, scalars, args, outs, (), aliases)
        if k == last:
            keep, send = out[2:]
        else:
            out = [in_vmem(x) for x in out]
            current = out[:2]
            blocks.append(out[2])
            grads += out[3:]
            held += [current] * slot

    mine = keep + exchange(send, "slab", 1)
    parts = [mine[:, k * cols : (k + 1) * cols] for k in range(n_col)]
    mine = parts[0]
    for k in (order[0], *order[:0:-1]):
        mine = mine + exchange(parts[k], "col", k)
    half, rows = cols // 2, width // 2
    parts = [jnp.concatenate([mine[k * half : (k + 1) * half], mine[rows:]]) for k in range(n_col)]
    parts = [parts[0]] + [exchange(parts[k], "slab", 2 * k) for k in (1, *range(n_col - 1, 1, -1))]
    hessian = sum(part[:half] for part in parts).T
    both = sum(part[half:] for part in parts).reshape(2, width)
    gradient = both[0]
    zone_misfit = both[1] * (width / (layers * plane * n_slab))
    return (hessian, gradient, zone_misfit)


def solution(mesh):
    in_specs = (
        P(None, "col", "slab"),
        P(None, "slab"),
        P(None, "slab", None),
        P("slab", None),
        P("slab", None),
    )
    out_specs = (P("col", "slab"), P(), P())
    return jax.shard_map(
        on_device, mesh=mesh, in_specs=in_specs, out_specs=out_specs, check_vma=False
    )
```

time: 111 us -> 73.2 us (0.66)
  local copies, waits for them, and re-layouts: 15.2 us -> 0.07 us
  waiting for transfers between devices: 32.6 us -> 21.9 us
  Pallas kernels: 36.7 us -> 26.8 us
  matrix products: 1.72 us -> 0 us
    unnamed x28 -> x8, local copies, waits for them, and re-layouts: 14.3 us -> 0.03 us
    ppermute x11, waiting for transfers between devices: 32.6 us -> 21.9 us  [exchange(): return lax.ppermute(value, axis, [(i, i ^ by) for i in range(count)])]
    pallas_call x8 -> x6, Pallas kernels: 31.4 us -> 23.4 us  [the longest x4 18.1 us: vmem_call(): pl.pallas_call(kernel, in_specs=[pl.BlockSpec(memory_space=pltpu.SMEM)] *...]
    pallas_call x3, Pallas kernels: 1.93 us -> 0.05 us  [crop(): pl.pallas_call(crop_kernel, in_specs=[pl.BlockSpec(memory_space=pltpu.VME...]
    dot_general x2 -> x0, matrix products: 1.72 us -> none  [the longest x1 0.92 us: small_sums(): lax.dot_general(residual_force, sensitivity, (((0, 1), (0, 2)), ((), ()))...]
  transfers between devices with their start and end apart: 15 -> 15, of which waited for: 7 -> 10; matrix products, arithmetic and copies ran while one was open for 2% -> 0% of each run, Pallas kernels for 26% -> 25%
where the time goes in v4:
time: 73.2 us; the launch traced here: 72.9 us
  Pallas kernels  26.8 us (37%)
  starting transfers between devices  22 us (30%)
  waiting for transfers between devices  21.9 us (30%)
  other arithmetic  1.36 us (2%)
  between operations  0.82 us (1%)
    ppermute x11, waiting for transfers between devices, exchange(): return lax.ppermute(value, axis, [(i, i ^ by) for i in range(count)])  21.9 us
    pallas_call x4, Pallas kernels, vmem_call(): pl.pallas_call(kernel, in_specs=[pl.BlockSpec(memory_space=pltpu.SMEM)] *...  18.1 us
    ppermute x11, starting transfers between devices, exchange(): return lax.ppermute(value, axis, [(i, i ^ by) for i in range(count)])  16.6 us
    ppermute x4, starting transfers between devices, shifted(): return lax.ppermute(value, axis, pairs)  5.35 us
    pallas_call x2, Pallas kernels, pack(): pl.pallas_call(functools.partial(pack_kernel, layers, plane, n_col, specs...  5.24 us
    pallas_call x1, Pallas kernels, build(): pl.pallas_call(functools.partial(build_kernel, layers, width), grid_spec=...  3.36 us
  transfers between devices with their start and end apart: 15, of which 10 were waited for; matrix products, arithmetic and copies ran while one was open for 0% of the time, Pallas kernels for 25%

profile of v4, /device:TPU:0, one launch (start us, length us, event | category | flops | bytes accessed | tf_op | source)
XLA Modules:
  0.0 72.9 jit_solution(18254399803684734255)
XLA Ops:
  0.6 2.4 %pack.2 = (bf16[128,3328]{1,0:T(8,128)(2,1)S(1)}, bf16[128,3328]{1,0:T(8,128)(2,1)S(1)}, s32[3]{0:T(128)S(1)}) custom-call(bf16[3,128,4096]{2,1,0:T(8,128)(2,1)} %sens_ref.3), custom_call_target="tpu_custom_call" | custom-call | bytes 4194304 | tf_op jit(solution)/shard_map/pack/pallas_call | solution.py:114
  3.0 0.0 copy-start
  3.0 0.0 copy-start.1
  3.0 0.0 copy-start.2
  3.1 0.0 copy-start.3
  3.1 3.0 %collective-permute-start.2 = (bf16[128,3328]{1,0:T(8,128)(2,1)S(1)}, bf16[128,3328]{1,0:T(8,128)(2,1)S(1)}, u32[]{:S(2)}, u32[]{:S(2)}) collective-permute-start(bf16[128,3328]{1,0:T(8,128)(2,1)S(1)} %get-tuple-element.32), channel_id=1, source_target_pairs={{0,2},{1,3},{2,0},{3,1},{4,6},{5,7},{6,4},{7,5},{8,10},{9,11},{10,... | collective-permute-start | bytes 2555912 | tf_op jit(solution)/shard_map/ppermute | solution.py:18
  6.1 1.5 %collective-permute-start.6 = (bf16[128,3328]{1,0:T(8,128)(2,1)S(1)}, bf16[128,3328]{1,0:T(8,128)(2,1)S(1)}, u32[]{:S(2)}, u32[]{:S(2)}) collective-permute-start(bf16[128,3328]{1,0:T(8,128)(2,1)S(1)} %get-tuple-element.45), channel_id=1, source_target_pairs={{0,1},{1,0},{2,3},{3,2},{4,5},{5,4},{6,7},{7,6},{8,9},{9,8},{10,11... | collective-permute-start | bytes 2555912 | tf_op jit(solution)/shard_map/ppermute | solution.py:18
  7.6 2.9 %pack.3 = (bf16[128,1792]{1,0:T(8,128)(2,1)S(1)}, bf16[128,1536]{1,0:T(8,128)(2,1)S(1)}, bf16[128,1024]{1,0:T(8,128)(2,1)S(1)}, bf16[128,2304]{1,0:T(8,128)(2,1)S(1)}, s32[3]{0:T(128)S(1)}) custom-call(bf16[3,128,4096]{2,1,0:T(8,128)(2,1)} %sens_ref.3, s32[3]{0:T(128)S(1)} %get-tuple-element.28.refs_0_), custom_call_target="tpu_custom_call" | custom-call | bytes 4194304 | tf_op jit(solution)/shard_map/pack/pallas_call | solution.py:114
  10.5 1.3 %collective-permute-start.3 = (bf16[128,1024]{1,0:T(8,128)(2,1)S(1)}, bf16[128,1024]{1,0:T(8,128)(2,1)S(1)}, u32[]{:S(2)}, u32[]{:S(2)}) collective-permute-start(bf16[128,1024]{1,0:T(8,128)(2,1)S(1)} %get-tuple-element.33.refs_0_), channel_id=1, source_target_pairs={{4,0},{8,4},{12,8},{16,12},{20,16},{24,20},{28,24},{5,1},{9,5},{13... | collective-permute-start | bytes 786440 | tf_op jit(solution)/shard_map/ppermute | solution.py:24
  11.8 0.1 collective-permute-start
  11.9 0.0 copy-done
  11.9 0.0 copy-done.1
  11.9 0.0 copy-done.2
  11.9 0.0 copy-done.3
  11.9 3.4 %build.1 = (bf16[2,16896,256]{2,1,0:T(8,128)(2,1)S(1)}, bf16[2,8,256,256]{3,2,1,0:T(8,128)(2,1)S(1)}, bf16[2,256,256]{2,1,0:T(8,128)(2,1)S(1)}, bf16[16,4096]{1,0:T(8,128)(2,1)S(1)}, f32[4,128]{1,0:T(4,128)S(1)}) custom-call(s32[3]{0:T(128)S(1)} %get-tuple-element.29.place.refs_0_, f32[6,4,1024]{2,1,0:T(4,128)S(1)} %copy-done.1, s32[4,1024]{1,0:T(4,128)S(1)} %copy-done.2, ...), custom_call_target="tpu_custom_call" | custom-call | bytes 12582912 | tf_op jit(solution)/shard_map/build/pallas_call | solution.py:302
  15.3 0.0 collective-permute-done.3.refs_2_
  15.3 3.3 %image.4 = (bf16[256,4096]{1,0:T(8,128)(2,1)S(1)}, bf16[256,4096]{1,0:T(8,128)(2,1)S(1)}, f32[1,128,128]{2,1,0:T(8,128)S(1)}) custom-call(bf16[128,1024]{1,0:T(8,128)(2,1)S(1)} %get-tuple-element.33.refs_0_, bf16[128,2304]{1,0:T(8,128)(2,1)S(1)} %get-tuple-element.34.refs_1_, bf16[128,1024]{1,0:T(8,128)(2,1)S(1)} %collective-permute-done.3.refs_2_, ...), custom_call_target="tpu_custom_call" | custom-call | bytes 16777216 | tf_op jit(solution)/shard_map/image/pallas_call | solution.py:462
  18.6 6.5 %collective-permute-done.2.piece_ref.refs_0_ = bf16[128,3328]{1,0:T(8,128)(2,1)S(1)} collective-permute-done((bf16[128,3328]{1,0:T(8,128)(2,1)S(1)}, bf16[128,3328]{1,0:T(8,128)(2,1)S(1)}, u32[]{:S(2)}, u32[]{:S(2)}) %collective-permute-start.2) | collective-permute-done | bytes 852000 | tf_op jit(solution)/shard_map/ppermute | solution.py:18
  25.1 1.3 %collective-permute-start.4 = (bf16[128,1024]{1,0:T(8,128)(2,1)S(1)}, bf16[128,1024]{1,0:T(8,128)(2,1)S(1)}, u32[]{:S(2)}, u32[]{:S(2)}) collective-permute-start(bf16[128,1024]{1,0:T(8,128)(2,1)S(1)} %crop.3), channel_id=1, source_target_pairs={{4,0},{8,4},{12,8},{16,12},{20,16},{24,20},{28,24},{5,1},{9,5},{13... | collective-permute-start | bytes 786440 | tf_op jit(solution)/shard_map/ppermute | solution.py:24
  26.4 3.0 %collective-permute-start.1 = (bf16[128,1536]{1,0:T(8,128)(2,1)S(1)}, bf16[128,1536]{1,0:T(8,128)(2,1)S(1)}, u32[]{:S(2)}, u32[]{:S(2)}) collective-permute-start(bf16[128,1536]{1,0:T(8,128)(2,1)S(1)} %get-tuple-element.31), channel_id=1, source_target_pairs={{0,3},{1,2},{2,1},{3,0},{4,7},{5,6},{6,5},{7,4},{8,11},{9,10},{10,... | collective-permute-start | bytes 1179656 | tf_op jit(solution)/shard_map/ppermute | solution.py:18
  29.4 0.0 collective-permute-done.6.piece_ref.refs_0_
  29.4 1.3 %collective-permute-start.7 = (bf16[128,1024]{1,0:T(8,128)(2,1)S(1)}, bf16[128,1024]{1,0:T(8,128)(2,1)S(1)}, u32[]{:S(2)}, u32[]{:S(2)}) collective-permute-start(bf16[128,1024]{1,0:T(8,128)(2,1)S(1)} %crop.5), channel_id=1, source_target_pairs={{4,0},{8,4},{12,8},{16,12},{20,16},{24,20},{28,24},{5,1},{9,5},{13... | collective-permute-start | bytes 786440 | tf_op jit(solution)/shard_map/ppermute | solution.py:24
  30.7 0.0 collective-permute-done.4.refs_1_
  30.7 4.1 %image.5 = (bf16[256,4096]{1,0:T(8,128)(2,1)S(1)}, bf16[256,4096]{1,0:T(8,128)(2,1)S(1)}, f32[2,128,128]{2,1,0:T(8,128)S(1)}, f32[8,256]{1,0:T(8,128)S(1)}) custom-call(bf16[128,3328]{1,0:T(8,128)(2,1)S(1)} %collective-permute-done.2.piece_ref.refs_0_, ...), custom_call_target="tpu_custom_call", output_to_operand_aliasing={{0}: (6, {}), {1}: (7, {})} | custom-call | bytes 16777216 | tf_op jit(solution)/shard_map/image/pallas_call | solution.py:462
  34.8 2.5 %collective-permute-done.piece_ref.refs_1_ = bf16[128,1792]{1,0:T(8,128)(2,1)S(1)} collective-permute-done((bf16[128,1792]{1,0:T(8,128)(2,1)S(1)}, bf16[128,1792]{1,0:T(8,128)(2,1)S(1)}, u32[]{:S(2)}, u32[]{:S(2)}) %collective-permute-start) | collective-permute-done | bytes 458784 | tf_op jit(solution)/shard_map/ppermute | solution.py:18
  37.3 1.5 %collective-permute-start.5 = (bf16[128,1024]{1,0:T(8,128)(2,1)S(1)}, bf16[128,1024]{1,0:T(8,128)(2,1)S(1)}, u32[]{:S(2)}, u32[]{:S(2)}) collective-permute-start(bf16[128,1024]{1,0:T(8,128)(2,1)S(1)} %crop.4), channel_id=1, source_target_pairs={{4,0},{8,4},{12,8},{16,12},{20,16},{24,20},{28,24},{5,1},{9,5},{13... | collective-permute-start | bytes 786440 | tf_op jit(solution)/shard_map/ppermute | solution.py:24
  38.8 0.0 collective-permute-done.7.refs_1_
  38.8 4.6 %image.6 = (bf16[256,4096]{1,0:T(8,128)(2,1)S(1)}, bf16[256,4096]{1,0:T(8,128)(2,1)S(1)}, f32[3,128,128]{2,1,0:T(8,128)S(1)}) custom-call(bf16[128,3328]{1,0:T(8,128)(2,1)S(1)} %collective-permute-done.6.piece_ref.refs_0_, bf16[128,1024]{1,0:T(8,128)(2,1)S(1)} %collective-permute-done.7.refs_1_, ...), custom_call_target="tpu_custom_call" | custom-call | bytes 16777216 | tf_op jit(solution)/shard_map/image/pallas_call | solution.py:462
  43.3 1.2 %collective-permute-done.1.refs_2_ = bf16[128,1536]{1,0:T(8,128)(2,1)S(1)} collective-permute-done((bf16[128,1536]{1,0:T(8,128)(2,1)S(1)}, bf16[128,1536]{1,0:T(8,128)(2,1)S(1)}, u32[]{:S(2)}, u32[]{:S(2)}) %collective-permute-start.1) | collective-permute-done | bytes 393248 | tf_op jit(solution)/shard_map/ppermute | solution.py:18
  44.6 0.0 collective-permute-done.5.refs_3_
  44.6 6.3 %image.7 = (bf16[256,4096]{1,0:T(8,128)(2,1)S(1)}, bf16[256,4096]{1,0:T(8,128)(2,1)S(1)}, f32[264,512]{1,0:T(8,128)S(1)}, f32[264,512]{1,0:T(8,128)S(1)}) custom-call(s32[3]{0:T(128)S(1)} %get-tuple-element.29.place.refs_0_, bf16[128,1792]{1,0:T(8,128)(2,1)S(1)} %collective-permute-done.piece_ref.refs_1_, ...), custom_call_target="tpu_custom_call", output_to_operand_aliasing={{0}: (15, {}), {1}: (16, {})} | custom-call | bytes 16777216 | tf_op jit(solution)/shard_map/image/pallas_call | solution.py:462
  50.8 0.9 %collective-permute-start.8 = (f32[264,512]{1,0:T(8,128)S(1)}, f32[264,512]{1,0:T(8,128)S(1)}, u32[]{:S(2)}, u32[]{:S(2)}) collective-permute-start(f32[264,512]{1,0:T(8,128)S(1)} %get-tuple-element.52), channel_id=1, source_target_pairs={{0,4},{4,0},{8,12},{12,8},{16,20},{20,16},{24,28},{28,24},{1,5},{5... | collective-permute-start | bytes 1622024 | tf_op jit(solution)/shard_map/ppermute | solution.py:18
  51.7 1.6 %collective-permute-done.8 = f32[264,512]{1,0:T(8,128)S(1)} collective-permute-done((f32[264,512]{1,0:T(8,128)S(1)}, f32[264,512]{1,0:T(8,128)S(1)}, u32[]{:S(2)}, u32[]{:S(2)}) %collective-permute-start.8) | collective-permute-done | bytes 540704 | tf_op jit(solution)/shard_map/ppermute | solution.py:18
  53.3 0.1 add.30
  53.4 1.6 %collective-permute-start.9 = (f32[264,128]{1,0:T(8,128)S(1)}, f32[264,128]{1,0:T(8,128)S(1)}, u32[]{:S(2)}, u32[]{:S(2)}) collective-permute-start(f32[264,128]{1,0:T(8,128)S(1)} %get-tuple-element.53), channel_id=1, source_target_pairs={{0,2},{1,3},{2,0},{3,1},{4,6},{5,7},{6,4},{7,5},{8,10},{9,11},{10,... | collective-permute-start | bytes 405512 | tf_op jit(solution)/shard_map/ppermute | solution.py:18
  55.0 1.5 %collective-permute-start.11 = (f32[264,128]{1,0:T(8,128)S(1)}, f32[264,128]{1,0:T(8,128)S(1)}, u32[]{:S(2)}, u32[]{:S(2)}) collective-permute-start(f32[264,128]{1,0:T(8,128)S(1)} %get-tuple-element.54), channel_id=1, source_target_pairs={{0,1},{1,0},{2,3},{3,2},{4,5},{5,4},{6,7},{7,6},{8,9},{9,8},{10,11... | collective-permute-start | bytes 405512 | tf_op jit(solution)/shard_map/ppermute | solution.py:18
  56.5 0.5 collective-permute-start.10
  57.0 2.4 %collective-permute-done.9 = f32[264,128]{1,0:T(8,128)S(1)} collective-permute-done((f32[264,128]{1,0:T(8,128)S(1)}, f32[264,128]{1,0:T(8,128)S(1)}, u32[]{:S(2)}, u32[]{:S(2)}) %collective-permute-start.9) | collective-permute-done | bytes 135200 | tf_op jit(solution)/shard_map/ppermute | solution.py:18
  59.4 2.1 %collective-permute-done.11 = f32[264,128]{1,0:T(8,128)S(1)} collective-permute-done((f32[264,128]{1,0:T(8,128)S(1)}, f32[264,128]{1,0:T(8,128)S(1)}, u32[]{:S(2)}, u32[]{:S(2)}) %collective-permute-start.11) | collective-permute-done | bytes 135200 | tf_op jit(solution)/shard_map/ppermute | solution.py:18
  61.5 2.0 %collective-permute-done.10 = f32[264,128]{1,0:T(8,128)S(1)} collective-permute-done((f32[264,128]{1,0:T(8,128)S(1)}, f32[264,128]{1,0:T(8,128)S(1)}, u32[]{:S(2)}, u32[]{:S(2)}) %collective-permute-start.10) | collective-permute-done | bytes 135200 | tf_op jit(solution)/shard_map/ppermute | solution.py:18
  63.5 3.2 %collective-permute-start.13 = (f32[72,128]{1,0:T(8,128)S(1)}, f32[72,128]{1,0:T(8,128)S(1)}, u32[]{:S(2)}, u32[]{:S(2)}) collective-permute-start(f32[72,128]{1,0:T(8,128)S(1)} %concatenate.12), channel_id=1, source_target_pairs={{0,24},{4,28},{8,16},{12,20},{16,8},{20,12},{24,0},{28,4},{1,25},{... | collective-permute-start | bytes 110600 | tf_op jit(solution)/shard_map/ppermute | solution.py:18
  66.8 0.0 collective-permute-start.12
  66.8 1.2 %collective-permute-start.14 = (f32[72,128]{1,0:T(8,128)S(1)}, f32[72,128]{1,0:T(8,128)S(1)}, u32[]{:S(2)}, u32[]{:S(2)}) collective-permute-start(f32[72,128]{1,0:T(8,128)S(1)} %get-tuple-element.61), channel_id=1, source_target_pairs={{0,16},{4,20},{8,24},{12,28},{16,0},{20,4},{24,8},{28,12},{1,17},{... | collective-permute-start | bytes 110600 | tf_op jit(solution)/shard_map/ppermute | solution.py:18
  68.0 1.4 %collective-permute-done.13 = f32[72,128]{1,0:T(8,128)S(1)} collective-permute-done((f32[72,128]{1,0:T(8,128)S(1)}, f32[72,128]{1,0:T(8,128)S(1)}, u32[]{:S(2)}, u32[]{:S(2)}) %collective-permute-start.13) | collective-permute-done | bytes 36896 | tf_op jit(solution)/shard_map/ppermute | solution.py:18
  69.3 1.4 %collective-permute-done.12 = f32[72,128]{1,0:T(8,128)S(1)} collective-permute-done((f32[72,128]{1,0:T(8,128)S(1)}, f32[72,128]{1,0:T(8,128)S(1)}, u32[]{:S(2)}, u32[]{:S(2)}) %collective-permute-start.12) | collective-permute-done | bytes 36896 | tf_op jit(solution)/shard_map/ppermute | solution.py:18
  70.7 1.0 %collective-permute-done.14 = f32[72,128]{1,0:T(8,128)S(1)} collective-permute-done((f32[72,128]{1,0:T(8,128)S(1)}, f32[72,128]{1,0:T(8,128)S(1)}, u32[]{:S(2)}, u32[]{:S(2)}) %collective-permute-start.14) | collective-permute-done | bytes 36896 | tf_op jit(solution)/shard_map/ppermute | solution.py:18
  71.7 0.6 multiply_bitcast_fusion
  72.3 0.6 fusion.2
  (10 shorter events, 0.2 us)
Async XLA Ops:
  3.0 8.9 %copy-start = (bf16[3,4096]{1,0:T(4,128)(2,1)S(1)}, bf16[3,4096]{1,0:T(4,128)(2,1)}, u32[]{:S(2)}) copy-start(bf16[3,4096]{1,0:T(4,128)(2,1)} %refs_3_.1) | copy-start | bytes 73732
  3.0 8.9 %copy-start.1 = (f32[6,4,1024]{2,1,0:T(4,128)S(1)}, f32[6,4,1024]{2,1,0:T(4,128)}, u32[]{:S(2)}) copy-start(f32[6,4,1024]{2,1,0:T(4,128)} %moments_ref.1) | copy-start | bytes 294916
  3.0 8.9 %copy-start.2 = (s32[4,1024]{1,0:T(4,128)S(1)}, s32[4,1024]{1,0:T(4,128)}, u32[]{:S(2)}) copy-start(s32[4,1024]{1,0:T(4,128)} %label_ref.1) | copy-start | bytes 49156
  3.1 8.9 %copy-start.3 = (f32[4,1024]{1,0:T(4,128)S(1)}, f32[4,1024]{1,0:T(4,128)}, u32[]{:S(2)}) copy-start(f32[4,1024]{1,0:T(4,128)} %misfit_ref.1) | copy-start | bytes 49156
  3.1 22.0 %collective-permute-start.2 = (bf16[128,3328]{1,0:T(8,128)(2,1)S(1)}, bf16[128,3328]{1,0:T(8,128)(2,1)S(1)}, u32[]{:S(2)}, u32[]{:S(2)}) collective-permute-start(bf16[128,3328]{1,0:T(8,128)(2,1)S(1)} %get-tuple-element.32), channel_id=1, source_target_pairs={{0,2},{1,3},{2,0},{3,1},{4,6},{5,7},{6,4},{7,5},{8,10},{9,11},{10,... | collective-permute-start | bytes 2555912 | tf_op jit(solution)/shard_map/ppermute | solution.py:18
  6.1 23.3 %collective-permute-start.6 = (bf16[128,3328]{1,0:T(8,128)(2,1)S(1)}, bf16[128,3328]{1,0:T(8,128)(2,1)S(1)}, u32[]{:S(2)}, u32[]{:S(2)}) collective-permute-start(bf16[128,3328]{1,0:T(8,128)(2,1)S(1)} %get-tuple-element.45), channel_id=1, source_target_pairs={{0,1},{1,0},{2,3},{3,2},{4,5},{5,4},{6,7},{7,6},{8,9},{9,8},{10,11... | collective-permute-start | bytes 2555912 | tf_op jit(solution)/shard_map/ppermute | solution.py:18
  10.5 4.8 %collective-permute-start.3 = (bf16[128,1024]{1,0:T(8,128)(2,1)S(1)}, bf16[128,1024]{1,0:T(8,128)(2,1)S(1)}, u32[]{:S(2)}, u32[]{:S(2)}) collective-permute-start(bf16[128,1024]{1,0:T(8,128)(2,1)S(1)} %get-tuple-element.33.refs_0_), channel_id=1, source_target_pairs={{4,0},{8,4},{12,8},{16,12},{20,16},{24,20},{28,24},{5,1},{9,5},{13... | collective-permute-start | bytes 786440 | tf_op jit(solution)/shard_map/ppermute | solution.py:24
  11.8 25.5 %collective-permute-start = (bf16[128,1792]{1,0:T(8,128)(2,1)S(1)}, bf16[128,1792]{1,0:T(8,128)(2,1)S(1)}, u32[]{:S(2)}, u32[]{:S(2)}) collective-permute-start(bf16[128,1792]{1,0:T(8,128)(2,1)S(1)} %get-tuple-element.30), channel_id=1, source_target_pairs={{0,3},{1,2},{2,1},{3,0},{4,7},{5,6},{6,5},{7,4},{8,11},{9,10},{10,... | collective-permute-start | bytes 1376264 | tf_op jit(solution)/shard_map/ppermute | solution.py:18
  25.1 5.6 %collective-permute-start.4 = (bf16[128,1024]{1,0:T(8,128)(2,1)S(1)}, bf16[128,1024]{1,0:T(8,128)(2,1)S(1)}, u32[]{:S(2)}, u32[]{:S(2)}) collective-permute-start(bf16[128,1024]{1,0:T(8,128)(2,1)S(1)} %crop.3), channel_id=1, source_target_pairs={{4,0},{8,4},{12,8},{16,12},{20,16},{24,20},{28,24},{5,1},{9,5},{13... | collective-permute-start | bytes 786440 | tf_op jit(solution)/shard_map/ppermute | solution.py:24
  26.4 18.2 %collective-permute-start.1 = (bf16[128,1536]{1,0:T(8,128)(2,1)S(1)}, bf16[128,1536]{1,0:T(8,128)(2,1)S(1)}, u32[]{:S(2)}, u32[]{:S(2)}) collective-permute-start(bf16[128,1536]{1,0:T(8,128)(2,1)S(1)} %get-tuple-element.31), channel_id=1, source_target_pairs={{0,3},{1,2},{2,1},{3,0},{4,7},{5,6},{6,5},{7,4},{8,11},{9,10},{10,... | collective-permute-start | bytes 1179656 | tf_op jit(solution)/shard_map/ppermute | solution.py:18
  29.4 9.4 %collective-permute-start.7 = (bf16[128,1024]{1,0:T(8,128)(2,1)S(1)}, bf16[128,1024]{1,0:T(8,128)(2,1)S(1)}, u32[]{:S(2)}, u32[]{:S(2)}) collective-permute-start(bf16[128,1024]{1,0:T(8,128)(2,1)S(1)} %crop.5), channel_id=1, source_target_pairs={{4,0},{8,4},{12,8},{16,12},{20,16},{24,20},{28,24},{5,1},{9,5},{13... | collective-permute-start | bytes 786440 | tf_op jit(solution)/shard_map/ppermute | solution.py:24
  37.3 7.3 %collective-permute-start.5 = (bf16[128,1024]{1,0:T(8,128)(2,1)S(1)}, bf16[128,1024]{1,0:T(8,128)(2,1)S(1)}, u32[]{:S(2)}, u32[]{:S(2)}) collective-permute-start(bf16[128,1024]{1,0:T(8,128)(2,1)S(1)} %crop.4), channel_id=1, source_target_pairs={{4,0},{8,4},{12,8},{16,12},{20,16},{24,20},{28,24},{5,1},{9,5},{13... | collective-permute-start | bytes 786440 | tf_op jit(solution)/shard_map/ppermute | solution.py:24
  50.8 2.5 %collective-permute-start.8 = (f32[264,512]{1,0:T(8,128)S(1)}, f32[264,512]{1,0:T(8,128)S(1)}, u32[]{:S(2)}, u32[]{:S(2)}) collective-permute-start(f32[264,512]{1,0:T(8,128)S(1)} %get-tuple-element.52), channel_id=1, source_target_pairs={{0,4},{4,0},{8,12},{12,8},{16,20},{20,16},{24,28},{28,24},{1,5},{5... | collective-permute-start | bytes 1622024 | tf_op jit(solution)/shard_map/ppermute | solution.py:18
  53.4 5.9 %collective-permute-start.9 = (f32[264,128]{1,0:T(8,128)S(1)}, f32[264,128]{1,0:T(8,128)S(1)}, u32[]{:S(2)}, u32[]{:S(2)}) collective-permute-start(f32[264,128]{1,0:T(8,128)S(1)} %get-tuple-element.53), channel_id=1, source_target_pairs={{0,2},{1,3},{2,0},{3,1},{4,6},{5,7},{6,4},{7,5},{8,10},{9,11},{10,... | collective-permute-start | bytes 405512 | tf_op jit(solution)/shard_map/ppermute | solution.py:18
  55.0 6.4 %collective-permute-start.11 = (f32[264,128]{1,0:T(8,128)S(1)}, f32[264,128]{1,0:T(8,128)S(1)}, u32[]{:S(2)}, u32[]{:S(2)}) collective-permute-start(f32[264,128]{1,0:T(8,128)S(1)} %get-tuple-element.54), channel_id=1, source_target_pairs={{0,1},{1,0},{2,3},{3,2},{4,5},{5,4},{6,7},{7,6},{8,9},{9,8},{10,11... | collective-permute-start | bytes 405512 | tf_op jit(solution)/shard_map/ppermute | solution.py:18
  56.5 6.9 %collective-permute-start.10 = (f32[264,128]{1,0:T(8,128)S(1)}, f32[264,128]{1,0:T(8,128)S(1)}, u32[]{:S(2)}, u32[]{:S(2)}) collective-permute-start(f32[264,128]{1,0:T(8,128)S(1)} %get-tuple-element.55), channel_id=1, source_target_pairs={{0,3},{1,2},{2,1},{3,0},{4,7},{5,6},{6,5},{7,4},{8,11},{9,10},{10,... | collective-permute-start | bytes 405512 | tf_op jit(solution)/shard_map/ppermute | solution.py:18
  63.5 5.8 %collective-permute-start.13 = (f32[72,128]{1,0:T(8,128)S(1)}, f32[72,128]{1,0:T(8,128)S(1)}, u32[]{:S(2)}, u32[]{:S(2)}) collective-permute-start(f32[72,128]{1,0:T(8,128)S(1)} %concatenate.12), channel_id=1, source_target_pairs={{0,24},{4,28},{8,16},{12,20},{16,8},{20,12},{24,0},{28,4},{1,25},{... | collective-permute-start | bytes 110600 | tf_op jit(solution)/shard_map/ppermute | solution.py:18
  66.8 4.0 %collective-permute-start.12 = (f32[72,128]{1,0:T(8,128)S(1)}, f32[72,128]{1,0:T(8,128)S(1)}, u32[]{:S(2)}, u32[]{:S(2)}) collective-permute-start(f32[72,128]{1,0:T(8,128)S(1)} %get-tuple-element.60), channel_id=1, source_target_pairs={{0,8},{4,12},{8,0},{12,4},{16,24},{20,28},{24,16},{28,20},{1,9},{5... | collective-permute-start | bytes 110600 | tf_op jit(solution)/shard_map/ppermute | solution.py:18
  66.8 4.9 %collective-permute-start.14 = (f32[72,128]{1,0:T(8,128)S(1)}, f32[72,128]{1,0:T(8,128)S(1)}, u32[]{:S(2)}, u32[]{:S(2)}) collective-permute-start(f32[72,128]{1,0:T(8,128)S(1)} %get-tuple-element.61), channel_id=1, source_target_pairs={{0,16},{4,20},{8,24},{12,28},{16,0},{20,4},{24,8},{28,12},{1,17},{... | collective-permute-start | bytes 110600 | tf_op jit(solution)/shard_map/ppermute | solution.py:18

commit v5 on v4

--- a/solution.py
+++ b/solution.py
@@ -381,7 +381,8 @@
     value, image = (ref[slot * rows : (slot + 1) * rows] for ref in (values_ref, image_ref))
     found = []
     for v, i in held:
-        both = product(image, v[...]) + product(value, i[...])
+        both = jnp.dot(image, v[...], preferred_element_type=jnp.float32)
+        both += jnp.dot(value, i[...], preferred_element_type=jnp.float32)
         found += [both[:, :rows], both[:, rows:]]
     if slot:
         both = product(image, values_ref[...])
@@ -399,7 +400,7 @@
     values_ref[:, depth:] = halo_of(pieces[0], top_ref, layers, width)
 
 
-def image_kernel(layers, width, arrays, order, last, *refs):
+def image_kernel(layers, width, arrays, order, last, turn, *refs):
     refs, (pair, slot) = list(refs), divmod(len(order) - 1, 2)
     place = refs.pop(0) if last else None
     pieces = [refs.pop(0) for _ in range(arrays)]
@@ -408,7 +409,7 @@
     block_refs = [refs.pop(0) for _ in range(len(order) - 1 if last else 0)]
     grad_refs = [refs.pop(0) for _ in range(pair if last else 0)]
     zone_ref = refs.pop(0) if last else None
-    values_ref, image_ref, *outs = refs[2 * slot :]
+    values_ref, image_ref, *outs = refs[(4 if turn else 2) * slot :]
     rows = values_ref.shape[0] // 2
     part = slice(slot * rows, (slot + 1) * rows)
     fill(layers, width, pieces, top_ref, values_ref.at[part])
@@ -417,6 +418,12 @@
     nodes = slice(0, 3 * layers * width)
     grad = product(force_ref[:, nodes], values_ref[:, nodes])[:8] if slot else None
     if not last:
+        if turn:
+            turned, outs = outs[:2], outs[2:]
+            step = min(2 * TILE, width)
+            for start in range(0, values_ref.shape[1], step):
+                for ref, to in zip((values_ref, image_ref), turned):
+                    to[start : start + step, part] = ref[part, start : start + step].T
         for j, value in enumerate(found):
             outs[0][j] = value
         if slot:
@@ -511,6 +518,9 @@
         seen.append(k)
         args = [*pieces[k], top, *matrix, *(x for pair in held for x in pair)]
         outs = [two, two]
+        if len(seen) <= n_col - 2:
+            outs += [pltpu.VMEM((total, 2 * cols), jnp.bfloat16)] * 2
+        count = len(outs)
         if k == last:
             args += [*blocks, *grads, zone]
             outs += [wide, wide]
@@ -519,27 +529,27 @@
             outs += [pltpu.VMEM((8, 2 * cols), jnp.float32)] * slot
         scalars, aliases = [place] * (k == last), {}
         if slot:
-            aliases = {len(scalars) + len(args) + i: i for i in range(2)}
+            aliases = {len(scalars) + len(args) + i: i for i in range(count)}
             args += current
-        kernel = functools.partial(image_kernel, layers, lanes, len(pieces[k]), tuple(seen), k == last)
+        kernel = functools.partial(image_kernel, layers, lanes, len(pieces[k]), tuple(seen), k == last, count > 2)
         out = vmem_call(kernel, scalars, args, outs, (), aliases)
         if k == last:
             keep, send = out[2:]
         else:
             out = [in_vmem(x) for x in out]
-            current = out[:2]
-            blocks.append(out[2])
-            grads += out[3:]
-            held += [current] * slot
+            current = out[:count]
+            blocks.append(out[count])
+            grads += out[count + 1 :]
+            held += [current[2:]] * slot
 
     mine = keep + exchange(send, "slab", 1)
     parts = [mine[:, k * cols : (k + 1) * cols] for k in range(n_col)]
     mine = parts[0]
-    for k in (order[0], *order[:0:-1]):
+    for k in range(1, n_col):
         mine = mine + exchange(parts[k], "col", k)
     half, rows = cols // 2, width // 2
     parts = [jnp.concatenate([mine[k * half : (k + 1) * half], mine[rows:]]) for k in range(n_col)]
-    parts = [parts[0]] + [exchange(parts[k], "slab", 2 * k) for k in (1, *range(n_col - 1, 1, -1))]
+    parts = [parts[0]] + [exchange(parts[k], "slab", 2 * k) for k in range(1, n_col)]
     hessian = sum(part[:half] for part in parts).T
     both = sum(part[half:] for part in parts).reshape(2, width)
     gradient = both[0]

time: 73.2 us -> 72 us (0.984)
  Pallas kernels: 26.8 us -> 25.7 us
    pallas_call x4, Pallas kernels: 18.1 us -> 17 us  [vmem_call(): pl.pallas_call(kernel, in_specs=[pl.BlockSpec(memory_space=pltpu.SMEM)] *...]
  transfers between devices with their start and end apart: 15 -> 15, of which waited for: 10 -> 9; matrix products, arithmetic and copies ran while one was open for 0% -> 0% of each run, Pallas kernels for 25% -> 25%
where the time goes in v5:
time: 72 us; the launch traced here: 71.8 us
  Pallas kernels  25.7 us (36%)
  starting transfers between devices  22 us (31%)
  waiting for transfers between devices  21.8 us (30%)
  other arithmetic  1.35 us (2%)
  between operations  0.82 us (1%)
    ppermute x11, waiting for transfers between devices, exchange(): return lax.ppermute(value, axis, [(i, i ^ by) for i in range(count)])  21.8 us
    pallas_call x4, Pallas kernels, vmem_call(): pl.pallas_call(kernel, in_specs=[pl.BlockSpec(memory_space=pltpu.SMEM)] *...  17 us
    ppermute x11, starting transfers between devices, exchange(): return lax.ppermute(value, axis, [(i, i ^ by) for i in range(count)])  16.7 us
    ppermute x4, starting transfers between devices, shifted(): return lax.ppermute(value, axis, pairs)  5.35 us
    pallas_call x2, Pallas kernels, pack(): pl.pallas_call(functools.partial(pack_kernel, layers, plane, n_col, specs...  5.24 us
    pallas_call x1, Pallas kernels, build(): pl.pallas_call(functools.partial(build_kernel, layers, width), grid_spec=...  3.36 us
  transfers between devices with their start and end apart: 15, of which 9 were waited for; matrix products, arithmetic and copies ran while one was open for 0% of the time, Pallas kernels for 25%

profile of v5, /device:TPU:0, one launch (start us, length us, event | category | flops | bytes accessed | tf_op | source)
XLA Modules:
  0.0 71.8 jit_solution(12853864266829264981)
XLA Ops:
  0.6 2.4 %pack.2 = (bf16[128,3328]{1,0:T(8,128)(2,1)S(1)}, bf16[128,3328]{1,0:T(8,128)(2,1)S(1)}, s32[3]{0:T(128)S(1)}) custom-call(bf16[3,128,4096]{2,1,0:T(8,128)(2,1)} %sens_ref.3), custom_call_target="tpu_custom_call" | custom-call | bytes 4194304 | tf_op jit(solution)/shard_map/pack/pallas_call | solution.py:114
  3.0 0.0 copy-start
  3.0 0.0 copy-start.1
  3.0 0.0 copy-start.2
  3.1 0.0 copy-start.3
  3.1 3.0 %collective-permute-start.2 = (bf16[128,3328]{1,0:T(8,128)(2,1)S(1)}, bf16[128,3328]{1,0:T(8,128)(2,1)S(1)}, u32[]{:S(2)}, u32[]{:S(2)}) collective-permute-start(bf16[128,3328]{1,0:T(8,128)(2,1)S(1)} %get-tuple-element.34), channel_id=1, source_target_pairs={{0,2},{1,3},{2,0},{3,1},{4,6},{5,7},{6,4},{7,5},{8,10},{9,11},{10,... | collective-permute-start | bytes 2555912 | tf_op jit(solution)/shard_map/ppermute | solution.py:18
  6.1 1.5 %collective-permute-start.6 = (bf16[128,3328]{1,0:T(8,128)(2,1)S(1)}, bf16[128,3328]{1,0:T(8,128)(2,1)S(1)}, u32[]{:S(2)}, u32[]{:S(2)}) collective-permute-start(bf16[128,3328]{1,0:T(8,128)(2,1)S(1)} %get-tuple-element.49), channel_id=1, source_target_pairs={{0,1},{1,0},{2,3},{3,2},{4,5},{5,4},{6,7},{7,6},{8,9},{9,8},{10,11... | collective-permute-start | bytes 2555912 | tf_op jit(solution)/shard_map/ppermute | solution.py:18
  7.6 2.9 %pack.3 = (bf16[128,1792]{1,0:T(8,128)(2,1)S(1)}, bf16[128,1536]{1,0:T(8,128)(2,1)S(1)}, bf16[128,1024]{1,0:T(8,128)(2,1)S(1)}, bf16[128,2304]{1,0:T(8,128)(2,1)S(1)}, s32[3]{0:T(128)S(1)}) custom-call(bf16[3,128,4096]{2,1,0:T(8,128)(2,1)} %sens_ref.3, s32[3]{0:T(128)S(1)} %get-tuple-element.30.refs_0_), custom_call_target="tpu_custom_call" | custom-call | bytes 4194304 | tf_op jit(solution)/shard_map/pack/pallas_call | solution.py:114
  10.5 1.3 %collective-permute-start.3 = (bf16[128,1024]{1,0:T(8,128)(2,1)S(1)}, bf16[128,1024]{1,0:T(8,128)(2,1)S(1)}, u32[]{:S(2)}, u32[]{:S(2)}) collective-permute-start(bf16[128,1024]{1,0:T(8,128)(2,1)S(1)} %get-tuple-element.35.refs_0_), channel_id=1, source_target_pairs={{4,0},{8,4},{12,8},{16,12},{20,16},{24,20},{28,24},{5,1},{9,5},{13... | collective-permute-start | bytes 786440 | tf_op jit(solution)/shard_map/ppermute | solution.py:24
  11.8 0.1 collective-permute-start
  11.9 0.0 copy-done
  11.9 0.0 copy-done.1
  11.9 0.0 copy-done.2
  11.9 0.0 copy-done.3
  11.9 3.4 %build.1 = (bf16[2,16896,256]{2,1,0:T(8,128)(2,1)S(1)}, bf16[2,8,256,256]{3,2,1,0:T(8,128)(2,1)S(1)}, bf16[2,256,256]{2,1,0:T(8,128)(2,1)S(1)}, bf16[16,4096]{1,0:T(8,128)(2,1)S(1)}, f32[4,128]{1,0:T(4,128)S(1)}) custom-call(s32[3]{0:T(128)S(1)} %get-tuple-element.31.place.refs_0_, f32[6,4,1024]{2,1,0:T(4,128)S(1)} %copy-done.1, s32[4,1024]{1,0:T(4,128)S(1)} %copy-done.2, ...), custom_call_target="tpu_custom_call" | custom-call | bytes 12582912 | tf_op jit(solution)/shard_map/build/pallas_call | solution.py:302
  15.3 0.0 collective-permute-done.3.refs_2_
  15.3 3.5 %image.4 = (bf16[256,4096]{1,0:T(8,128)(2,1)S(1)}, bf16[256,4096]{1,0:T(8,128)(2,1)S(1)}, bf16[4096,256]{1,0:T(8,128)(2,1)S(1)}, bf16[4096,256]{1,0:T(8,128)(2,1)S(1)}, f32[1,128,128]{2,1,0:T(8,128)S(1)}) custom-call(bf16[128,1024]{1,0:T(8,128)(2,1)S(1)} %get-tuple-element.35.refs_0_, bf16[128,2304]{1,0:T(8,128)(2,1)S(1)} %get-tuple-element.36.refs_1_, ...), custom_call_target="tpu_custom_call" | custom-call | bytes 16777216 | tf_op jit(solution)/shard_map/image/pallas_call | solution.py:469
  18.8 6.2 %collective-permute-done.2.piece_ref.refs_0_ = bf16[128,3328]{1,0:T(8,128)(2,1)S(1)} collective-permute-done((bf16[128,3328]{1,0:T(8,128)(2,1)S(1)}, bf16[128,3328]{1,0:T(8,128)(2,1)S(1)}, u32[]{:S(2)}, u32[]{:S(2)}) %collective-permute-start.2) | collective-permute-done | bytes 852000 | tf_op jit(solution)/shard_map/ppermute | solution.py:18
  25.1 1.3 %collective-permute-start.4 = (bf16[128,1024]{1,0:T(8,128)(2,1)S(1)}, bf16[128,1024]{1,0:T(8,128)(2,1)S(1)}, u32[]{:S(2)}, u32[]{:S(2)}) collective-permute-start(bf16[128,1024]{1,0:T(8,128)(2,1)S(1)} %crop.3), channel_id=1, source_target_pairs={{4,0},{8,4},{12,8},{16,12},{20,16},{24,20},{28,24},{5,1},{9,5},{13... | collective-permute-start | bytes 786440 | tf_op jit(solution)/shard_map/ppermute | solution.py:24
  26.4 3.0 %collective-permute-start.1 = (bf16[128,1536]{1,0:T(8,128)(2,1)S(1)}, bf16[128,1536]{1,0:T(8,128)(2,1)S(1)}, u32[]{:S(2)}, u32[]{:S(2)}) collective-permute-start(bf16[128,1536]{1,0:T(8,128)(2,1)S(1)} %get-tuple-element.33), channel_id=1, source_target_pairs={{0,3},{1,2},{2,1},{3,0},{4,7},{5,6},{6,5},{7,4},{8,11},{9,10},{10,... | collective-permute-start | bytes 1179656 | tf_op jit(solution)/shard_map/ppermute | solution.py:18
  29.4 0.0 collective-permute-done.6.piece_ref.refs_0_
  29.4 1.3 %collective-permute-start.7 = (bf16[128,1024]{1,0:T(8,128)(2,1)S(1)}, bf16[128,1024]{1,0:T(8,128)(2,1)S(1)}, u32[]{:S(2)}, u32[]{:S(2)}) collective-permute-start(bf16[128,1024]{1,0:T(8,128)(2,1)S(1)} %crop.5), channel_id=1, source_target_pairs={{4,0},{8,4},{12,8},{16,12},{20,16},{24,20},{28,24},{5,1},{9,5},{13... | collective-permute-start | bytes 786440 | tf_op jit(solution)/shard_map/ppermute | solution.py:24
  30.7 0.0 collective-permute-done.4.refs_1_
  30.7 4.3 %image.5 = (bf16[256,4096]{1,0:T(8,128)(2,1)S(1)}, bf16[256,4096]{1,0:T(8,128)(2,1)S(1)}, bf16[4096,256]{1,0:T(8,128)(2,1)S(1)}, bf16[4096,256]{1,0:T(8,128)(2,1...) custom-call(bf16[128,3328]{1,0:T(8,128)(2,1)S(1)} %collective-permut, ...), custom_call_target="tpu_custom_call", output_to_operand_aliasing={{0}: (6, {}), {1}: (7, {}), {2}: (8, {}), {3}: (9, {})} | custom-call | bytes 16777216 | tf_op jit(solution)/shard_map/image/pallas_call | solution.py:469
  35.0 2.3 %collective-permute-done.piece_ref.refs_1_ = bf16[128,1792]{1,0:T(8,128)(2,1)S(1)} collective-permute-done((bf16[128,1792]{1,0:T(8,128)(2,1)S(1)}, bf16[128,1792]{1,0:T(8,128)(2,1)S(1)}, u32[]{:S(2)}, u32[]{:S(2)}) %collective-permute-start) | collective-permute-done | bytes 458784 | tf_op jit(solution)/shard_map/ppermute | solution.py:18
  37.3 1.5 %collective-permute-start.5 = (bf16[128,1024]{1,0:T(8,128)(2,1)S(1)}, bf16[128,1024]{1,0:T(8,128)(2,1)S(1)}, u32[]{:S(2)}, u32[]{:S(2)}) collective-permute-start(bf16[128,1024]{1,0:T(8,128)(2,1)S(1)} %crop.4), channel_id=1, source_target_pairs={{4,0},{8,4},{12,8},{16,12},{20,16},{24,20},{28,24},{5,1},{9,5},{13... | collective-permute-start | bytes 786440 | tf_op jit(solution)/shard_map/ppermute | solution.py:24
  38.8 0.0 collective-permute-done.7.refs_1_
  38.8 3.9 %image.6 = (bf16[256,4096]{1,0:T(8,128)(2,1)S(1)}, bf16[256,4096]{1,0:T(8,128)(2,1)S(1)}, f32[3,128,128]{2,1,0:T(8,128)S(1)}) custom-call(bf16[128,3328]{1,0:T(8,128)(2,1)S(1)} %collective-permute-done.6.piece_ref.refs_0_, bf16[128,1024]{1,0:T(8,128)(2,1)S(1)} %collective-permute-done.7.refs_1_, ...), custom_call_target="tpu_custom_call" | custom-call | bytes 16777216 | tf_op jit(solution)/shard_map/image/pallas_call | solution.py:469
  42.6 1.9 %collective-permute-done.1.refs_2_ = bf16[128,1536]{1,0:T(8,128)(2,1)S(1)} collective-permute-done((bf16[128,1536]{1,0:T(8,128)(2,1)S(1)}, bf16[128,1536]{1,0:T(8,128)(2,1)S(1)}, u32[]{:S(2)}, u32[]{:S(2)}) %collective-permute-start.1) | collective-permute-done | bytes 393248 | tf_op jit(solution)/shard_map/ppermute | solution.py:18
  44.6 0.0 collective-permute-done.5.refs_3_
  44.6 5.4 %image.7 = (bf16[256,4096]{1,0:T(8,128)(2,1)S(1)}, bf16[256,4096]{1,0:T(8,128)(2,1)S(1)}, f32[264,512]{1,0:T(8,128)S(1)}, f32[264,512]{1,0:T(8,128)S(1)}) custom-call(s32[3]{0:T(128)S(1)} %get-tuple-element.31.place.refs_0_, bf16[128,1792]{1,0:T(8,128)(2,1)S(1)} %collective-permute-done.piece_ref.refs_1_, ...), custom_call_target="tpu_custom_call", output_to_operand_aliasing={{0}: (15, {}), {1}: (16, {})} | custom-call | bytes 16777216 | tf_op jit(solution)/shard_map/image/pallas_call | solution.py:469
  50.0 1.0 %collective-permute-start.8 = (f32[264,512]{1,0:T(8,128)S(1)}, f32[264,512]{1,0:T(8,128)S(1)}, u32[]{:S(2)}, u32[]{:S(2)}) collective-permute-start(f32[264,512]{1,0:T(8,128)S(1)} %get-tuple-element.56), channel_id=1, source_target_pairs={{0,4},{4,0},{8,12},{12,8},{16,20},{20,16},{24,28},{28,24},{1,5},{5... | collective-permute-start | bytes 1622024 | tf_op jit(solution)/shard_map/ppermute | solution.py:18
  50.9 1.6 %collective-permute-done.8 = f32[264,512]{1,0:T(8,128)S(1)} collective-permute-done((f32[264,512]{1,0:T(8,128)S(1)}, f32[264,512]{1,0:T(8,128)S(1)}, u32[]{:S(2)}, u32[]{:S(2)}) %collective-permute-start.8) | collective-permute-done | bytes 540704 | tf_op jit(solution)/shard_map/ppermute | solution.py:18
  52.5 0.1 add.30
  52.6 2.5 %collective-permute-start.11 = (f32[264,128]{1,0:T(8,128)S(1)}, f32[264,128]{1,0:T(8,128)S(1)}, u32[]{:S(2)}, u32[]{:S(2)}) collective-permute-start(f32[264,128]{1,0:T(8,128)S(1)} %get-tuple-element.58), channel_id=1, source_target_pairs={{0,3},{1,2},{2,1},{3,0},{4,7},{5,6},{6,5},{7,4},{8,11},{9,10},{10,... | collective-permute-start | bytes 405512 | tf_op jit(solution)/shard_map/ppermute | solution.py:18
  55.2 0.5 collective-permute-start.10
  55.6 0.6 collective-permute-start.9
  56.2 3.6 %collective-permute-done.11 = f32[264,128]{1,0:T(8,128)S(1)} collective-permute-done((f32[264,128]{1,0:T(8,128)S(1)}, f32[264,128]{1,0:T(8,128)S(1)}, u32[]{:S(2)}, u32[]{:S(2)}) %collective-permute-start.11) | collective-permute-done | bytes 135200 | tf_op jit(solution)/shard_map/ppermute | solution.py:18
  59.8 2.5 %collective-permute-done.10 = f32[264,128]{1,0:T(8,128)S(1)} collective-permute-done((f32[264,128]{1,0:T(8,128)S(1)}, f32[264,128]{1,0:T(8,128)S(1)}, u32[]{:S(2)}, u32[]{:S(2)}) %collective-permute-start.10) | collective-permute-done | bytes 135200 | tf_op jit(solution)/shard_map/ppermute | solution.py:18
  62.4 0.1 collective-permute-done.9
  62.5 3.0 %collective-permute-start.14 = (f32[72,128]{1,0:T(8,128)S(1)}, f32[72,128]{1,0:T(8,128)S(1)}, u32[]{:S(2)}, u32[]{:S(2)}) collective-permute-start(f32[72,128]{1,0:T(8,128)S(1)} %concatenate.12), channel_id=1, source_target_pairs={{0,24},{4,28},{8,16},{12,20},{16,8},{20,12},{24,0},{28,4},{1,25},{... | collective-permute-start | bytes 110600 | tf_op jit(solution)/shard_map/ppermute | solution.py:18
  65.6 0.1 collective-permute-start.13
  65.6 1.4 %collective-permute-start.12 = (f32[72,128]{1,0:T(8,128)S(1)}, f32[72,128]{1,0:T(8,128)S(1)}, u32[]{:S(2)}, u32[]{:S(2)}) collective-permute-start(f32[72,128]{1,0:T(8,128)S(1)} %get-tuple-element.64), channel_id=1, source_target_pairs={{0,8},{4,12},{8,0},{12,4},{16,24},{20,28},{24,16},{28,20},{1,9},{5... | collective-permute-start | bytes 110600 | tf_op jit(solution)/shard_map/ppermute | solution.py:18
  67.0 1.5 %collective-permute-done.14 = f32[72,128]{1,0:T(8,128)S(1)} collective-permute-done((f32[72,128]{1,0:T(8,128)S(1)}, f32[72,128]{1,0:T(8,128)S(1)}, u32[]{:S(2)}, u32[]{:S(2)}) %collective-permute-start.14) | collective-permute-done | bytes 36896 | tf_op jit(solution)/shard_map/ppermute | solution.py:18
  68.5 2.1 %collective-permute-done.13 = f32[72,128]{1,0:T(8,128)S(1)} collective-permute-done((f32[72,128]{1,0:T(8,128)S(1)}, f32[72,128]{1,0:T(8,128)S(1)}, u32[]{:S(2)}, u32[]{:S(2)}) %collective-permute-start.13) | collective-permute-done | bytes 36896 | tf_op jit(solution)/shard_map/ppermute | solution.py:18
  70.5 0.0 collective-permute-done.12
  70.5 0.6 multiply_bitcast_fusion
  71.1 0.6 fusion.2
  (10 shorter events, 0.2 us)
Async XLA Ops:
  3.0 8.9 %copy-start = (bf16[3,4096]{1,0:T(4,128)(2,1)S(1)}, bf16[3,4096]{1,0:T(4,128)(2,1)}, u32[]{:S(2)}) copy-start(bf16[3,4096]{1,0:T(4,128)(2,1)} %refs_3_.1) | copy-start | bytes 73732
  3.0 8.9 %copy-start.1 = (f32[6,4,1024]{2,1,0:T(4,128)S(1)}, f32[6,4,1024]{2,1,0:T(4,128)}, u32[]{:S(2)}) copy-start(f32[6,4,1024]{2,1,0:T(4,128)} %moments_ref.1) | copy-start | bytes 294916
  3.0 8.9 %copy-start.2 = (s32[4,1024]{1,0:T(4,128)S(1)}, s32[4,1024]{1,0:T(4,128)}, u32[]{:S(2)}) copy-start(s32[4,1024]{1,0:T(4,128)} %label_ref.1) | copy-start | bytes 49156
  3.1 8.9 %copy-start.3 = (f32[4,1024]{1,0:T(4,128)S(1)}, f32[4,1024]{1,0:T(4,128)}, u32[]{:S(2)}) copy-start(f32[4,1024]{1,0:T(4,128)} %misfit_ref.1) | copy-start | bytes 49156
  3.1 22.0 %collective-permute-start.2 = (bf16[128,3328]{1,0:T(8,128)(2,1)S(1)}, bf16[128,3328]{1,0:T(8,128)(2,1)S(1)}, u32[]{:S(2)}, u32[]{:S(2)}) collective-permute-start(bf16[128,3328]{1,0:T(8,128)(2,1)S(1)} %get-tuple-element.34), channel_id=1, source_target_pairs={{0,2},{1,3},{2,0},{3,1},{4,6},{5,7},{6,4},{7,5},{8,10},{9,11},{10,... | collective-permute-start | bytes 2555912 | tf_op jit(solution)/shard_map/ppermute | solution.py:18
  6.1 23.3 %collective-permute-start.6 = (bf16[128,3328]{1,0:T(8,128)(2,1)S(1)}, bf16[128,3328]{1,0:T(8,128)(2,1)S(1)}, u32[]{:S(2)}, u32[]{:S(2)}) collective-permute-start(bf16[128,3328]{1,0:T(8,128)(2,1)S(1)} %get-tuple-element.49), channel_id=1, source_target_pairs={{0,1},{1,0},{2,3},{3,2},{4,5},{5,4},{6,7},{7,6},{8,9},{9,8},{10,11... | collective-permute-start | bytes 2555912 | tf_op jit(solution)/shard_map/ppermute | solution.py:18
  10.5 4.8 %collective-permute-start.3 = (bf16[128,1024]{1,0:T(8,128)(2,1)S(1)}, bf16[128,1024]{1,0:T(8,128)(2,1)S(1)}, u32[]{:S(2)}, u32[]{:S(2)}) collective-permute-start(bf16[128,1024]{1,0:T(8,128)(2,1)S(1)} %get-tuple-element.35.refs_0_), channel_id=1, source_target_pairs={{4,0},{8,4},{12,8},{16,12},{20,16},{24,20},{28,24},{5,1},{9,5},{13... | collective-permute-start | bytes 786440 | tf_op jit(solution)/shard_map/ppermute | solution.py:24
  11.8 25.5 %collective-permute-start = (bf16[128,1792]{1,0:T(8,128)(2,1)S(1)}, bf16[128,1792]{1,0:T(8,128)(2,1)S(1)}, u32[]{:S(2)}, u32[]{:S(2)}) collective-permute-start(bf16[128,1792]{1,0:T(8,128)(2,1)S(1)} %get-tuple-element.32), channel_id=1, source_target_pairs={{0,3},{1,2},{2,1},{3,0},{4,7},{5,6},{6,5},{7,4},{8,11},{9,10},{10,... | collective-permute-start | bytes 1376264 | tf_op jit(solution)/shard_map/ppermute | solution.py:18
  25.1 5.6 %collective-permute-start.4 = (bf16[128,1024]{1,0:T(8,128)(2,1)S(1)}, bf16[128,1024]{1,0:T(8,128)(2,1)S(1)}, u32[]{:S(2)}, u32[]{:S(2)}) collective-permute-start(bf16[128,1024]{1,0:T(8,128)(2,1)S(1)} %crop.3), channel_id=1, source_target_pairs={{4,0},{8,4},{12,8},{16,12},{20,16},{24,20},{28,24},{5,1},{9,5},{13... | collective-permute-start | bytes 786440 | tf_op jit(solution)/shard_map/ppermute | solution.py:24
  26.4 18.2 %collective-permute-start.1 = (bf16[128,1536]{1,0:T(8,128)(2,1)S(1)}, bf16[128,1536]{1,0:T(8,128)(2,1)S(1)}, u32[]{:S(2)}, u32[]{:S(2)}) collective-permute-start(bf16[128,1536]{1,0:T(8,128)(2,1)S(1)} %get-tuple-element.33), channel_id=1, source_target_pairs={{0,3},{1,2},{2,1},{3,0},{4,7},{5,6},{6,5},{7,4},{8,11},{9,10},{10,... | collective-permute-start | bytes 1179656 | tf_op jit(solution)/shard_map/ppermute | solution.py:18
  29.4 9.4 %collective-permute-start.7 = (bf16[128,1024]{1,0:T(8,128)(2,1)S(1)}, bf16[128,1024]{1,0:T(8,128)(2,1)S(1)}, u32[]{:S(2)}, u32[]{:S(2)}) collective-permute-start(bf16[128,1024]{1,0:T(8,128)(2,1)S(1)} %crop.5), channel_id=1, source_target_pairs={{4,0},{8,4},{12,8},{16,12},{20,16},{24,20},{28,24},{5,1},{9,5},{13... | collective-permute-start | bytes 786440 | tf_op jit(solution)/shard_map/ppermute | solution.py:24
  37.3 7.3 %collective-permute-start.5 = (bf16[128,1024]{1,0:T(8,128)(2,1)S(1)}, bf16[128,1024]{1,0:T(8,128)(2,1)S(1)}, u32[]{:S(2)}, u32[]{:S(2)}) collective-permute-start(bf16[128,1024]{1,0:T(8,128)(2,1)S(1)} %crop.4), channel_id=1, source_target_pairs={{4,0},{8,4},{12,8},{16,12},{20,16},{24,20},{28,24},{5,1},{9,5},{13... | collective-permute-start | bytes 786440 | tf_op jit(solution)/shard_map/ppermute | solution.py:24
  50.0 2.6 %collective-permute-start.8 = (f32[264,512]{1,0:T(8,128)S(1)}, f32[264,512]{1,0:T(8,128)S(1)}, u32[]{:S(2)}, u32[]{:S(2)}) collective-permute-start(f32[264,512]{1,0:T(8,128)S(1)} %get-tuple-element.56), channel_id=1, source_target_pairs={{0,4},{4,0},{8,12},{12,8},{16,20},{20,16},{24,28},{28,24},{1,5},{5... | collective-permute-start | bytes 1622024 | tf_op jit(solution)/shard_map/ppermute | solution.py:18
  52.6 7.2 %collective-permute-start.11 = (f32[264,128]{1,0:T(8,128)S(1)}, f32[264,128]{1,0:T(8,128)S(1)}, u32[]{:S(2)}, u32[]{:S(2)}) collective-permute-start(f32[264,128]{1,0:T(8,128)S(1)} %get-tuple-element.58), channel_id=1, source_target_pairs={{0,3},{1,2},{2,1},{3,0},{4,7},{5,6},{6,5},{7,4},{8,11},{9,10},{10,... | collective-permute-start | bytes 405512 | tf_op jit(solution)/shard_map/ppermute | solution.py:18
  55.2 7.2 %collective-permute-start.10 = (f32[264,128]{1,0:T(8,128)S(1)}, f32[264,128]{1,0:T(8,128)S(1)}, u32[]{:S(2)}, u32[]{:S(2)}) collective-permute-start(f32[264,128]{1,0:T(8,128)S(1)} %get-tuple-element.59), channel_id=1, source_target_pairs={{0,2},{1,3},{2,0},{3,1},{4,6},{5,7},{6,4},{7,5},{8,10},{9,11},{10,... | collective-permute-start | bytes 405512 | tf_op jit(solution)/shard_map/ppermute | solution.py:18
  55.6 6.8 %collective-permute-start.9 = (f32[264,128]{1,0:T(8,128)S(1)}, f32[264,128]{1,0:T(8,128)S(1)}, u32[]{:S(2)}, u32[]{:S(2)}) collective-permute-start(f32[264,128]{1,0:T(8,128)S(1)} %get-tuple-element.57), channel_id=1, source_target_pairs={{0,1},{1,0},{2,3},{3,2},{4,5},{5,4},{6,7},{7,6},{8,9},{9,8},{10,11... | collective-permute-start | bytes 405512 | tf_op jit(solution)/shard_map/ppermute | solution.py:18
  62.5 5.9 %collective-permute-start.14 = (f32[72,128]{1,0:T(8,128)S(1)}, f32[72,128]{1,0:T(8,128)S(1)}, u32[]{:S(2)}, u32[]{:S(2)}) collective-permute-start(f32[72,128]{1,0:T(8,128)S(1)} %concatenate.12), channel_id=1, source_target_pairs={{0,24},{4,28},{8,16},{12,20},{16,8},{20,12},{24,0},{28,4},{1,25},{... | collective-permute-start | bytes 110600 | tf_op jit(solution)/shard_map/ppermute | solution.py:18
  65.6 5.0 %collective-permute-start.13 = (f32[72,128]{1,0:T(8,128)S(1)}, f32[72,128]{1,0:T(8,128)S(1)}, u32[]{:S(2)}, u32[]{:S(2)}) collective-permute-start(f32[72,128]{1,0:T(8,128)S(1)} %get-tuple-element.65), channel_id=1, source_target_pairs={{0,16},{4,20},{8,24},{12,28},{16,0},{20,4},{24,8},{28,12},{1,17},{... | collective-permute-start | bytes 110600 | tf_op jit(solution)/shard_map/ppermute | solution.py:18
  65.6 4.9 %collective-permute-start.12 = (f32[72,128]{1,0:T(8,128)S(1)}, f32[72,128]{1,0:T(8,128)S(1)}, u32[]{:S(2)}, u32[]{:S(2)}) collective-permute-start(f32[72,128]{1,0:T(8,128)S(1)} %get-tuple-element.64), channel_id=1, source_target_pairs={{0,8},{4,12},{8,0},{12,4},{16,24},{20,28},{24,16},{28,20},{1,9},{5... | collective-permute-start | bytes 110600 | tf_op jit(solution)/shard_map/ppermute | solution.py:18

commit v6 on v4

--- a/solution.py
+++ b/solution.py
@@ -376,19 +376,18 @@
     return lax.dot_general(a, b, (((1,), (1,)), ((), ())), preferred_element_type=jnp.float32)
 
 
-def products(held, values_ref, image_ref, slot):
+def products(held, first, values_ref, image_ref, slot):
     rows = values_ref.shape[0] // 2
     value, image = (ref[slot * rows : (slot + 1) * rows] for ref in (values_ref, image_ref))
     found = []
     for v, i in held:
-        both = product(image, v[...]) + product(value, i[...])
+        both = jnp.dot(image, v[...], preferred_element_type=jnp.float32)
+        both += jnp.dot(value, i[...], preferred_element_type=jnp.float32)
         found += [both[:, :rows], both[:, rows:]]
     if slot:
-        both = product(image, values_ref[...])
-        found.append(both[:, :rows] + product(value, image_ref[:rows]))
-        own = both[:, rows:]
-    else:
-        own = product(image, value)
+        both = jnp.dot(image, first[0][:, :rows], preferred_element_type=jnp.float32)
+        found.append(both + jnp.dot(value, first[1][:, :rows], preferred_element_type=jnp.float32))
+    own = product(image, value)
     return [*found, own + own.T]
 
 
@@ -406,22 +405,28 @@
     top_ref, *matrix, force_ref = (refs.pop(0) for _ in range(5))
     held = [(refs.pop(0), refs.pop(0)) for _ in range(pair)]
     block_refs = [refs.pop(0) for _ in range(len(order) - 1 if last else 0)]
-    grad_refs = [refs.pop(0) for _ in range(pair if last else 0)]
+    grad_refs = [refs.pop(0) for _ in range(len(order) - 1 if last else 0)]
     zone_ref = refs.pop(0) if last else None
-    values_ref, image_ref, *outs = refs[2 * slot :]
+    first = [refs.pop(0) for _ in range(2 if last else 0)]
+    values_ref, image_ref, *outs = refs[(2 if last else 4) * slot :]
+    if not last:
+        first, outs = outs[:2], outs[2:]
     rows = values_ref.shape[0] // 2
     part = slice(slot * rows, (slot + 1) * rows)
     fill(layers, width, pieces, top_ref, values_ref.at[part])
     image_layers(layers, width, values_ref.at[part], image_ref.at[part], matrix)
-    found = products(held, values_ref, image_ref, slot)
+    found = products(held, first, values_ref, image_ref, slot)
     nodes = slice(0, 3 * layers * width)
-    grad = product(force_ref[:, nodes], values_ref[:, nodes])[:8] if slot else None
     if not last:
+        step = min(2 * TILE, width)
+        for start in range(0, values_ref.shape[1], step):
+            for ref, to in zip((values_ref, image_ref), first):
+                to[start : start + step, part] = ref[part, start : start + step].T
         for j, value in enumerate(found):
             outs[0][j] = value
-        if slot:
-            outs[1][...] = grad
+        outs[1][...] = jnp.dot(force_ref[:, nodes], first[0][nodes, part], preferred_element_type=jnp.float32)[:8]
         return
+    grad = product(force_ref[:, nodes], values_ref[part, nodes])[:8]
     keep_ref, send_ref = outs
     half, blocks = rows // 2, len(order)
     pairs = [(i, j) for i in order for j in order]
@@ -429,9 +434,8 @@
     row = lax.broadcasted_iota(jnp.int32, (blocks, rows), 0)
     small = jnp.zeros((blocks, rows), jnp.float32)
     grads = [*(r[...] for r in grad_refs), grad]
-    for j, name in enumerate(order):
-        value = grads[j // 2][:1, j % 2 * rows : (j % 2 + 1) * rows]
-        small = jnp.where(row == (place[0] ^ name), jnp.broadcast_to(value, (blocks, rows)), small)
+    for name, value in zip(order, grads):
+        small = jnp.where(row == (place[0] ^ name), jnp.broadcast_to(value[:1], (blocks, rows)), small)
     for j in range(blocks):
         columns = slice(j * rows, (j + 1) * rows)
         for ref in (keep_ref, send_ref):
@@ -510,36 +514,36 @@
         slot = len(seen) % 2
         seen.append(k)
         args = [*pieces[k], top, *matrix, *(x for pair in held for x in pair)]
-        outs = [two, two]
+        outs, scalars, aliases = [two, two], [], {}
         if k == last:
-            args += [*blocks, *grads, zone]
+            scalars = [place]
+            args += [*blocks, *grads, zone, *current[2:]]
+            current = current[:2]
             outs += [wide, wide]
         else:
-            outs.append(pltpu.VMEM((len(seen), cols, cols), jnp.float32))
-            outs += [pltpu.VMEM((8, 2 * cols), jnp.float32)] * slot
-        scalars, aliases = [place] * (k == last), {}
+            tall = pltpu.VMEM((total, 2 * cols), jnp.bfloat16)
+            outs += [tall, tall, pltpu.VMEM((len(seen), cols, cols), jnp.float32), pltpu.VMEM((8, cols), jnp.float32)]
         if slot:
-            aliases = {len(scalars) + len(args) + i: i for i in range(2)}
+            aliases = {len(scalars) + len(args) + i: i for i in range(len(current))}
             args += current
         kernel = functools.partial(image_kernel, layers, lanes, len(pieces[k]), tuple(seen), k == last)
         out = vmem_call(kernel, scalars, args, outs, (), aliases)
         if k == last:
             keep, send = out[2:]
         else:
-            out = [in_vmem(x) for x in out]
-            current = out[:2]
-            blocks.append(out[2])
-            grads += out[3:]
-            held += [current] * slot
+            *current, block, grad = [in_vmem(x) for x in out]
+            blocks.append(block)
+            grads.append(grad)
+            held += [current[2:]] * slot
 
     mine = keep + exchange(send, "slab", 1)
     parts = [mine[:, k * cols : (k + 1) * cols] for k in range(n_col)]
     mine = parts[0]
-    for k in (order[0], *order[:0:-1]):
+    for k in range(1, n_col):
         mine = mine + exchange(parts[k], "col", k)
     half, rows = cols // 2, width // 2
     parts = [jnp.concatenate([mine[k * half : (k + 1) * half], mine[rows:]]) for k in range(n_col)]
-    parts = [parts[0]] + [exchange(parts[k], "slab", 2 * k) for k in (1, *range(n_col - 1, 1, -1))]
+    parts = [parts[0]] + [exchange(parts[k], "slab", 2 * k) for k in range(1, n_col)]
     hessian = sum(part[:half] for part in parts).T
     both = sum(part[half:] for part in parts).reshape(2, width)
     gradient = both[0]

time: 73.2 us -> 71.8 us (0.981)
  Pallas kernels: 26.8 us -> 25.9 us
    pallas_call x4, Pallas kernels: 18.1 us -> 17.3 us  [vmem_call(): pl.pallas_call(kernel, in_specs=[pl.BlockSpec(memory_space=pltpu.SMEM)] *...]
  transfers between devices with their start and end apart: 15 -> 15, of which waited for: 10 -> 9; matrix products, arithmetic and copies ran while one was open for 0% -> 0% of each run, Pallas kernels for 25% -> 26%
where the time goes in v6:
time: 71.8 us; the launch traced here: 71.6 us
  Pallas kernels  25.9 us (36%)
  starting transfers between devices  22 us (31%)
  waiting for transfers between devices  21.4 us (30%)
  other arithmetic  1.36 us (2%)
  between operations  0.83 us (1%)
    ppermute x11, waiting for transfers between devices, exchange(): return lax.ppermute(value, axis, [(i, i ^ by) for i in range(count)])  21.4 us
    pallas_call x4, Pallas kernels, vmem_call(): pl.pallas_call(kernel, in_specs=[pl.BlockSpec(memory_space=pltpu.SMEM)] *...  17.3 us
    ppermute x11, starting transfers between devices, exchange(): return lax.ppermute(value, axis, [(i, i ^ by) for i in range(count)])  16.7 us
    ppermute x4, starting transfers between devices, shifted(): return lax.ppermute(value, axis, pairs)  5.35 us
    pallas_call x2, Pallas kernels, pack(): pl.pallas_call(functools.partial(pack_kernel, layers, plane, n_col, specs...  5.24 us
    pallas_call x1, Pallas kernels, build(): pl.pallas_call(functools.partial(build_kernel, layers, width), grid_spec=...  3.36 us
  transfers between devices with their start and end apart: 15, of which 9 were waited for; matrix products, arithmetic and copies ran while one was open for 0% of the time, Pallas kernels for 26%

profile of v6, /device:TPU:0, one launch (start us, length us, event | category | flops | bytes accessed | tf_op | source)
XLA Modules:
  0.0 71.6 jit_solution(7147677940474041304)
XLA Ops:
  0.6 2.4 %pack.2 = (bf16[128,3328]{1,0:T(8,128)(2,1)S(1)}, bf16[128,3328]{1,0:T(8,128)(2,1)S(1)}, s32[3]{0:T(128)S(1)}) custom-call(bf16[3,128,4096]{2,1,0:T(8,128)(2,1)} %sens_ref.3), custom_call_target="tpu_custom_call" | custom-call | bytes 4194304 | tf_op jit(solution)/shard_map/pack/pallas_call | solution.py:114
  3.0 0.0 copy-start
  3.0 0.0 copy-start.1
  3.0 0.0 copy-start.2
  3.1 0.0 copy-start.3
  3.1 3.0 %collective-permute-start.2 = (bf16[128,3328]{1,0:T(8,128)(2,1)S(1)}, bf16[128,3328]{1,0:T(8,128)(2,1)S(1)}, u32[]{:S(2)}, u32[]{:S(2)}) collective-permute-start(bf16[128,3328]{1,0:T(8,128)(2,1)S(1)} %get-tuple-element.38), channel_id=1, source_target_pairs={{0,2},{1,3},{2,0},{3,1},{4,6},{5,7},{6,4},{7,5},{8,10},{9,11},{10,... | collective-permute-start | bytes 2555912 | tf_op jit(solution)/shard_map/ppermute | solution.py:18
  6.1 1.5 %collective-permute-start.6 = (bf16[128,3328]{1,0:T(8,128)(2,1)S(1)}, bf16[128,3328]{1,0:T(8,128)(2,1)S(1)}, u32[]{:S(2)}, u32[]{:S(2)}) collective-permute-start(bf16[128,3328]{1,0:T(8,128)(2,1)S(1)} %get-tuple-element.53), channel_id=1, source_target_pairs={{0,1},{1,0},{2,3},{3,2},{4,5},{5,4},{6,7},{7,6},{8,9},{9,8},{10,11... | collective-permute-start | bytes 2555912 | tf_op jit(solution)/shard_map/ppermute | solution.py:18
  7.6 2.9 %pack.3 = (bf16[128,1792]{1,0:T(8,128)(2,1)S(1)}, bf16[128,1536]{1,0:T(8,128)(2,1)S(1)}, bf16[128,1024]{1,0:T(8,128)(2,1)S(1)}, bf16[128,2304]{1,0:T(8,128)(2,1)S(1)}, s32[3]{0:T(128)S(1)}) custom-call(bf16[3,128,4096]{2,1,0:T(8,128)(2,1)} %sens_ref.3, s32[3]{0:T(128)S(1)} %get-tuple-element.34.refs_0_), custom_call_target="tpu_custom_call" | custom-call | bytes 4194304 | tf_op jit(solution)/shard_map/pack/pallas_call | solution.py:114
  10.5 1.3 %collective-permute-start.3 = (bf16[128,1024]{1,0:T(8,128)(2,1)S(1)}, bf16[128,1024]{1,0:T(8,128)(2,1)S(1)}, u32[]{:S(2)}, u32[]{:S(2)}) collective-permute-start(bf16[128,1024]{1,0:T(8,128)(2,1)S(1)} %get-tuple-element.39.refs_0_), channel_id=1, source_target_pairs={{4,0},{8,4},{12,8},{16,12},{20,16},{24,20},{28,24},{5,1},{9,5},{13... | collective-permute-start | bytes 786440 | tf_op jit(solution)/shard_map/ppermute | solution.py:24
  11.8 0.1 collective-permute-start
  11.9 0.0 copy-done
  11.9 0.0 copy-done.1
  11.9 0.0 copy-done.2
  11.9 0.0 copy-done.3
  11.9 3.4 %build.1 = (bf16[2,16896,256]{2,1,0:T(8,128)(2,1)S(1)}, bf16[2,8,256,256]{3,2,1,0:T(8,128)(2,1)S(1)}, bf16[2,256,256]{2,1,0:T(8,128)(2,1)S(1)}, bf16[16,4096]{1,0:T(8,128)(2,1)S(1)}, f32[4,128]{1,0:T(4,128)S(1)}) custom-call(s32[3]{0:T(128)S(1)} %get-tuple-element.35.place.refs_0_, f32[6,4,1024]{2,1,0:T(4,128)S(1)} %copy-done.1, s32[4,1024]{1,0:T(4,128)S(1)} %copy-done.2, ...), custom_call_target="tpu_custom_call" | custom-call | bytes 12582912 | tf_op jit(solution)/shard_map/build/pallas_call | solution.py:302
  15.3 0.0 collective-permute-done.3.refs_2_
  15.3 3.6 %image.4 = (bf16[256,4096]{1,0:T(8,128)(2,1)S(1)}, bf16[256,4096]{1,0:T(8,128)(2,1)S(1)}, bf16[4096,256]{1,0:T(8,128)(2,1)S(1)}, bf16[4096,256]{1,0:T(8,128)(2,1...) custom-call(bf16[128,1024]{1,0:T(8,128)(2,1)S(1)} %get-tuple-element.39.refs_0_, ...), custom_call_target="tpu_custom_call" | custom-call | bytes 16777216 | tf_op jit(solution)/shard_map/image/pallas_call | solution.py:466
  18.9 6.1 %collective-permute-done.2.piece_ref.refs_0_ = bf16[128,3328]{1,0:T(8,128)(2,1)S(1)} collective-permute-done((bf16[128,3328]{1,0:T(8,128)(2,1)S(1)}, bf16[128,3328]{1,0:T(8,128)(2,1)S(1)}, u32[]{:S(2)}, u32[]{:S(2)}) %collective-permute-start.2) | collective-permute-done | bytes 852000 | tf_op jit(solution)/shard_map/ppermute | solution.py:18
  25.1 1.3 %collective-permute-start.4 = (bf16[128,1024]{1,0:T(8,128)(2,1)S(1)}, bf16[128,1024]{1,0:T(8,128)(2,1)S(1)}, u32[]{:S(2)}, u32[]{:S(2)}) collective-permute-start(bf16[128,1024]{1,0:T(8,128)(2,1)S(1)} %crop.3), channel_id=1, source_target_pairs={{4,0},{8,4},{12,8},{16,12},{20,16},{24,20},{28,24},{5,1},{9,5},{13... | collective-permute-start | bytes 786440 | tf_op jit(solution)/shard_map/ppermute | solution.py:24
  26.4 3.0 %collective-permute-start.1 = (bf16[128,1536]{1,0:T(8,128)(2,1)S(1)}, bf16[128,1536]{1,0:T(8,128)(2,1)S(1)}, u32[]{:S(2)}, u32[]{:S(2)}) collective-permute-start(bf16[128,1536]{1,0:T(8,128)(2,1)S(1)} %get-tuple-element.37), channel_id=1, source_target_pairs={{0,3},{1,2},{2,1},{3,0},{4,7},{5,6},{6,5},{7,4},{8,11},{9,10},{10,... | collective-permute-start | bytes 1179656 | tf_op jit(solution)/shard_map/ppermute | solution.py:18
  29.4 0.0 collective-permute-done.6.piece_ref.refs_0_
  29.4 1.3 %collective-permute-start.7 = (bf16[128,1024]{1,0:T(8,128)(2,1)S(1)}, bf16[128,1024]{1,0:T(8,128)(2,1)S(1)}, u32[]{:S(2)}, u32[]{:S(2)}) collective-permute-start(bf16[128,1024]{1,0:T(8,128)(2,1)S(1)} %crop.5), channel_id=1, source_target_pairs={{4,0},{8,4},{12,8},{16,12},{20,16},{24,20},{28,24},{5,1},{9,5},{13... | collective-permute-start | bytes 786440 | tf_op jit(solution)/shard_map/ppermute | solution.py:24
  30.7 0.0 collective-permute-done.4.refs_1_
  30.7 4.2 %image.5 = (bf16[256,4096]{1,0:T(8,128)(2,1)S(1)}, bf16[256,4096]{1,0:T(8,128)(2,1)S(1)}, bf16[4096,256]{1,0:T(8,128)(2,1)S(1)}, bf16[4096,256]{1,0:T(8,128)(2,1...) custom-call(bf16[128,3328]{1,0:T(8,128)(2,1)S(1)} %collective-permut, ...), custom_call_target="tpu_custom_call", output_to_operand_aliasing={{0}: (6, {}), {1}: (7, {}), {2}: (8, {}), {3}: (9, {})} | custom-call | bytes 16777216 | tf_op jit(solution)/shard_map/image/pallas_call | solution.py:466
  34.9 2.3 %collective-permute-done.piece_ref.refs_1_ = bf16[128,1792]{1,0:T(8,128)(2,1)S(1)} collective-permute-done((bf16[128,1792]{1,0:T(8,128)(2,1)S(1)}, bf16[128,1792]{1,0:T(8,128)(2,1)S(1)}, u32[]{:S(2)}, u32[]{:S(2)}) %collective-permute-start) | collective-permute-done | bytes 458784 | tf_op jit(solution)/shard_map/ppermute | solution.py:18
  37.3 1.5 %collective-permute-start.5 = (bf16[128,1024]{1,0:T(8,128)(2,1)S(1)}, bf16[128,1024]{1,0:T(8,128)(2,1)S(1)}, u32[]{:S(2)}, u32[]{:S(2)}) collective-permute-start(bf16[128,1024]{1,0:T(8,128)(2,1)S(1)} %crop.4), channel_id=1, source_target_pairs={{4,0},{8,4},{12,8},{16,12},{20,16},{24,20},{28,24},{5,1},{9,5},{13... | collective-permute-start | bytes 786440 | tf_op jit(solution)/shard_map/ppermute | solution.py:24
  38.8 0.0 collective-permute-done.7.refs_1_
  38.8 4.2 %image.6 = (bf16[256,4096]{1,0:T(8,128)(2,1)S(1)}, bf16[256,4096]{1,0:T(8,128)(2,1)S(1)}, bf16[4096,256]{1,0:T(8,128)(2,1)S(1)}, bf16[4096,256]{1,0:T(8,128)(2,1...) custom-call(bf16[128,3328]{1,0:T(8,128)(2,1)S(1)} %collective-permute-done.6.piece_ref.refs_0_, ...), custom_call_target="tpu_custom_call" | custom-call | bytes 16777216 | tf_op jit(solution)/shard_map/image/pallas_call | solution.py:466
  43.0 1.6 %collective-permute-done.1.refs_2_ = bf16[128,1536]{1,0:T(8,128)(2,1)S(1)} collective-permute-done((bf16[128,1536]{1,0:T(8,128)(2,1)S(1)}, bf16[128,1536]{1,0:T(8,128)(2,1)S(1)}, u32[]{:S(2)}, u32[]{:S(2)}) %collective-permute-start.1) | collective-permute-done | bytes 393248 | tf_op jit(solution)/shard_map/ppermute | solution.py:18
  44.6 0.0 collective-permute-done.5.refs_3_
  44.6 5.2 %image.7 = (bf16[256,4096]{1,0:T(8,128)(2,1)S(1)}, bf16[256,4096]{1,0:T(8,128)(2,1)S(1)}, f32[264,512]{1,0:T(8,128)S(1)}, f32[264,512]{1,0:T(8,128)S(1)}) custom-call(s32[3]{0:T(128)S(1)} %get-tuple-element.35.place.refs_0_, bf16[128,1792]{1,0:T(8,128)(2,1)S(1)} %collective-permute-done.piece_ref.refs_1_, ...), custom_call_target="tpu_custom_call", output_to_operand_aliasing={{0}: (19, {}), {1}: (20, {})} | custom-call | bytes 16777216 | tf_op jit(solution)/shard_map/image/pallas_call | solution.py:466
  49.8 1.0 %collective-permute-start.8 = (f32[264,512]{1,0:T(8,128)S(1)}, f32[264,512]{1,0:T(8,128)S(1)}, u32[]{:S(2)}, u32[]{:S(2)}) collective-permute-start(f32[264,512]{1,0:T(8,128)S(1)} %get-tuple-element.64), channel_id=1, source_target_pairs={{0,4},{4,0},{8,12},{12,8},{16,20},{20,16},{24,28},{28,24},{1,5},{5... | collective-permute-start | bytes 1622024 | tf_op jit(solution)/shard_map/ppermute | solution.py:18
  50.8 1.6 %collective-permute-done.8 = f32[264,512]{1,0:T(8,128)S(1)} collective-permute-done((f32[264,512]{1,0:T(8,128)S(1)}, f32[264,512]{1,0:T(8,128)S(1)}, u32[]{:S(2)}, u32[]{:S(2)}) %collective-permute-start.8) | collective-permute-done | bytes 540704 | tf_op jit(solution)/shard_map/ppermute | solution.py:18
  52.3 0.1 add.30
  52.4 2.5 %collective-permute-start.11 = (f32[264,128]{1,0:T(8,128)S(1)}, f32[264,128]{1,0:T(8,128)S(1)}, u32[]{:S(2)}, u32[]{:S(2)}) collective-permute-start(f32[264,128]{1,0:T(8,128)S(1)} %get-tuple-element.66), channel_id=1, source_target_pairs={{0,3},{1,2},{2,1},{3,0},{4,7},{5,6},{6,5},{7,4},{8,11},{9,10},{10,... | collective-permute-start | bytes 405512 | tf_op jit(solution)/shard_map/ppermute | solution.py:18
  55.0 0.5 collective-permute-start.10
  55.4 0.6 collective-permute-start.9
  56.0 3.6 %collective-permute-done.11 = f32[264,128]{1,0:T(8,128)S(1)} collective-permute-done((f32[264,128]{1,0:T(8,128)S(1)}, f32[264,128]{1,0:T(8,128)S(1)}, u32[]{:S(2)}, u32[]{:S(2)}) %collective-permute-start.11) | collective-permute-done | bytes 135200 | tf_op jit(solution)/shard_map/ppermute | solution.py:18
  59.6 2.5 %collective-permute-done.10 = f32[264,128]{1,0:T(8,128)S(1)} collective-permute-done((f32[264,128]{1,0:T(8,128)S(1)}, f32[264,128]{1,0:T(8,128)S(1)}, u32[]{:S(2)}, u32[]{:S(2)}) %collective-permute-start.10) | collective-permute-done | bytes 135200 | tf_op jit(solution)/shard_map/ppermute | solution.py:18
  62.2 0.1 collective-permute-done.9
  62.4 3.1 %collective-permute-start.14 = (f32[72,128]{1,0:T(8,128)S(1)}, f32[72,128]{1,0:T(8,128)S(1)}, u32[]{:S(2)}, u32[]{:S(2)}) collective-permute-start(f32[72,128]{1,0:T(8,128)S(1)} %concatenate.12), channel_id=1, source_target_pairs={{0,24},{4,28},{8,16},{12,20},{16,8},{20,12},{24,0},{28,4},{1,25},{... | collective-permute-start | bytes 110600 | tf_op jit(solution)/shard_map/ppermute | solution.py:18
  65.4 0.0 collective-permute-start.13
  65.5 1.3 %collective-permute-start.12 = (f32[72,128]{1,0:T(8,128)S(1)}, f32[72,128]{1,0:T(8,128)S(1)}, u32[]{:S(2)}, u32[]{:S(2)}) collective-permute-start(f32[72,128]{1,0:T(8,128)S(1)} %get-tuple-element.72), channel_id=1, source_target_pairs={{0,8},{4,12},{8,0},{12,4},{16,24},{20,28},{24,16},{28,20},{1,9},{5... | collective-permute-start | bytes 110600 | tf_op jit(solution)/shard_map/ppermute | solution.py:18
  66.8 1.5 %collective-permute-done.14 = f32[72,128]{1,0:T(8,128)S(1)} collective-permute-done((f32[72,128]{1,0:T(8,128)S(1)}, f32[72,128]{1,0:T(8,128)S(1)}, u32[]{:S(2)}, u32[]{:S(2)}) %collective-permute-start.14) | collective-permute-done | bytes 36896 | tf_op jit(solution)/shard_map/ppermute | solution.py:18
  68.3 2.1 %collective-permute-done.13 = f32[72,128]{1,0:T(8,128)S(1)} collective-permute-done((f32[72,128]{1,0:T(8,128)S(1)}, f32[72,128]{1,0:T(8,128)S(1)}, u32[]{:S(2)}, u32[]{:S(2)}) %collective-permute-start.13) | collective-permute-done | bytes 36896 | tf_op jit(solution)/shard_map/ppermute | solution.py:18
  70.3 0.0 collective-permute-done.12
  70.4 0.6 multiply_bitcast_fusion
  70.9 0.6 fusion.2
  (10 shorter events, 0.2 us)
Async XLA Ops:
  3.0 8.9 %copy-start = (bf16[3,4096]{1,0:T(4,128)(2,1)S(1)}, bf16[3,4096]{1,0:T(4,128)(2,1)}, u32[]{:S(2)}) copy-start(bf16[3,4096]{1,0:T(4,128)(2,1)} %refs_3_.1) | copy-start | bytes 73732
  3.0 8.9 %copy-start.1 = (f32[6,4,1024]{2,1,0:T(4,128)S(1)}, f32[6,4,1024]{2,1,0:T(4,128)}, u32[]{:S(2)}) copy-start(f32[6,4,1024]{2,1,0:T(4,128)} %moments_ref.1) | copy-start | bytes 294916
  3.0 8.9 %copy-start.2 = (s32[4,1024]{1,0:T(4,128)S(1)}, s32[4,1024]{1,0:T(4,128)}, u32[]{:S(2)}) copy-start(s32[4,1024]{1,0:T(4,128)} %label_ref.1) | copy-start | bytes 49156
  3.1 8.9 %copy-start.3 = (f32[4,1024]{1,0:T(4,128)S(1)}, f32[4,1024]{1,0:T(4,128)}, u32[]{:S(2)}) copy-start(f32[4,1024]{1,0:T(4,128)} %misfit_ref.1) | copy-start | bytes 49156
  3.1 22.0 %collective-permute-start.2 = (bf16[128,3328]{1,0:T(8,128)(2,1)S(1)}, bf16[128,3328]{1,0:T(8,128)(2,1)S(1)}, u32[]{:S(2)}, u32[]{:S(2)}) collective-permute-start(bf16[128,3328]{1,0:T(8,128)(2,1)S(1)} %get-tuple-element.38), channel_id=1, source_target_pairs={{0,2},{1,3},{2,0},{3,1},{4,6},{5,7},{6,4},{7,5},{8,10},{9,11},{10,... | collective-permute-start | bytes 2555912 | tf_op jit(solution)/shard_map/ppermute | solution.py:18
  6.1 23.3 %collective-permute-start.6 = (bf16[128,3328]{1,0:T(8,128)(2,1)S(1)}, bf16[128,3328]{1,0:T(8,128)(2,1)S(1)}, u32[]{:S(2)}, u32[]{:S(2)}) collective-permute-start(bf16[128,3328]{1,0:T(8,128)(2,1)S(1)} %get-tuple-element.53), channel_id=1, source_target_pairs={{0,1},{1,0},{2,3},{3,2},{4,5},{5,4},{6,7},{7,6},{8,9},{9,8},{10,11... | collective-permute-start | bytes 2555912 | tf_op jit(solution)/shard_map/ppermute | solution.py:18
  10.5 4.8 %collective-permute-start.3 = (bf16[128,1024]{1,0:T(8,128)(2,1)S(1)}, bf16[128,1024]{1,0:T(8,128)(2,1)S(1)}, u32[]{:S(2)}, u32[]{:S(2)}) collective-permute-start(bf16[128,1024]{1,0:T(8,128)(2,1)S(1)} %get-tuple-element.39.refs_0_), channel_id=1, source_target_pairs={{4,0},{8,4},{12,8},{16,12},{20,16},{24,20},{28,24},{5,1},{9,5},{13... | collective-permute-start | bytes 786440 | tf_op jit(solution)/shard_map/ppermute | solution.py:24
  11.8 25.5 %collective-permute-start = (bf16[128,1792]{1,0:T(8,128)(2,1)S(1)}, bf16[128,1792]{1,0:T(8,128)(2,1)S(1)}, u32[]{:S(2)}, u32[]{:S(2)}) collective-permute-start(bf16[128,1792]{1,0:T(8,128)(2,1)S(1)} %get-tuple-element.36), channel_id=1, source_target_pairs={{0,3},{1,2},{2,1},{3,0},{4,7},{5,6},{6,5},{7,4},{8,11},{9,10},{10,... | collective-permute-start | bytes 1376264 | tf_op jit(solution)/shard_map/ppermute | solution.py:18
  25.1 5.6 %collective-permute-start.4 = (bf16[128,1024]{1,0:T(8,128)(2,1)S(1)}, bf16[128,1024]{1,0:T(8,128)(2,1)S(1)}, u32[]{:S(2)}, u32[]{:S(2)}) collective-permute-start(bf16[128,1024]{1,0:T(8,128)(2,1)S(1)} %crop.3), channel_id=1, source_target_pairs={{4,0},{8,4},{12,8},{16,12},{20,16},{24,20},{28,24},{5,1},{9,5},{13... | collective-permute-start | bytes 786440 | tf_op jit(solution)/shard_map/ppermute | solution.py:24
  26.4 18.2 %collective-permute-start.1 = (bf16[128,1536]{1,0:T(8,128)(2,1)S(1)}, bf16[128,1536]{1,0:T(8,128)(2,1)S(1)}, u32[]{:S(2)}, u32[]{:S(2)}) collective-permute-start(bf16[128,1536]{1,0:T(8,128)(2,1)S(1)} %get-tuple-element.37), channel_id=1, source_target_pairs={{0,3},{1,2},{2,1},{3,0},{4,7},{5,6},{6,5},{7,4},{8,11},{9,10},{10,... | collective-permute-start | bytes 1179656 | tf_op jit(solution)/shard_map/ppermute | solution.py:18
  29.4 9.4 %collective-permute-start.7 = (bf16[128,1024]{1,0:T(8,128)(2,1)S(1)}, bf16[128,1024]{1,0:T(8,128)(2,1)S(1)}, u32[]{:S(2)}, u32[]{:S(2)}) collective-permute-start(bf16[128,1024]{1,0:T(8,128)(2,1)S(1)} %crop.5), channel_id=1, source_target_pairs={{4,0},{8,4},{12,8},{16,12},{20,16},{24,20},{28,24},{5,1},{9,5},{13... | collective-permute-start | bytes 786440 | tf_op jit(solution)/shard_map/ppermute | solution.py:24
  37.3 7.3 %collective-permute-start.5 = (bf16[128,1024]{1,0:T(8,128)(2,1)S(1)}, bf16[128,1024]{1,0:T(8,128)(2,1)S(1)}, u32[]{:S(2)}, u32[]{:S(2)}) collective-permute-start(bf16[128,1024]{1,0:T(8,128)(2,1)S(1)} %crop.4), channel_id=1, source_target_pairs={{4,0},{8,4},{12,8},{16,12},{20,16},{24,20},{28,24},{5,1},{9,5},{13... | collective-permute-start | bytes 786440 | tf_op jit(solution)/shard_map/ppermute | solution.py:24
  49.8 2.5 %collective-permute-start.8 = (f32[264,512]{1,0:T(8,128)S(1)}, f32[264,512]{1,0:T(8,128)S(1)}, u32[]{:S(2)}, u32[]{:S(2)}) collective-permute-start(f32[264,512]{1,0:T(8,128)S(1)} %get-tuple-element.64), channel_id=1, source_target_pairs={{0,4},{4,0},{8,12},{12,8},{16,20},{20,16},{24,28},{28,24},{1,5},{5... | collective-permute-start | bytes 1622024 | tf_op jit(solution)/shard_map/ppermute | solution.py:18
  52.4 7.2 %collective-permute-start.11 = (f32[264,128]{1,0:T(8,128)S(1)}, f32[264,128]{1,0:T(8,128)S(1)}, u32[]{:S(2)}, u32[]{:S(2)}) collective-permute-start(f32[264,128]{1,0:T(8,128)S(1)} %get-tuple-element.66), channel_id=1, source_target_pairs={{0,3},{1,2},{2,1},{3,0},{4,7},{5,6},{6,5},{7,4},{8,11},{9,10},{10,... | collective-permute-start | bytes 405512 | tf_op jit(solution)/shard_map/ppermute | solution.py:18
  55.0 7.2 %collective-permute-start.10 = (f32[264,128]{1,0:T(8,128)S(1)}, f32[264,128]{1,0:T(8,128)S(1)}, u32[]{:S(2)}, u32[]{:S(2)}) collective-permute-start(f32[264,128]{1,0:T(8,128)S(1)} %get-tuple-element.67), channel_id=1, source_target_pairs={{0,2},{1,3},{2,0},{3,1},{4,6},{5,7},{6,4},{7,5},{8,10},{9,11},{10,... | collective-permute-start | bytes 405512 | tf_op jit(solution)/shard_map/ppermute | solution.py:18
  55.4 6.8 %collective-permute-start.9 = (f32[264,128]{1,0:T(8,128)S(1)}, f32[264,128]{1,0:T(8,128)S(1)}, u32[]{:S(2)}, u32[]{:S(2)}) collective-permute-start(f32[264,128]{1,0:T(8,128)S(1)} %get-tuple-element.65), channel_id=1, source_target_pairs={{0,1},{1,0},{2,3},{3,2},{4,5},{5,4},{6,7},{7,6},{8,9},{9,8},{10,11... | collective-permute-start | bytes 405512 | tf_op jit(solution)/shard_map/ppermute | solution.py:18
  62.4 5.9 %collective-permute-start.14 = (f32[72,128]{1,0:T(8,128)S(1)}, f32[72,128]{1,0:T(8,128)S(1)}, u32[]{:S(2)}, u32[]{:S(2)}) collective-permute-start(f32[72,128]{1,0:T(8,128)S(1)} %concatenate.12), channel_id=1, source_target_pairs={{0,24},{4,28},{8,16},{12,20},{16,8},{20,12},{24,0},{28,4},{1,25},{... | collective-permute-start | bytes 110600 | tf_op jit(solution)/shard_map/ppermute | solution.py:18
  65.4 4.9 %collective-permute-start.13 = (f32[72,128]{1,0:T(8,128)S(1)}, f32[72,128]{1,0:T(8,128)S(1)}, u32[]{:S(2)}, u32[]{:S(2)}) collective-permute-start(f32[72,128]{1,0:T(8,128)S(1)} %get-tuple-element.73), channel_id=1, source_target_pairs={{0,16},{4,20},{8,24},{12,28},{16,0},{20,4},{24,8},{28,12},{1,17},{... | collective-permute-start | bytes 110600 | tf_op jit(solution)/shard_map/ppermute | solution.py:18
  65.5 4.9 %collective-permute-start.12 = (f32[72,128]{1,0:T(8,128)S(1)}, f32[72,128]{1,0:T(8,128)S(1)}, u32[]{:S(2)}, u32[]{:S(2)}) collective-permute-start(f32[72,128]{1,0:T(8,128)S(1)} %get-tuple-element.72), channel_id=1, source_target_pairs={{0,8},{4,12},{8,0},{12,4},{16,24},{20,28},{24,16},{28,20},{1,9},{5... | collective-permute-start | bytes 110600 | tf_op jit(solution)/shard_map/ppermute | solution.py:18
